TPU v7x, 512 devices: a whole 4x8x8 slice. The times are simulated.
512 devices in a mesh: sub: 512 (over z, y, x, core).
Axes of the slice: x: 4, y: 8, z: 8, core: 2. Of those that a mesh axis runs over, the one named last changes fastest.
Arguments:
- deflation: bfloat16 [524288, 128], P('sub'), may hold values from -0.1875 to 0.1875
- op_tiles: bfloat16 [24576, 128, 128], P('sub'), may hold values from -0.21875 to 0.21875
- tile_cols: int32 [24576], P('sub'), may hold values from 0 to 7
- diag_coef: float32 [524288], P('sub'), may hold values from 1 to 4
- fine_rhs: bfloat16 [524288, 128], P('sub'), may hold values from -6 to 6
- adjacency: int32 [512, 8], P('sub'), may hold values from 0 to 1, as said below
- margin_rows: int32 [512, 8, 512], P('sub'), may hold values from 0 to 1023
Outputs:
- fine_residual: bfloat16 [524288, 128], P('sub')
- coarse_residual: float32 [65536, 128], P('sub')
Inputs may be any that keep to these rules, and one draw needn't show every extreme that they name: Symmetric: adjacency[i, s] equals adjacency[(i + o_s) mod 512, s'] with o_s' = -o_s; every subdomain is coupled to both cycle neighbours (slots of offsets 1 and -1); the degrees of subdomains differ widely.
All inputs are finite; a program needn't handle non-finite values.
Results may differ from a plain program's by a relative error of at most 0.0095.
Values may be sent and summed in bfloat16 or wider, within the bound.
No kernel may reach another device: no remote copies, remote signals or barrier semaphores. Data moves between devices by JAX's collectives and lax.ppermute only.
A program may use at most 64 MiB of HBM per device.

v0:
```python
import jax
import jax.numpy as jnp
from jax import lax
from jax.sharding import PartitionSpec as P

BLK = 128
TPR = 6


OFFSETS = (1, 2, 4, 8, -1, -2, -4, -8)
CHEB_CENTER = 2.5
CHEB_HALF = 1.5
RHO_FIRST = CHEB_HALF / CHEB_CENTER
RHO_SECOND = 1.0 / (2.0 * CHEB_CENTER / CHEB_HALF - RHO_FIRST)


def shifted(block, axis, distance):
    devices = range(lax.axis_size(axis))
    route = [((i - distance) % len(devices), i) for i in devices]
    return lax.ppermute(block, axis, route)


def tile_apply(op_tiles, tile_cols, values_in):
    local_n, columns_n = values_in.shape
    block_n = local_n // BLK
    picked = values_in.reshape(block_n, BLK, columns_n)[tile_cols]
    products = jnp.einsum("tab,tbw->taw", op_tiles, picked, preferred_element_type=jnp.float32)
    return products.reshape(block_n, TPR, BLK, columns_n).sum(axis=1).reshape(local_n, columns_n)


def cross(left, right):
    return lax.dot_general(
        left, right, (((0,), (0,)), ((), ())), preferred_element_type=jnp.float32
    )


def per_device(deflation, op_tiles, tile_cols, diag_coef, fine_rhs, adjacency, margin_rows):
    weights_adj = adjacency[0].astype(jnp.float32)
    row_lists = margin_rows[0]
    width_k = deflation.shape[1]
    images = (
        diag_coef[:, None] * deflation.astype(jnp.float32)
        + tile_apply(op_tiles, tile_cols, deflation)
    ).astype(jnp.bfloat16)
    own_block = cross(deflation, images)
    coarse_rhs = cross(deflation, fine_rhs)
    stacked = jnp.concatenate([deflation[row_lists], images[row_lists]], axis=-1)
    pair_blocks = [None] * len(OFFSETS)
    basis_rows = [None] * len(OFFSETS)
    for offset in OFFSETS:
        back_slot = OFFSETS.index(-offset)
        received = shifted(stacked[OFFSETS.index(offset)], "sub", offset)
        basis_rows[back_slot] = received[:, :width_k]
        mine_rows = stacked[back_slot]
        summed_pair = cross(mine_rows[:, :width_k], received[:, width_k:]) + cross(
            mine_rows[:, width_k:], received[:, :width_k]
        )
        pair_blocks[back_slot] = 0.5 * summed_pair * weights_adj[back_slot]

    def apply_coarse(vector):
        result = jnp.dot(own_block, vector, precision=lax.Precision.HIGHEST)
        remotes = []
        for slot_id, offset in enumerate(OFFSETS):
            remote = shifted(vector, "sub", -offset)
            remotes.append(remote)
            result = result + jnp.dot(pair_blocks[slot_id], remote, precision=lax.Precision.HIGHEST)
        return (result, remotes)

    first = coarse_rhs / CHEB_CENTER
    first_image, first_remotes = apply_coarse(first)
    resid_one = coarse_rhs - first_image
    second = RHO_SECOND * RHO_FIRST * first + 2.0 * RHO_SECOND / CHEB_HALF * resid_one
    coarse_sol = first + second
    second_image, second_remotes = apply_coarse(second)
    coarse_residual = resid_one - second_image
    coeffs = coarse_sol.astype(jnp.bfloat16)
    local_corr = jnp.dot(deflation, coeffs, preferred_element_type=jnp.float32).astype(jnp.bfloat16)
    summed = local_corr.astype(jnp.float32)
    for slot_id in range(len(OFFSETS)):
        partner_coeffs = (first_remotes[slot_id] + second_remotes[slot_id]).astype(jnp.bfloat16)
        arrived = jnp.dot(
            basis_rows[slot_id], partner_coeffs, preferred_element_type=jnp.float32
        ).astype(jnp.bfloat16)
        summed = summed.at[row_lists[slot_id]].add(
            weights_adj[slot_id] * arrived.astype(jnp.float32)
        )
    merged = summed.astype(jnp.bfloat16)
    fine_image = diag_coef[:, None] * merged.astype(jnp.float32) + tile_apply(
        op_tiles, tile_cols, merged
    )
    fine_residual = (fine_rhs.astype(jnp.float32) - fine_image).astype(jnp.bfloat16)
    return (fine_residual, coarse_residual)


def solution(mesh):
    placed = (
        P("sub", None),
        P("sub", None, None),
        P("sub"),
        P("sub"),
        P("sub", None),
        P("sub", None),
        P("sub", None, None),
    )
    return jax.shard_map(
        per_device,
        mesh=mesh,
        in_specs=placed,
        out_specs=(P("sub", None), P("sub", None)),
        check_vma=False,
    )
```

profile of v0, /device:TPU:1, one launch (start us, length us, event | category | flops | bytes accessed | tf_op | source)
XLA Modules:
  0.0 247.0 jit_solution(14457615936856598709)
XLA Ops:
  0.7 2.1 broadcast_multiply_fusion
  2.7 8.8 %collective-permute-start.1 = (f32[128,128]{1,0:T(8,128)}, f32[128,128]{1,0:T(8,128)}, u32[]{:S(2)}, u32[]{:S(2)}) collective-permute-start(f32[128,128]{1,0:T(8,128)} %get-tuple-element.26), channel_id=1, source_target_pairs={{1,0},{2,1},{3,2},{4,3},{5,4},{6,5},{7,6},{8,7},{9,8},{10,9},{11,1... | collective-permute-start | bytes 196616 | tf_op jit(solution)/shard_map/ppermute | solution.py:20
  11.5 10.7 %collective-permute-start.5 = (f32[128,128]{1,0:T(8,128)}, f32[128,128]{1,0:T(8,128)S(1)}, u32[]{:S(2)}, u32[]{:S(2)}) collective-permute-start(f32[128,128]{1,0:T(8,128)} %get-tuple-element.26), channel_id=1, source_target_pairs={{4,0},{5,1},{6,2},{7,3},{8,4},{9,5},{10,6},{11,7},{12,8},{13,9},{1... | collective-permute-start | bytes 196616 | tf_op jit(solution)/shard_map/ppermute | solution.py:20
  22.2 3.0 %collective-permute-start.7 = (f32[128,128]{1,0:T(8,128)}, f32[128,128]{1,0:T(8,128)}, u32[]{:S(2)}, u32[]{:S(2)}) collective-permute-start(f32[128,128]{1,0:T(8,128)} %get-tuple-element.26), channel_id=1, source_target_pairs={{8,0},{9,1},{10,2},{11,3},{12,4},{13,5},{14,6},{15,7},{16,8},{17,9... | collective-permute-start | bytes 196616 | tf_op jit(solution)/shard_map/ppermute | solution.py:20
  26.7 2.9 %fusion.109 = f32[48,128,128]{2,1,0:T(8,128)} fusion(bf16[48,128,128]{2,1,0:T(8,128)(2,1)S(1)} %gather_fusion, bf16[48,128,128]{2,1,0:T(8,128)(2,1)S(1)} %copy-done), kind=kOutput, calls=%fused_computation.182 | convolution fusion | flops 201326592 | bytes 6291456 | tf_op jit(solution)/shard_map/tab,tbw->taw/dot_general | solution.py:27
  29.6 2.1 reduce_sum.18
  32.8 12.1 %gather_fusion.1 = bf16[4096,128]{1,0:T(8,128)(2,1)S(1)} fusion(bf16[1024,128]{1,0:T(8,128)(2,1)S(1)} %copy-done.1, s32[4096]{0:T(1024)S(1)} %broadcast_clamp_fusion), kind=kCustom, calls=%fused_computation.1 | custom fusion | bytes 2113536 | tf_op jit(solution)/shard_map/gather | solution.py:47
  44.9 1.2 fusion.42
  46.2 14.9 %gather_fusion.2 = bf16[4096,128]{1,0:T(8,128)(2,1)} fusion(bf16[1024,128]{1,0:T(8,128)(2,1)S(1)} %fusion.42, s32[4096]{0:T(1024)S(1)} %broadcast_clamp_fusion), kind=kCustom, calls=%fused_computation.2 | custom fusion | bytes 2113536 | tf_op jit(solution)/shard_map/gather | solution.py:47
  61.1 2.6 %fusion.56 = (bf16[512,256]{1,0:T(8,128)(2,1)}, bf16[512,256]{1,0:T(8,128)(2,1)}, bf16[512,256]{1,0:T(8,128)(2,1)S(1)}, bf16[512,256]{1,0:T(8,128)(2,1)}, bf16[5...) fusion(bf16[8,512,128]{2,1,0:T(8,128)(2,1)} %bitcast.125, ...), kind=kLoop, calls=%fused_computation.106 | loop fusion | flops 4194304 | bytes 4194304 | tf_op jit(solution)/shard_map/squeeze | solution.py:54
  63.6 2.6 %collective-permute-start = (bf16[512,256]{1,0:T(8,128)(2,1)}, bf16[512,256]{1,0:T(8,128)(2,1)}, u32[]{:S(2)}, u32[]{:S(2)}) collective-permute-start(bf16[512,256]{1,0:T(8,128)(2,1)} %get-tuple-element.3), channel_id=1, source_target_pairs={{1,0},{2,1},{3,2},{4,3},{5,4},{6,5},{7,6},{8,7},{9,8},{10,9},{11,1... | collective-permute-start | bytes 786440 | tf_op jit(solution)/shard_map/ppermute | solution.py:20
  66.3 3.1 %collective-permute-start.8 = (bf16[512,256]{1,0:T(8,128)(2,1)}, bf16[512,256]{1,0:T(8,128)(2,1)}, u32[]{:S(2)}, u32[]{:S(2)}) collective-permute-start(bf16[512,256]{1,0:T(8,128)(2,1)} %get-tuple-element.2), channel_id=1, source_target_pairs={{511,0},{0,1},{1,2},{2,3},{3,4},{4,5},{5,6},{6,7},{7,8},{8,9},{9,1... | collective-permute-start | bytes 786440 | tf_op jit(solution)/shard_map/ppermute | solution.py:20
  77.4 3.9 %collective-permute-start.4 = (bf16[512,256]{1,0:T(8,128)(2,1)}, bf16[512,256]{1,0:T(8,128)(2,1)S(1)}, u32[]{:S(2)}, u32[]{:S(2)}) collective-permute-start(bf16[512,256]{1,0:T(8,128)(2,1)} %get-tuple-element.7), channel_id=1, source_target_pairs={{4,0},{5,1},{6,2},{7,3},{8,4},{9,5},{10,6},{11,7},{12,8},{13,9},{1... | collective-permute-start | bytes 786440 | tf_op jit(solution)/shard_map/ppermute | solution.py:20
  81.4 1.2 fusion.86
  82.6 3.0 %collective-permute-start.6 = (bf16[512,256]{1,0:T(8,128)(2,1)}, bf16[512,256]{1,0:T(8,128)(2,1)S(1)}, u32[]{:S(2)}, u32[]{:S(2)}) collective-permute-start(bf16[512,256]{1,0:T(8,128)(2,1)} %get-tuple-element.8), channel_id=1, source_target_pairs={{8,0},{9,1},{10,2},{11,3},{12,4},{13,5},{14,6},{15,7},{16,8},{17,9... | collective-permute-start | bytes 786440 | tf_op jit(solution)/shard_map/ppermute | solution.py:20
  85.6 1.2 fusion.70
  86.8 2.6 %collective-permute-done.4 = bf16[512,256]{1,0:T(8,128)(2,1)S(1)} collective-permute-done((bf16[512,256]{1,0:T(8,128)(2,1)}, bf16[512,256]{1,0:T(8,128)(2,1)S(1)}, u32[]{:S(2)}, u32[]{:S(2)}) %collective-permute-start.4) | collective-permute-done | bytes 262176 | tf_op jit(solution)/shard_map/ppermute | solution.py:20
  89.3 4.0 %collective-permute-start.10 = (bf16[512,256]{1,0:T(8,128)(2,1)S(1)}, bf16[512,256]{1,0:T(8,128)(2,1)S(1)}, u32[]{:S(2)}, u32[]{:S(2)}) collective-permute-start(bf16[512,256]{1,0:T(8,128)(2,1)S(1)} %get-tuple-element.4), channel_id=1, source_target_pairs={{510,0},{511,1},{0,2},{1,3},{2,4},{3,5},{4,6},{5,7},{6,8},{7,9},{8... | collective-permute-start | bytes 786440 | tf_op jit(solution)/shard_map/ppermute | solution.py:20
  93.4 1.1 fusion.78
  94.5 2.5 %collective-permute-start.12 = (bf16[512,256]{1,0:T(8,128)(2,1)}, bf16[512,256]{1,0:T(8,128)(2,1)S(1)}, u32[]{:S(2)}, u32[]{:S(2)}) collective-permute-start(bf16[512,256]{1,0:T(8,128)(2,1)} %get-tuple-element.6), channel_id=1, source_target_pairs={{508,0},{509,1},{510,2},{511,3},{0,4},{1,5},{2,6},{3,7},{4,8},{5,9... | collective-permute-start | bytes 786440 | tf_op jit(solution)/shard_map/ppermute | solution.py:20
  97.3 8.2 %collective-permute-done.10 = bf16[512,256]{1,0:T(8,128)(2,1)S(1)} collective-permute-done((bf16[512,256]{1,0:T(8,128)(2,1)S(1)}, bf16[512,256]{1,0:T(8,128)(2,1)S(1)}, u32[]{:S(2)}, u32[]{:S(2)}) %collective-permute-start.10) | collective-permute-done | bytes 262176 | tf_op jit(solution)/shard_map/ppermute | solution.py:20
  105.5 1.9 collective-permute-start.14
  107.7 3.7 %collective-permute-done.12 = bf16[512,256]{1,0:T(8,128)(2,1)S(1)} collective-permute-done((bf16[512,256]{1,0:T(8,128)(2,1)}, bf16[512,256]{1,0:T(8,128)(2,1)S(1)}, u32[]{:S(2)}, u32[]{:S(2)}) %collective-permute-start.12) | collective-permute-done | bytes 262176 | tf_op jit(solution)/shard_map/ppermute | solution.py:20
  111.3 4.5 %collective-permute-start.2 = (bf16[512,256]{1,0:T(8,128)(2,1)S(1)}, bf16[512,256]{1,0:T(8,128)(2,1)S(1)}, u32[]{:S(2)}, u32[]{:S(2)}) collective-permute-start(bf16[512,256]{1,0:T(8,128)(2,1)S(1)} %copy-done.4), channel_id=1, source_target_pairs={{2,0},{3,1},{4,2},{5,3},{6,4},{7,5},{8,6},{9,7},{10,8},{11,9},{12,... | collective-permute-start | bytes 786440 | tf_op jit(solution)/shard_map/ppermute | solution.py:20
  116.1 2.4 collective-permute-done.14
  118.5 1.9 collective-permute-start.9
  120.8 1.9 collective-permute-start.11
  123.0 1.2 fusion.22
  124.7 1.2 fusion.30
  127.0 2.2 collective-permute-start.13
  129.2 1.0 convolution_add_fusion.10
  130.3 1.9 collective-permute-start.15
  132.4 8.7 %collective-permute-start.3 = (f32[128,128]{1,0:T(8,128)}, f32[128,128]{1,0:T(8,128)S(1)}, u32[]{:S(2)}, u32[]{:S(2)}) collective-permute-start(f32[128,128]{1,0:T(8,128)} %get-tuple-element.26), channel_id=1, source_target_pairs={{2,0},{3,1},{4,2},{5,3},{6,4},{7,5},{8,6},{9,7},{10,8},{11,9},{12,... | collective-permute-start | bytes 196616 | tf_op jit(solution)/shard_map/ppermute | solution.py:20
  141.1 1.0 fusion.112
  145.0 3.7 %collective-permute-start.16 = (f32[128,128]{1,0:T(8,128)S(1)}, f32[128,128]{1,0:T(8,128)}, u32[]{:S(2)}, u32[]{:S(2)}) collective-permute-start(f32[128,128]{1,0:T(8,128)S(1)} %get-tuple-element.28), channel_id=1, source_target_pairs={{1,0},{2,1},{3,2},{4,3},{5,4},{6,5},{7,6},{8,7},{9,8},{10,9},{11,1... | collective-permute-start | bytes 196616 | tf_op jit(solution)/shard_map/ppermute | solution.py:20
  148.7 4.6 %collective-permute-start.18 = (f32[128,128]{1,0:T(8,128)S(1)}, f32[128,128]{1,0:T(8,128)}, u32[]{:S(2)}, u32[]{:S(2)}) collective-permute-start(f32[128,128]{1,0:T(8,128)S(1)} %get-tuple-element.28), channel_id=1, source_target_pairs={{4,0},{5,1},{6,2},{7,3},{8,4},{9,5},{10,6},{11,7},{12,8},{13,9},{1... | collective-permute-start | bytes 196616 | tf_op jit(solution)/shard_map/ppermute | solution.py:20
  153.2 3.6 %collective-permute-start.19 = (f32[128,128]{1,0:T(8,128)S(1)}, f32[128,128]{1,0:T(8,128)}, u32[]{:S(2)}, u32[]{:S(2)}) collective-permute-start(f32[128,128]{1,0:T(8,128)S(1)} %get-tuple-element.28), channel_id=1, source_target_pairs={{8,0},{9,1},{10,2},{11,3},{12,4},{13,5},{14,6},{15,7},{16,8},{17,9... | collective-permute-start | bytes 196616 | tf_op jit(solution)/shard_map/ppermute | solution.py:20
  156.9 5.7 %collective-permute-start.20 = (f32[128,128]{1,0:T(8,128)S(1)}, f32[128,128]{1,0:T(8,128)}, u32[]{:S(2)}, u32[]{:S(2)}) collective-permute-start(f32[128,128]{1,0:T(8,128)S(1)} %get-tuple-element.28), channel_id=1, source_target_pairs={{511,0},{0,1},{1,2},{2,3},{3,4},{4,5},{5,6},{6,7},{7,8},{8,9},{9,1... | collective-permute-start | bytes 196616 | tf_op jit(solution)/shard_map/ppermute | solution.py:20
  162.6 2.8 %collective-permute-start.22 = (f32[128,128]{1,0:T(8,128)S(1)}, f32[128,128]{1,0:T(8,128)}, u32[]{:S(2)}, u32[]{:S(2)}) collective-permute-start(f32[128,128]{1,0:T(8,128)S(1)} %get-tuple-element.28), channel_id=1, source_target_pairs={{508,0},{509,1},{510,2},{511,3},{0,4},{1,5},{2,6},{3,7},{4,8},{5,9... | collective-permute-start | bytes 196616 | tf_op jit(solution)/shard_map/ppermute | solution.py:20
  165.9 7.5 %collective-permute-done.22 = f32[128,128]{1,0:T(8,128)} collective-permute-done((f32[128,128]{1,0:T(8,128)S(1)}, f32[128,128]{1,0:T(8,128)}, u32[]{:S(2)}, u32[]{:S(2)}) %collective-permute-start.22) | collective-permute-done | bytes 65568 | tf_op jit(solution)/shard_map/ppermute | solution.py:20
  173.4 2.0 collective-permute-start.21
  175.4 1.7 fusion.5
  177.2 6.7 %collective-permute-done.21 = f32[128,128]{1,0:T(8,128)S(1)} collective-permute-done((f32[128,128]{1,0:T(8,128)S(1)}, f32[128,128]{1,0:T(8,128)S(1)}, u32[]{:S(2)}, u32[]{:S(2)}) %collective-permute-start.21) | collective-permute-done | bytes 65568 | tf_op jit(solution)/shard_map/ppermute | solution.py:20
  183.9 1.9 collective-permute-start.23
  185.8 1.6 fusion.7
  187.5 2.1 collective-permute-start.17
  189.5 1.7 fusion.9
  191.2 1.7 fusion.11
  192.9 1.6 fusion.13
  194.6 1.5 fusion.15
  196.1 2.5 fusion.17
  198.6 3.9 %scatter_fusion = f32[1024,128]{1,0:T(8,128)S(1)} fusion(f32[1024,128]{1,0:T(8,128)S(1)} %copy.15, s32[512]{0:T(512)S(1)} %bitcast.134, f32[512,128]{1,0:T(8,128)} %fusion.17), kind=kCustom, calls=%fused_computation.4 | custom fusion | flops 65536 | bytes 788480 | tf_op jit(solution)/shard_map/scatter-add | solution.py:84
  202.5 4.1 %scatter_fusion.1 = f32[1024,128]{1,0:T(8,128)S(1)} fusion(f32[1024,128]{1,0:T(8,128)S(1)} %scatter_fusion, s32[512]{0:T(512)S(1)} %bitcast.133, f32[512,128]{1,0:T(8,128)} %fusion.15), kind=kCustom, calls=%fused_computation.5 | custom fusion | flops 65536 | bytes 788480 | tf_op jit(solution)/shard_map/scatter-add | solution.py:84
  206.6 3.5 %scatter_fusion.2 = f32[1024,128]{1,0:T(8,128)S(1)} fusion(f32[1024,128]{1,0:T(8,128)S(1)} %scatter_fusion.1, s32[512]{0:T(512)S(1)} %bitcast.132, f32[512,128]{1,0:T(8,128)S(1)} %fusion.13), kind=kCustom, calls=%fused_computation.6 | custom fusion | flops 65536 | bytes 788480 | tf_op jit(solution)/shard_map/scatter-add | solution.py:84
  210.2 3.5 %scatter_fusion.3 = f32[1024,128]{1,0:T(8,128)S(1)} fusion(f32[1024,128]{1,0:T(8,128)S(1)} %scatter_fusion.2, s32[512]{0:T(512)S(1)} %bitcast.131, f32[512,128]{1,0:T(8,128)S(1)} %fusion.11), kind=kCustom, calls=%fused_computation.7 | custom fusion | flops 65536 | bytes 788480 | tf_op jit(solution)/shard_map/scatter-add | solution.py:84
  213.7 3.5 %scatter_fusion.4 = f32[1024,128]{1,0:T(8,128)S(1)} fusion(f32[1024,128]{1,0:T(8,128)S(1)} %scatter_fusion.3, s32[512]{0:T(512)S(1)} %bitcast.130, f32[512,128]{1,0:T(8,128)S(1)} %fusion.9), kind=kCustom, calls=%fused_computation.8 | custom fusion | flops 65536 | bytes 788480 | tf_op jit(solution)/shard_map/scatter-add | solution.py:84
  217.2 3.5 %scatter_fusion.5 = f32[1024,128]{1,0:T(8,128)S(1)} fusion(f32[1024,128]{1,0:T(8,128)S(1)} %scatter_fusion.4, s32[512]{0:T(512)S(1)} %bitcast.129, f32[512,128]{1,0:T(8,128)S(1)} %fusion.7), kind=kCustom, calls=%fused_computation.9 | custom fusion | flops 65536 | bytes 788480 | tf_op jit(solution)/shard_map/scatter-add | solution.py:84
  220.8 3.7 %scatter_fusion.6 = f32[1024,128]{1,0:T(8,128)S(1)} fusion(f32[1024,128]{1,0:T(8,128)S(1)} %scatter_fusion.5, s32[512]{0:T(512)S(1)} %bitcast.128, f32[512,128]{1,0:T(8,128)S(1)} %fusion.5), kind=kCustom, calls=%fused_computation.10 | custom fusion | flops 65536 | bytes 788480 | tf_op jit(solution)/shard_map/scatter-add | solution.py:84
  224.6 1.6 fusion.3
  226.2 3.5 %scatter_fusion.7 = f32[1024,128]{1,0:T(8,128)S(1)} fusion(f32[1024,128]{1,0:T(8,128)S(1)} %scatter_fusion.6, s32[512]{0:T(512)S(1)} %bitcast.127, f32[512,128]{1,0:T(8,128)S(1)} %fusion.3), kind=kCustom, calls=%fused_computation.11 | custom fusion | flops 65536 | bytes 788480 | tf_op jit(solution)/shard_map/scatter-add | solution.py:84
  229.8 2.1 gather_fusion.3
  231.9 4.3 %fusion.117 = f32[48,128,128]{2,1,0:T(8,128)} fusion(bf16[48,128,128]{2,1,0:T(8,128)(2,1)} %gather_fusion.3, bf16[48,128,128]{2,1,0:T(8,128)(2,1)S(1)} %copy-done), kind=kOutput, calls=%fused_computation.190 | convolution fusion | flops 201326592 | bytes 6291456 | tf_op jit(solution)/shard_map/tab,tbw->taw/dot_general | solution.py:27
  236.1 2.2 reduce_sum.19
  245.1 1.0 convolution_add_fusion.1
  (192 shorter events, 19.2 us)
Async XLA Ops:
  0.6 26.1 %copy-start = (bf16[48,128,128]{2,1,0:T(8,128)(2,1)S(1)}, bf16[48,128,128]{2,1,0:T(8,128)(2,1)}, u32[]{:S(2)}) copy-start(bf16[48,128,128]{2,1,0:T(8,128)(2,1)} %param.8) | copy-start | bytes 4718596
  0.6 25.2 %copy-start.1 = (bf16[1024,128]{1,0:T(8,128)(2,1)S(1)}, bf16[1024,128]{1,0:T(8,128)(2,1)}, u32[]{:S(2)}) copy-start(bf16[1024,128]{1,0:T(8,128)(2,1)} %param.7) | copy-start | bytes 786436
  2.7 124.3 %collective-permute-start.1 = (f32[128,128]{1,0:T(8,128)}, f32[128,128]{1,0:T(8,128)}, u32[]{:S(2)}, u32[]{:S(2)}) collective-permute-start(f32[128,128]{1,0:T(8,128)} %get-tuple-element.26), channel_id=1, source_target_pairs={{1,0},{2,1},{3,2},{4,3},{5,4},{6,5},{7,6},{8,7},{9,8},{10,9},{11,1... | collective-permute-start | bytes 196616 | tf_op jit(solution)/shard_map/ppermute | solution.py:20
  11.5 118.7 %collective-permute-start.5 = (f32[128,128]{1,0:T(8,128)}, f32[128,128]{1,0:T(8,128)S(1)}, u32[]{:S(2)}, u32[]{:S(2)}) collective-permute-start(f32[128,128]{1,0:T(8,128)} %get-tuple-element.26), channel_id=1, source_target_pairs={{4,0},{5,1},{6,2},{7,3},{8,4},{9,5},{10,6},{11,7},{12,8},{13,9},{1... | collective-permute-start | bytes 196616 | tf_op jit(solution)/shard_map/ppermute | solution.py:20
  22.2 110.2 %collective-permute-start.7 = (f32[128,128]{1,0:T(8,128)}, f32[128,128]{1,0:T(8,128)}, u32[]{:S(2)}, u32[]{:S(2)}) collective-permute-start(f32[128,128]{1,0:T(8,128)} %get-tuple-element.26), channel_id=1, source_target_pairs={{8,0},{9,1},{10,2},{11,3},{12,4},{13,5},{14,6},{15,7},{16,8},{17,9... | collective-permute-start | bytes 196616 | tf_op jit(solution)/shard_map/ppermute | solution.py:20
  32.7 12.2 %copy-start.54 = (f32[1024]{0:T(1024)S(1)}, f32[1024]{0:T(1024)}, u32[]{:S(2)}) copy-start(f32[1024]{0:T(1024)} %param.10) | copy-start | bytes 12292
  61.1 8.6 %copy-start.65 = (s32[1,8]{1,0:T(1,128)S(1)}, s32[1,8]{1,0:T(1,128)}, u32[]{:S(2)}) copy-start(s32[1,8]{1,0:T(1,128)} %param.12) | copy-start | bytes 100
  63.6 33.5 %copy-start.5 = (bf16[512,256]{1,0:T(8,128)(2,1)S(1)}, bf16[512,256]{1,0:T(8,128)(2,1)}, u32[]{:S(2)}) copy-start(bf16[512,256]{1,0:T(8,128)(2,1)} %get-tuple-element.9) | copy-start | bytes 786436
  63.6 43.8 %copy-start.4 = (bf16[512,256]{1,0:T(8,128)(2,1)S(1)}, bf16[512,256]{1,0:T(8,128)(2,1)}, u32[]{:S(2)}) copy-start(bf16[512,256]{1,0:T(8,128)(2,1)} %get-tuple-element.5) | copy-start | bytes 786436
  63.6 52.3 %copy-start.3 = (bf16[512,256]{1,0:T(8,128)(2,1)S(1)}, bf16[512,256]{1,0:T(8,128)(2,1)}, u32[]{:S(2)}) copy-start(bf16[512,256]{1,0:T(8,128)(2,1)} %get-tuple-element.7) | copy-start | bytes 786436
  63.6 56.8 %copy-start.2 = (bf16[512,256]{1,0:T(8,128)(2,1)S(1)}, bf16[512,256]{1,0:T(8,128)(2,1)}, u32[]{:S(2)}) copy-start(bf16[512,256]{1,0:T(8,128)(2,1)} %get-tuple-element.8) | copy-start | bytes 786436
  63.6 13.8 %collective-permute-start = (bf16[512,256]{1,0:T(8,128)(2,1)}, bf16[512,256]{1,0:T(8,128)(2,1)}, u32[]{:S(2)}, u32[]{:S(2)}) collective-permute-start(bf16[512,256]{1,0:T(8,128)(2,1)} %get-tuple-element.3), channel_id=1, source_target_pairs={{1,0},{2,1},{3,2},{4,3},{5,4},{6,5},{7,6},{8,7},{9,8},{10,9},{11,1... | collective-permute-start | bytes 786440 | tf_op jit(solution)/shard_map/ppermute | solution.py:20
  66.3 16.3 %collective-permute-start.8 = (bf16[512,256]{1,0:T(8,128)(2,1)}, bf16[512,256]{1,0:T(8,128)(2,1)}, u32[]{:S(2)}, u32[]{:S(2)}) collective-permute-start(bf16[512,256]{1,0:T(8,128)(2,1)} %get-tuple-element.2), channel_id=1, source_target_pairs={{511,0},{0,1},{1,2},{2,3},{3,4},{4,5},{5,6},{6,7},{7,8},{8,9},{9,1... | collective-permute-start | bytes 786440 | tf_op jit(solution)/shard_map/ppermute | solution.py:20
  71.2 53.0 %copy-start.6 = (bf16[512,256]{1,0:T(8,128)(2,1)S(1)}, bf16[512,256]{1,0:T(8,128)(2,1)}, u32[]{:S(2)}) copy-start(bf16[512,256]{1,0:T(8,128)(2,1)} %get-tuple-element.6) | copy-start | bytes 786436
  77.4 11.9 %collective-permute-start.4 = (bf16[512,256]{1,0:T(8,128)(2,1)}, bf16[512,256]{1,0:T(8,128)(2,1)S(1)}, u32[]{:S(2)}, u32[]{:S(2)}) collective-permute-start(bf16[512,256]{1,0:T(8,128)(2,1)} %get-tuple-element.7), channel_id=1, source_target_pairs={{4,0},{5,1},{6,2},{7,3},{8,4},{9,5},{10,6},{11,7},{12,8},{13,9},{1... | collective-permute-start | bytes 786440 | tf_op jit(solution)/shard_map/ppermute | solution.py:20
  82.6 11.9 %collective-permute-start.6 = (bf16[512,256]{1,0:T(8,128)(2,1)}, bf16[512,256]{1,0:T(8,128)(2,1)S(1)}, u32[]{:S(2)}, u32[]{:S(2)}) collective-permute-start(bf16[512,256]{1,0:T(8,128)(2,1)} %get-tuple-element.8), channel_id=1, source_target_pairs={{8,0},{9,1},{10,2},{11,3},{12,4},{13,5},{14,6},{15,7},{16,8},{17,9... | collective-permute-start | bytes 786440 | tf_op jit(solution)/shard_map/ppermute | solution.py:20
  89.3 35.4 %copy-start.12 = (bf16[512,256]{1,0:T(8,128)(2,1)}, bf16[512,256]{1,0:T(8,128)(2,1)S(1)}, u32[]{:S(2)}) copy-start(bf16[512,256]{1,0:T(8,128)(2,1)S(1)} %collective-permute-done.4) | copy-start | bytes 786436
  89.3 16.2 %collective-permute-start.10 = (bf16[512,256]{1,0:T(8,128)(2,1)S(1)}, bf16[512,256]{1,0:T(8,128)(2,1)S(1)}, u32[]{:S(2)}, u32[]{:S(2)}) collective-permute-start(bf16[512,256]{1,0:T(8,128)(2,1)S(1)} %get-tuple-element.4), channel_id=1, source_target_pairs={{510,0},{511,1},{0,2},{1,3},{2,4},{3,5},{4,6},{5,7},{6,8},{7,9},{8... | collective-permute-start | bytes 786440 | tf_op jit(solution)/shard_map/ppermute | solution.py:20
  94.5 31.4 %copy-start.14 = (bf16[512,256]{1,0:T(8,128)(2,1)}, bf16[512,256]{1,0:T(8,128)(2,1)S(1)}, u32[]{:S(2)}) copy-start(bf16[512,256]{1,0:T(8,128)(2,1)S(1)} %collective-permute-done.6) | copy-start | bytes 786436
  94.5 16.8 %collective-permute-start.12 = (bf16[512,256]{1,0:T(8,128)(2,1)}, bf16[512,256]{1,0:T(8,128)(2,1)S(1)}, u32[]{:S(2)}, u32[]{:S(2)}) collective-permute-start(bf16[512,256]{1,0:T(8,128)(2,1)} %get-tuple-element.6), channel_id=1, source_target_pairs={{508,0},{509,1},{510,2},{511,3},{0,4},{1,5},{2,6},{3,7},{4,8},{5,9... | collective-permute-start | bytes 786440 | tf_op jit(solution)/shard_map/ppermute | solution.py:20
  105.5 20.7 %copy-start.18 = (bf16[512,256]{1,0:T(8,128)(2,1)}, bf16[512,256]{1,0:T(8,128)(2,1)S(1)}, u32[]{:S(2)}) copy-start(bf16[512,256]{1,0:T(8,128)(2,1)S(1)} %collective-permute-done.10) | copy-start | bytes 786436
  105.5 13.0 %collective-permute-start.14 = (bf16[512,256]{1,0:T(8,128)(2,1)S(1)}, bf16[512,256]{1,0:T(8,128)(2,1)S(1)}, u32[]{:S(2)}, u32[]{:S(2)}) collective-permute-start(bf16[512,256]{1,0:T(8,128)(2,1)S(1)} %copy-done.5), channel_id=1, source_target_pairs={{504,0},{505,1},{506,2},{507,3},{508,4},{509,5},{510,6},{511,7},{0... | collective-permute-start | bytes 786440 | tf_op jit(solution)/shard_map/ppermute | solution.py:20
  111.3 15.1 %copy-start.20 = (bf16[512,256]{1,0:T(8,128)(2,1)}, bf16[512,256]{1,0:T(8,128)(2,1)S(1)}, u32[]{:S(2)}) copy-start(bf16[512,256]{1,0:T(8,128)(2,1)S(1)} %collective-permute-done.12) | copy-start | bytes 786436
  111.3 9.5 %collective-permute-start.2 = (bf16[512,256]{1,0:T(8,128)(2,1)S(1)}, bf16[512,256]{1,0:T(8,128)(2,1)S(1)}, u32[]{:S(2)}, u32[]{:S(2)}) collective-permute-start(bf16[512,256]{1,0:T(8,128)(2,1)S(1)} %copy-done.4), channel_id=1, source_target_pairs={{2,0},{3,1},{4,2},{5,3},{6,4},{7,5},{8,6},{9,7},{10,8},{11,9},{12,... | collective-permute-start | bytes 786440 | tf_op jit(solution)/shard_map/ppermute | solution.py:20
  118.5 8.2 %copy-start.10 = (bf16[512,256]{1,0:T(8,128)(2,1)}, bf16[512,256]{1,0:T(8,128)(2,1)S(1)}, u32[]{:S(2)}) copy-start(bf16[512,256]{1,0:T(8,128)(2,1)S(1)} %collective-permute-done.14) | copy-start | bytes 786436
  118.5 23.7 %collective-permute-start.9 = (f32[128,128]{1,0:T(8,128)}, f32[128,128]{1,0:T(8,128)S(1)}, u32[]{:S(2)}, u32[]{:S(2)}) collective-permute-start(f32[128,128]{1,0:T(8,128)} %get-tuple-element.26), channel_id=1, source_target_pairs={{511,0},{0,1},{1,2},{2,3},{3,4},{4,5},{5,6},{6,7},{7,8},{8,9},{9,1... | collective-permute-start | bytes 196616 | tf_op jit(solution)/shard_map/ppermute | solution.py:20
  120.8 21.6 %collective-permute-start.11 = (f32[128,128]{1,0:T(8,128)}, f32[128,128]{1,0:T(8,128)S(1)}, u32[]{:S(2)}, u32[]{:S(2)}) collective-permute-start(f32[128,128]{1,0:T(8,128)} %get-tuple-element.26), channel_id=1, source_target_pairs={{510,0},{511,1},{0,2},{1,3},{2,4},{3,5},{4,6},{5,7},{6,8},{7,9},{8... | collective-permute-start | bytes 196616 | tf_op jit(solution)/shard_map/ppermute | solution.py:20
  123.0 6.2 %copy-start.49 = (f32[128,128]{1,0:T(8,128)S(1)}, f32[128,128]{1,0:T(8,128)}, u32[]{:S(2)}) copy-start(f32[128,128]{1,0:T(8,128)} %fusion.107) | copy-start | bytes 196612
  124.2 8.2 %copy-start.33 = (f32[128,128]{1,0:T(8,128)}, f32[128,128]{1,0:T(8,128)S(1)}, u32[]{:S(2)}) copy-start(f32[128,128]{1,0:T(8,128)S(1)} %fusion.22) | copy-start | bytes 196612
  124.5 18.0 %copy-start.21 = (f32[128,128]{1,0:T(8,128)}, f32[128,128]{1,0:T(8,128)S(1)}, u32[]{:S(2)}) copy-start(f32[128,128]{1,0:T(8,128)S(1)} %fusion.28) | copy-start | bytes 196612
  124.7 18.2 %copy-start.23 = (f32[128,128]{1,0:T(8,128)}, f32[128,128]{1,0:T(8,128)S(1)}, u32[]{:S(2)}) copy-start(f32[128,128]{1,0:T(8,128)S(1)} %fusion.29) | copy-start | bytes 196612
  126.0 17.0 %copy-start.25 = (f32[128,128]{1,0:T(8,128)}, f32[128,128]{1,0:T(8,128)S(1)}, u32[]{:S(2)}) copy-start(f32[128,128]{1,0:T(8,128)S(1)} %fusion.30) | copy-start | bytes 196612
  126.2 16.7 %copy-start.27 = (f32[128,128]{1,0:T(8,128)}, f32[128,128]{1,0:T(8,128)S(1)}, u32[]{:S(2)}) copy-start(f32[128,128]{1,0:T(8,128)S(1)} %fusion.31) | copy-start | bytes 196612
  126.5 16.5 %copy-start.29 = (f32[128,128]{1,0:T(8,128)}, f32[128,128]{1,0:T(8,128)S(1)}, u32[]{:S(2)}) copy-start(f32[128,128]{1,0:T(8,128)S(1)} %fusion.32) | copy-start | bytes 196612
  126.5 17.6 %copy-start.9 = (f32[128,128]{1,0:T(8,128)S(1)}, f32[128,128]{1,0:T(8,128)}, u32[]{:S(2)}) copy-start(f32[128,128]{1,0:T(8,128)} %copy-done.8) | copy-start | bytes 196612
  126.7 16.2 %copy-start.31 = (f32[128,128]{1,0:T(8,128)}, f32[128,128]{1,0:T(8,128)S(1)}, u32[]{:S(2)}) copy-start(f32[128,128]{1,0:T(8,128)S(1)} %fusion.33) | copy-start | bytes 196612
  127.0 35.6 %copy-start.35 = (f32[128,128]{1,0:T(8,128)}, f32[128,128]{1,0:T(8,128)S(1)}, u32[]{:S(2)}) copy-start(f32[128,128]{1,0:T(8,128)S(1)} %fusion.23) | copy-start | bytes 196612
  127.0 15.7 %collective-permute-start.13 = (f32[128,128]{1,0:T(8,128)}, f32[128,128]{1,0:T(8,128)S(1)}, u32[]{:S(2)}, u32[]{:S(2)}) collective-permute-start(f32[128,128]{1,0:T(8,128)} %get-tuple-element.26), channel_id=1, source_target_pairs={{508,0},{509,1},{510,2},{511,3},{0,4},{1,5},{2,6},{3,7},{4,8},{5,9... | collective-permute-start | bytes 196616 | tf_op jit(solution)/shard_map/ppermute | solution.py:20
  130.3 12.9 %copy-start.37 = (f32[128,128]{1,0:T(8,128)}, f32[128,128]{1,0:T(8,128)S(1)}, u32[]{:S(2)}) copy-start(f32[128,128]{1,0:T(8,128)S(1)} %collective-permute-done.5) | copy-start | bytes 196612
  130.3 12.7 %collective-permute-start.15 = (f32[128,128]{1,0:T(8,128)}, f32[128,128]{1,0:T(8,128)S(1)}, u32[]{:S(2)}, u32[]{:S(2)}) collective-permute-start(f32[128,128]{1,0:T(8,128)} %get-tuple-element.26), channel_id=1, source_target_pairs={{504,0},{505,1},{506,2},{507,3},{508,4},{509,5},{510,6},{511,7},{0... | collective-permute-start | bytes 196616 | tf_op jit(solution)/shard_map/ppermute | solution.py:20
  132.4 10.8 %collective-permute-start.3 = (f32[128,128]{1,0:T(8,128)}, f32[128,128]{1,0:T(8,128)S(1)}, u32[]{:S(2)}, u32[]{:S(2)}) collective-permute-start(f32[128,128]{1,0:T(8,128)} %get-tuple-element.26), channel_id=1, source_target_pairs={{2,0},{3,1},{4,2},{5,3},{6,4},{7,5},{8,6},{9,7},{10,8},{11,9},{12,... | collective-permute-start | bytes 196616 | tf_op jit(solution)/shard_map/ppermute | solution.py:20
  142.2 23.2 %copy-start.41 = (f32[128,128]{1,0:T(8,128)}, f32[128,128]{1,0:T(8,128)S(1)}, u32[]{:S(2)}) copy-start(f32[128,128]{1,0:T(8,128)S(1)} %collective-permute-done.9) | copy-start | bytes 196612
  142.4 23.0 %copy-start.42 = (f32[128,128]{1,0:T(8,128)}, f32[128,128]{1,0:T(8,128)S(1)}, u32[]{:S(2)}) copy-start(f32[128,128]{1,0:T(8,128)S(1)} %collective-permute-done.11) | copy-start | bytes 196612
  143.2 42.6 %copy-start.19 = (bf16[512,256]{1,0:T(8,128)(2,1)S(1)}, bf16[512,256]{1,0:T(8,128)(2,1)}, u32[]{:S(2)}) copy-start(bf16[512,256]{1,0:T(8,128)(2,1)} %copy-done.18) | copy-start | bytes 786436
  143.2 22.2 %copy-start.45 = (f32[128,128]{1,0:T(8,128)}, f32[128,128]{1,0:T(8,128)S(1)}, u32[]{:S(2)}) copy-start(f32[128,128]{1,0:T(8,128)S(1)} %collective-permute-done.3) | copy-start | bytes 196612
  145.0 46.2 %copy-start.15 = (bf16[512,256]{1,0:T(8,128)(2,1)S(1)}, bf16[512,256]{1,0:T(8,128)(2,1)}, u32[]{:S(2)}) copy-start(bf16[512,256]{1,0:T(8,128)(2,1)} %copy-done.14) | copy-start | bytes 786436
  145.0 51.1 %collective-permute-start.16 = (f32[128,128]{1,0:T(8,128)S(1)}, f32[128,128]{1,0:T(8,128)}, u32[]{:S(2)}, u32[]{:S(2)}) collective-permute-start(f32[128,128]{1,0:T(8,128)S(1)} %get-tuple-element.28), channel_id=1, source_target_pairs={{1,0},{2,1},{3,2},{4,3},{5,4},{6,5},{7,6},{8,7},{9,8},{10,9},{11,1... | collective-permute-start | bytes 196616 | tf_op jit(solution)/shard_map/ppermute | solution.py:20
  148.7 44.2 %collective-permute-start.18 = (f32[128,128]{1,0:T(8,128)S(1)}, f32[128,128]{1,0:T(8,128)}, u32[]{:S(2)}, u32[]{:S(2)}) collective-permute-start(f32[128,128]{1,0:T(8,128)S(1)} %get-tuple-element.28), channel_id=1, source_target_pairs={{4,0},{5,1},{6,2},{7,3},{8,4},{9,5},{10,6},{11,7},{12,8},{13,9},{1... | collective-permute-start | bytes 196616 | tf_op jit(solution)/shard_map/ppermute | solution.py:20
  153.2 38.0 %collective-permute-start.19 = (f32[128,128]{1,0:T(8,128)S(1)}, f32[128,128]{1,0:T(8,128)}, u32[]{:S(2)}, u32[]{:S(2)}) collective-permute-start(f32[128,128]{1,0:T(8,128)S(1)} %get-tuple-element.28), channel_id=1, source_target_pairs={{8,0},{9,1},{10,2},{11,3},{12,4},{13,5},{14,6},{15,7},{16,8},{17,9... | collective-permute-start | bytes 196616 | tf_op jit(solution)/shard_map/ppermute | solution.py:20
  156.9 30.5 %collective-permute-start.20 = (f32[128,128]{1,0:T(8,128)S(1)}, f32[128,128]{1,0:T(8,128)}, u32[]{:S(2)}, u32[]{:S(2)}) collective-permute-start(f32[128,128]{1,0:T(8,128)S(1)} %get-tuple-element.28), channel_id=1, source_target_pairs={{511,0},{0,1},{1,2},{2,3},{3,4},{4,5},{5,6},{6,7},{7,8},{8,9},{9,1... | collective-permute-start | bytes 196616 | tf_op jit(solution)/shard_map/ppermute | solution.py:20
  162.6 10.8 %collective-permute-start.22 = (f32[128,128]{1,0:T(8,128)S(1)}, f32[128,128]{1,0:T(8,128)}, u32[]{:S(2)}, u32[]{:S(2)}) collective-permute-start(f32[128,128]{1,0:T(8,128)S(1)} %get-tuple-element.28), channel_id=1, source_target_pairs={{508,0},{509,1},{510,2},{511,3},{0,4},{1,5},{2,6},{3,7},{4,8},{5,9... | collective-permute-start | bytes 196616 | tf_op jit(solution)/shard_map/ppermute | solution.py:20
  165.7 27.2 %copy-start.38 = (f32[128,128]{1,0:T(8,128)S(1)}, f32[128,128]{1,0:T(8,128)}, u32[]{:S(2)}) copy-start(f32[128,128]{1,0:T(8,128)} %copy-done.37) | copy-start | bytes 196612
  165.9 27.0 %copy-start.13 = (bf16[512,256]{1,0:T(8,128)(2,1)S(1)}, bf16[512,256]{1,0:T(8,128)(2,1)}, u32[]{:S(2)}) copy-start(bf16[512,256]{1,0:T(8,128)(2,1)} %copy-done.12) | copy-start | bytes 786436
  165.9 28.7 %copy-start.17 = (bf16[512,256]{1,0:T(8,128)(2,1)S(1)}, bf16[512,256]{1,0:T(8,128)(2,1)}, u32[]{:S(2)}) copy-start(bf16[512,256]{1,0:T(8,128)(2,1)} %copy-done.16) | copy-start | bytes 786436
  165.9 28.7 %copy-start.46 = (f32[128,128]{1,0:T(8,128)S(1)}, f32[128,128]{1,0:T(8,128)}, u32[]{:S(2)}) copy-start(f32[128,128]{1,0:T(8,128)} %copy-done.45) | copy-start | bytes 196612
  173.4 10.4 %collective-permute-start.21 = (f32[128,128]{1,0:T(8,128)S(1)}, f32[128,128]{1,0:T(8,128)S(1)}, u32[]{:S(2)}, u32[]{:S(2)}) collective-permute-start(f32[128,128]{1,0:T(8,128)S(1)} %get-tuple-element.28), channel_id=1, source_target_pairs={{510,0},{511,1},{0,2},{1,3},{2,4},{3,5},{4,6},{5,7},{6,8},{7,9},{8... | collective-permute-start | bytes 196616 | tf_op jit(solution)/shard_map/ppermute | solution.py:20
  177.2 21.4 %copy-start.63 = (s32[512,1]{0,1:T(1,128)S(1)}, s32[512,1]{0,1:T(1,128)}, u32[]{:S(2)}) copy-start(s32[512,1]{0,1:T(1,128)} %get-tuple-element.16) | copy-start | bytes 6148
  183.9 40.7 %collective-permute-start.23 = (f32[128,128]{1,0:T(8,128)S(1)}, f32[128,128]{1,0:T(8,128)}, u32[]{:S(2)}, u32[]{:S(2)}) collective-permute-start(f32[128,128]{1,0:T(8,128)S(1)} %get-tuple-element.28), channel_id=1, source_target_pairs={{504,0},{505,1},{506,2},{507,3},{508,4},{509,5},{510,6},{511,7},{0... | collective-permute-start | bytes 196616 | tf_op jit(solution)/shard_map/ppermute | solution.py:20
  187.5 7.1 %collective-permute-start.17 = (f32[128,128]{1,0:T(8,128)S(1)}, f32[128,128]{1,0:T(8,128)S(1)}, u32[]{:S(2)}, u32[]{:S(2)}) collective-permute-start(f32[128,128]{1,0:T(8,128)S(1)} %get-tuple-element.28), channel_id=1, source_target_pairs={{2,0},{3,1},{4,2},{5,3},{6,4},{7,5},{8,6},{9,7},{10,8},{11,9},{12,... | collective-permute-start | bytes 196616 | tf_op jit(solution)/shard_map/ppermute | solution.py:20
  238.6 6.5 %copy-start.34 = (f32[128,128]{1,0:T(8,128)S(1)}, f32[128,128]{1,0:T(8,128)}, u32[]{:S(2)}) copy-start(f32[128,128]{1,0:T(8,128)} %copy-done.33) | copy-start | bytes 196612
  238.6 6.5 %copy-start.48 = (f32[128,128]{1,0:T(8,128)S(1)}, f32[128,128]{1,0:T(8,128)}, u32[]{:S(2)}) copy-start(f32[128,128]{1,0:T(8,128)} %fusion.118) | copy-start | bytes 196612
  238.6 7.5 %copy-start.36 = (f32[128,128]{1,0:T(8,128)S(1)}, f32[128,128]{1,0:T(8,128)}, u32[]{:S(2)}) copy-start(f32[128,128]{1,0:T(8,128)} %copy-done.35) | copy-start | bytes 196612
  238.6 7.5 %copy-start.50 = (f32[128,128]{1,0:T(8,128)S(1)}, f32[128,128]{1,0:T(8,128)}, u32[]{:S(2)}) copy-start(f32[128,128]{1,0:T(8,128)} %get-tuple-element.29) | copy-start | bytes 196612
  238.6 7.5 %copy-start.52 = (f32[128,128]{1,0:T(8,128)S(1)}, f32[128,128]{1,0:T(8,128)}, u32[]{:S(2)}) copy-start(f32[128,128]{1,0:T(8,128)} %copy-done.51) | copy-start | bytes 196612
  (26 other events, 85.6 us)
where the time goes:
time: 249 us; the launch traced here: 247 us
  starting transfers between devices  91 us (37%)
  matrix products  45.2 us (18%)
  other arithmetic  39.6 us (16%)
  local copies, waits for them, and re-layouts  32.9 us (13%)
  waiting for transfers between devices  31.2 us (13%)
  between operations  7.17 us (3%)
    ppermute x24, starting transfers between devices, shifted(): return lax.ppermute(block, axis, route)  91 us
    ppermute x24, waiting for transfers between devices, shifted(): return lax.ppermute(block, axis, route)  31.2 us
    scatter-add x8, other arithmetic, per_device(): summed.at[row_lists[slot_id]]  29.2 us
    gather x1, local copies, waits for them, and re-layouts, per_device(): images[row_lists]  14.9 us
    dot_general x8, matrix products, per_device(): jnp.dot(basis_rows[slot_id], partner_coeffs, preferred_element_type=jnp.f...  14 us
    gather x1, local copies, waits for them, and re-layouts, per_device(): deflation[row_lists]  12.1 us
    dot_general x16, matrix products, apply_coarse(): jnp.dot(pair_blocks[slot_id], remote, precision=lax.Precision.HIGHEST)  11.3 us
    dot_general x18, matrix products, cross(): lax.dot_general(left, right, (((0,), (0,)), ((), ())), preferred_element_...  10.8 us
  transfers between devices with their start and end apart: 24, of which 7 were waited for; matrix products, arithmetic and copies ran while one was open for 37% of the time, Pallas kernels for 0%

commit v1 on v0

v1 whole, which is shorter than its diff:
```python
import functools

import jax
import jax.numpy as jnp
from jax import lax
from jax.experimental import pallas as pl
from jax.experimental.pallas import tpu as pltpu
from jax.sharding import PartitionSpec as P

BLK = 128
TPR = 6
NB = 8
OV = 512
NLOC = 1024
K = 128
CHEB_CENTER = 2.5
CHEB_HALF = 1.5
RHO_FIRST = CHEB_HALF / CHEB_CENTER
RHO_SECOND = 1.0 / (2.0 * CHEB_CENTER / CHEB_HALF - RHO_FIRST)
F32 = jnp.float32
BF16 = jnp.bfloat16
VMEM = pl.BlockSpec(memory_space=pltpu.VMEM)
SMEM = pl.BlockSpec(memory_space=pltpu.SMEM)
NT = (((1,), (1,)), ((), ()))
STEPS = tuple((power, colour) for power in range(4) for colour in (0, 1))


def swapped(block, power, colour):
    n, o = lax.axis_size("sub"), 1 << power
    route = [(i, (i + o) % n if (i // o) % 2 == colour else (i - o) % n) for i in range(n)]
    return lax.ppermute(block, "sub", route)


def slot_of(step, me):
    power, colour = STEPS[step]
    bit = lax.rem(lax.div(me, 1 << power), 2)
    return power + 4 * (bit if colour == 0 else 1 - bit)


def split(x):
    hi = x.astype(BF16)
    return hi, (x - hi.astype(F32)).astype(BF16)


def column(diag_ref, b):
    return jnp.broadcast_to(diag_ref[b : b + 1, :], (BLK, BLK)).T


def tile_row(cols_ref, tiles_ref, v_ref, b):
    acc = None
    for t in range(TPR * b, TPR * (b + 1)):
        rows = pl.ds(pl.multiple_of(cols_ref[t] * BLK, BLK), BLK)
        term = jnp.dot(tiles_ref[t], v_ref[rows, :], preferred_element_type=F32)
        acc = term if acc is None else acc + term
    return acc


def picks(margin_ref, slot):
    rows = margin_ref[pl.ds(slot, 1), :]
    ids = lax.broadcasted_iota(jnp.int32, (NLOC, OV), 0)
    return jnp.where(ids == rows, 1.0, 0.0).astype(BF16)


def prepare(cols_ref, z_ref, tiles_ref, diag_ref, rhs_ref, margin_ref, *rest):
    payloads, (own_ref, coarse_ref), (zit, im_rhs) = rest[:8], rest[8:10], rest[10:]
    me = lax.axis_index("sub")
    for b in range(NB):
        rows = slice(b * BLK, (b + 1) * BLK)
        z = z_ref[rows, :]
        image = (column(diag_ref, b) * z.astype(F32) + tile_row(cols_ref, tiles_ref, z_ref, b)).astype(BF16)
        zit[:K, rows] = z.T
        zit[K:, rows] = image.T
        im_rhs[rows, :K] = image
        im_rhs[rows, K:] = rhs_ref[rows, :]
    both = jnp.dot(zit[:K, :], im_rhs[...], preferred_element_type=F32)
    own_ref[...] = both[:, :K]
    coarse = both[:, K:]
    coarse_ref[...] = coarse
    hi, lo = split(coarse / CHEB_CENTER)
    for step, out in enumerate(payloads):
        onehot = picks(margin_ref, slot_of(step, me))
        out[:, :OV] = jnp.dot(zit[...], onehot, preferred_element_type=F32).astype(BF16)
        out[:K, OV:] = hi
        out[K:, OV:] = lo


def apply_split(e_hi, e_lo, v_hi, v_lo):
    dot = functools.partial(jnp.dot, preferred_element_type=F32)
    return dot(e_hi, v_hi) + (dot(e_lo, v_hi) + dot(e_hi, v_lo))


def iterate(adj_ref, own_ref, coarse_ref, *rest):
    mine, theirs = rest[:8], rest[8:16]
    ehi_ref, elo_ref, resid_ref, second_ref, send_ref, v_ref = rest[16:]
    me = lax.axis_index("sub")
    coarse = coarse_ref[...]
    first = coarse / CHEB_CENTER
    ehi_ref[:, :K], elo_ref[:, :K] = split(own_ref[...])
    v_ref[:K, :K], v_ref[:K, K:] = split(first)
    for step in range(8):
        block = lax.dot_general(mine[step][:, :OV], theirs[step][:, :OV], NT, preferred_element_type=F32)
        weight = adj_ref[0, slot_of(step, me)].astype(F32) * 0.5
        cols = slice((step + 1) * K, (step + 2) * K)
        ehi_ref[:, cols], elo_ref[:, cols] = split((block[:K, K:] + block[K:, :K]) * weight)
        v_ref[cols, :K] = theirs[step][:K, OV:]
        v_ref[cols, K:] = theirs[step][K:, OV:]
    image = apply_split(ehi_ref[...], elo_ref[...], v_ref[:, :K], v_ref[:, K:])
    resid = coarse - image
    second = RHO_SECOND * RHO_FIRST * first + (2.0 * RHO_SECOND / CHEB_HALF) * resid
    resid_ref[...] = resid
    second_ref[...] = second
    send_ref[:, :K], send_ref[:, K:] = split(second)


def finish(cols_ref, adj_ref, z_ref, tiles_ref, diag_ref, rhs_ref, margin_ref, coarse_ref, ehi_ref, elo_ref, resid_ref, second_ref, *rest):
    theirs, seconds = rest[:8], rest[8:16]
    fine_ref, coarse_out, v_ref, summed, merged = rest[16:]
    me = lax.axis_index("sub")
    second = second_ref[...]
    v_ref[:K, :K], v_ref[:K, K:] = split(second)
    coeffs = (coarse_ref[...] / CHEB_CENTER + second).astype(BF16)
    local = jnp.dot(z_ref[...], coeffs, preferred_element_type=F32)
    summed[...] = local.astype(BF16).astype(F32)
    for step in range(8):
        cols = slice((step + 1) * K, (step + 2) * K)
        arrived_second = seconds[step][...]
        v_ref[cols, :] = arrived_second
        parts = theirs[step][:K, OV:].astype(F32) + theirs[step][K:, OV:].astype(F32)
        parts += arrived_second[:, :K].astype(F32) + arrived_second[:, K:].astype(F32)
        slot = slot_of(step, me)
        corr = jnp.dot(parts.T.astype(BF16), theirs[step][:K, :OV], preferred_element_type=F32).astype(BF16)
        corr = corr * adj_ref[0, slot].astype(BF16)
        summed[...] += lax.dot_general(picks(margin_ref, slot), corr, NT, preferred_element_type=F32)
    coarse_out[...] = resid_ref[...] - apply_split(ehi_ref[...], elo_ref[...], v_ref[:, :K], v_ref[:, K:])
    merged[...] = summed[...].astype(BF16)
    for b in range(NB):
        rows = slice(b * BLK, (b + 1) * BLK)
        image = column(diag_ref, b) * merged[rows, :].astype(F32) + tile_row(cols_ref, tiles_ref, merged, b)
        fine_ref[rows, :] = (rhs_ref[rows, :].astype(F32) - image).astype(BF16)


PARAMS = pltpu.CompilerParams(vmem_limit_bytes=48 * 1024 * 1024)


def arr(shape, dtype):
    return jax.ShapeDtypeStruct(shape, dtype)


def per_device(deflation, op_tiles, tile_cols, diag_coef, fine_rhs, adjacency, margin_rows):
    diag = diag_coef.reshape(NB, BLK)
    margin = margin_rows[0]
    *payloads, own, coarse = pl.pallas_call(
        prepare,
        name="prepare",
        in_specs=[SMEM] + [VMEM] * 5,
        out_specs=[VMEM] * 10,
        out_shape=[arr((2 * K, OV + K), BF16)] * 8 + [arr((K, K), F32)] * 2,
        scratch_shapes=[pltpu.VMEM((2 * K, NLOC), BF16), pltpu.VMEM((NLOC, 2 * K), BF16)],
        compiler_params=PARAMS,
    )(tile_cols, deflation, op_tiles, diag, fine_rhs, margin)
    theirs = [swapped(block, *step) for block, step in zip(payloads, STEPS)]
    ehi, elo, resid, second, send = pl.pallas_call(
        iterate,
        name="iterate",
        in_specs=[SMEM] + [VMEM] * 18,
        out_specs=[VMEM] * 5,
        out_shape=[arr((K, 9 * K), BF16)] * 2 + [arr((K, K), F32)] * 2 + [arr((K, 2 * K), BF16)],
        scratch_shapes=[pltpu.VMEM((9 * K, 2 * K), BF16)],
        compiler_params=PARAMS,
    )(adjacency, own, coarse, *payloads, *theirs)
    seconds = [swapped(send, *step) for step in STEPS]
    return tuple(
        pl.pallas_call(
            finish,
            name="finish",
            in_specs=[SMEM] * 2 + [VMEM] * 26,
            out_specs=[VMEM] * 2,
            out_shape=[arr((NLOC, K), BF16), arr((K, K), F32)],
            scratch_shapes=[
                pltpu.VMEM((9 * K, 2 * K), BF16),
                pltpu.VMEM((NLOC, K), F32),
                pltpu.VMEM((NLOC, K), BF16),
            ],
            compiler_params=PARAMS,
        )(tile_cols, adjacency, deflation, op_tiles, diag, fine_rhs, margin, coarse, ehi, elo, resid, second, *theirs, *seconds)
    )


def solution(mesh):
    return jax.shard_map(
        per_device,
        mesh=mesh,
        in_specs=(P("sub", None), P("sub", None, None), P("sub"), P("sub"), P("sub", None), P("sub", None), P("sub", None, None)),
        out_specs=(P("sub", None), P("sub", None)),
        check_vma=False,
    )
```

time: 249 us -> 100 us (0.40)
  matrix products: 45.2 us -> 0 us
  other arithmetic: 39.6 us -> 0 us
  local copies, waits for them, and re-layouts: 32.9 us -> 5.38 us
  starting transfers between devices: 91 us -> 70.1 us
  waiting for transfers between devices: 31.2 us -> 10.8 us
  Pallas kernels: 0 us -> 12.2 us
  between operations: 7.17 us -> 0.89 us
    dot_general x47 -> x0, matrix products: 45.2 us -> none  [the longest x8 14 us: per_device(): jnp.dot(basis_rows[slot_id], partner_coeffs, preferred_element_type=jnp.f...]
    gather x4 -> x0, local copies, waits for them, and re-layouts: 30 us -> none  [the longest x1 14.9 us: per_device(): images[row_lists]]
    scatter-add x8 -> x0, other arithmetic: 29.2 us -> none  [per_device(): summed.at[row_lists[slot_id]]]
    ppermute x24 -> x16, starting transfers between devices: 91 us -> 70.1 us  [swapped(): return lax.ppermute(block, 'sub', route)]
    ppermute x24 -> x16, waiting for transfers between devices: 31.2 us -> 10.8 us  [swapped(): return lax.ppermute(block, 'sub', route)]
    pallas_call x0 -> x3, Pallas kernels: none -> 12.2 us  [the longest x1 7.1 us: per_device(): pl.pallas_call(finish, name='finish', in_specs=[SMEM] * 2 + [VMEM] * 26,...]
    unnamed x133 -> x20, local copies, waits for them, and re-layouts: 0.88 us -> 5.38 us
    reduce_sum x2 -> x0, other arithmetic: 4.28 us -> none  [tile_apply(): products.reshape(block_n, TPR, BLK, columns_n).sum(axis=1)]
  transfers between devices with their start and end apart: 24 -> 16, of which waited for: 7 -> 4; matrix products, arithmetic and copies ran while one was open for 37% -> 0% of each run, Pallas kernels for 0% -> 0%
where the time goes in v1:
time: 100 us; the launch traced here: 99.5 us
  starting transfers between devices  70.1 us (70%)
  Pallas kernels  12.2 us (12%)
  waiting for transfers between devices  10.8 us (11%)
  local copies, waits for them, and re-layouts  5.38 us (5%)
    ppermute x16, starting transfers between devices, swapped(): return lax.ppermute(block, 'sub', route)  70.1 us
    ppermute x16, waiting for transfers between devices, swapped(): return lax.ppermute(block, 'sub', route)  10.8 us
    pallas_call x1, Pallas kernels, per_device(): pl.pallas_call(finish, name='finish', in_specs=[SMEM] * 2 + [VMEM] * 26,...  7.1 us
    unnamed x20, local copies, waits for them, and re-layouts  5.38 us
    pallas_call x1, Pallas kernels, per_device(): pl.pallas_call(prepare, name='prepare', in_specs=[SMEM] + [VMEM] * 5, out...  3.5 us
  transfers between devices with their start and end apart: 16, of which 4 were waited for; matrix products, arithmetic and copies ran while one was open for 0% of the time, Pallas kernels for 0%

profile of v1, /device:TPU:1, one launch (start us, length us, event | category | flops | bytes accessed | tf_op | source)
XLA Modules:
  0.0 99.5 jit_solution(1947934861706178413)
XLA Ops:
  0.6 0.0 copy-start.9
  0.6 0.0 copy-start
  0.7 1.4 %copy-done = bf16[48,128,128]{2,1,0:T(8,128)(2,1)S(1)} copy-done((bf16[48,128,128]{2,1,0:T(8,128)(2,1)S(1)}, bf16[48,128,128]{2,1,0:T(8,128)(2,1)}, u32[]{:S(2)}) %copy-start) | copy-done | bytes 1572888
  2.1 0.0 copy-start.2
  2.1 0.9 copy-done.2
  3.0 0.0 copy-start.4
  3.0 0.9 copy-done.4
  4.0 0.0 copy-start.6
  4.0 0.7 copy-done.6
  4.7 0.0 copy-start.7
  4.7 0.7 copy-done.7
  5.4 0.0 copy-start.8
  5.4 0.7 copy-done.8
  6.0 3.5 %prepare.1 = (bf16[256,640]{1,0:T(8,128)(2,1)S(1)}, bf16[256,640]{1,0:T(8,128)(2,1)S(1)}, bf16[256,640]{1,0:T(8,128)(2,1)S(1)}, bf16[256,640]{1,0:T(8,128)(2,1)S...) custom-call(s32[48]{0:T(128)S(1)} %copy-done.8, ...), custom_call_target="tpu_custom_call" | custom-call | tf_op jit(solution)/shard_map/prepare/pallas_call | solution.py:152
  9.5 8.8 %collective-permute-start = (bf16[256,640]{1,0:T(8,128)(2,1)S(1)}, bf16[256,640]{1,0:T(8,128)(2,1)S(1)}, u32[]{:S(2)}, u32[]{:S(2)}) collective-permute-start(bf16[256,640]{1,0:T(8,128)(2,1)S(1)} %get-tuple-element.19.rest_0_), channel_id=1, source_target_pairs={{0,1},{1,0},{2,3},{3,2},{4,5},{5,4},{6,7},{7,6},{8,9},{9,8},{10,11... | collective-permute-start | bytes 983048 | tf_op jit(solution)/shard_map/ppermute | solution.py:31
  18.3 1.9 %collective-permute-start.1 = (bf16[256,640]{1,0:T(8,128)(2,1)S(1)}, bf16[256,640]{1,0:T(8,128)(2,1)S(1)}, u32[]{:S(2)}, u32[]{:S(2)}) collective-permute-start(bf16[256,640]{1,0:T(8,128)(2,1)S(1)} %get-tuple-element.20.rest_1_), channel_id=1, source_target_pairs={{0,511},{1,2},{2,1},{3,4},{4,3},{5,6},{6,5},{7,8},{8,7},{9,10},{10... | collective-permute-start | bytes 983048 | tf_op jit(solution)/shard_map/ppermute | solution.py:31
  20.2 1.9 %collective-permute-start.2 = (bf16[256,640]{1,0:T(8,128)(2,1)S(1)}, bf16[256,640]{1,0:T(8,128)(2,1)S(1)}, u32[]{:S(2)}, u32[]{:S(2)}) collective-permute-start(bf16[256,640]{1,0:T(8,128)(2,1)S(1)} %get-tuple-element.21.rest_2_), channel_id=1, source_target_pairs={{0,2},{1,3},{2,0},{3,1},{4,6},{5,7},{6,4},{7,5},{8,10},{9,11},{10,... | collective-permute-start | bytes 983048 | tf_op jit(solution)/shard_map/ppermute | solution.py:31
  22.2 11.8 %collective-permute-start.3 = (bf16[256,640]{1,0:T(8,128)(2,1)S(1)}, bf16[256,640]{1,0:T(8,128)(2,1)S(1)}, u32[]{:S(2)}, u32[]{:S(2)}) collective-permute-start(bf16[256,640]{1,0:T(8,128)(2,1)S(1)} %get-tuple-element.22.rest_3_), channel_id=1, source_target_pairs={{0,510},{1,511},{2,4},{3,5},{4,2},{5,3},{6,8},{7,9},{8,6},{9,7},{1... | collective-permute-start | bytes 983048 | tf_op jit(solution)/shard_map/ppermute | solution.py:31
  33.9 1.9 %collective-permute-start.4 = (bf16[256,640]{1,0:T(8,128)(2,1)S(1)}, bf16[256,640]{1,0:T(8,128)(2,1)S(1)}, u32[]{:S(2)}, u32[]{:S(2)}) collective-permute-start(bf16[256,640]{1,0:T(8,128)(2,1)S(1)} %get-tuple-element.23.rest_4_), channel_id=1, source_target_pairs={{0,4},{1,5},{2,6},{3,7},{4,0},{5,1},{6,2},{7,3},{8,12},{9,13},{10,... | collective-permute-start | bytes 983048 | tf_op jit(solution)/shard_map/ppermute | solution.py:31
  35.9 0.0 collective-permute-done.rest_8_.rest_0_
  35.9 5.7 %collective-permute-start.5 = (bf16[256,640]{1,0:T(8,128)(2,1)S(1)}, bf16[256,640]{1,0:T(8,128)(2,1)S(1)}, u32[]{:S(2)}, u32[]{:S(2)}) collective-permute-start(bf16[256,640]{1,0:T(8,128)(2,1)S(1)} %get-tuple-element.24.rest_5_), channel_id=1, source_target_pairs={{0,508},{1,509},{2,510},{3,511},{4,8},{5,9},{6,10},{7,11},{8,4},{9... | collective-permute-start | bytes 983048 | tf_op jit(solution)/shard_map/ppermute | solution.py:31
  41.5 0.0 collective-permute-done.1.rest_9_.rest_1_
  41.6 2.3 %collective-permute-start.6 = (bf16[256,640]{1,0:T(8,128)(2,1)S(1)}, bf16[256,640]{1,0:T(8,128)(2,1)S(1)}, u32[]{:S(2)}, u32[]{:S(2)}) collective-permute-start(bf16[256,640]{1,0:T(8,128)(2,1)S(1)} %get-tuple-element.25.rest_6_), channel_id=1, source_target_pairs={{0,8},{1,9},{2,10},{3,11},{4,12},{5,13},{6,14},{7,15},{8,0},{9,1},... | collective-permute-start | bytes 983048 | tf_op jit(solution)/shard_map/ppermute | solution.py:31
  43.9 0.0 collective-permute-done.2.rest_10_.rest_2_
  43.9 3.6 %collective-permute-start.7 = (bf16[256,640]{1,0:T(8,128)(2,1)S(1)}, bf16[256,640]{1,0:T(8,128)(2,1)S(1)}, u32[]{:S(2)}, u32[]{:S(2)}) collective-permute-start(bf16[256,640]{1,0:T(8,128)(2,1)S(1)} %get-tuple-element.26.rest_7_), channel_id=1, source_target_pairs={{0,504},{1,505},{2,506},{3,507},{4,508},{5,509},{6,510},{7,511},{8... | collective-permute-start | bytes 983048 | tf_op jit(solution)/shard_map/ppermute | solution.py:31
  47.5 0.0 collective-permute-done.3.rest_11_.rest_3_
  47.5 8.1 %collective-permute-done.4.rest_12_.rest_4_ = bf16[256,640]{1,0:T(8,128)(2,1)S(1)} collective-permute-done((bf16[256,640]{1,0:T(8,128)(2,1)S(1)}, bf16[256,640]{1,0:T(8,128)(2,1)S(1)}, u32[]{:S(2)}, u32[]{:S(2)}) %collective-permute-start.4) | collective-permute-done | bytes 327712 | tf_op jit(solution)/shard_map/ppermute | solution.py:31
  55.7 0.0 collective-permute-done.5.rest_13_.rest_5_
  55.7 0.5 collective-permute-done.6.rest_14_.rest_6_
  56.2 1.3 %collective-permute-done.7.rest_15_.rest_7_ = bf16[256,640]{1,0:T(8,128)(2,1)S(1)} collective-permute-done((bf16[256,640]{1,0:T(8,128)(2,1)S(1)}, bf16[256,640]{1,0:T(8,128)(2,1)S(1)}, u32[]{:S(2)}, u32[]{:S(2)}) %collective-permute-start.7) | collective-permute-done | bytes 327712 | tf_op jit(solution)/shard_map/ppermute | solution.py:31
  57.5 0.0 copy-done.9
  57.5 0.0 copy-start.1
  57.5 0.0 copy-start.3
  57.5 0.0 copy-start.5
  57.5 1.7 %iterate.1 = (bf16[128,1152]{1,0:T(8,128)(2,1)S(1)}, bf16[128,1152]{1,0:T(8,128)(2,1)S(1)}, f32[128,128]{1,0:T(8,128)S(1)}, f32[128,128]{1,0:T(8,128)S(1)}, bf16[128,256]{1,0:T(8,128)(2,1)S(1)}) custom-call(s32[1,8]{1,0:T(1,128)S(1)} %copy-done.9, f32[128,128]{1,0:T(8,128)S(1)} %get-tuple-element.18.own_ref, f32[128,128]{1,0:T(8,128)S(1)} %get-tuple-element.17.coarse_ref, ...), custom_call_target="tpu_custom_call" | custom-call | tf_op jit(solution)/shard_map/iterate/pallas_call | solution.py:162
  59.2 7.4 %collective-permute-start.15 = (bf16[128,256]{1,0:T(8,128)(2,1)S(1)}, bf16[128,256]{1,0:T(8,128)(2,1)S(1)}, u32[]{:S(2)}, u32[]{:S(2)}) collective-permute-start(bf16[128,256]{1,0:T(8,128)(2,1)S(1)} %get-tuple-element.31), channel_id=1, source_target_pairs={{0,504},{1,505},{2,506},{3,507},{4,508},{5,509},{6,510},{7,511},{8... | collective-permute-start | bytes 196616 | tf_op jit(solution)/shard_map/ppermute | solution.py:31
  66.6 1.9 %collective-permute-start.14 = (bf16[128,256]{1,0:T(8,128)(2,1)S(1)}, bf16[128,256]{1,0:T(8,128)(2,1)S(1)}, u32[]{:S(2)}, u32[]{:S(2)}) collective-permute-start(bf16[128,256]{1,0:T(8,128)(2,1)S(1)} %get-tuple-element.31), channel_id=1, source_target_pairs={{0,8},{1,9},{2,10},{3,11},{4,12},{5,13},{6,14},{7,15},{8,0},{9,1},... | collective-permute-start | bytes 196616 | tf_op jit(solution)/shard_map/ppermute | solution.py:31
  68.5 2.6 %collective-permute-start.13 = (bf16[128,256]{1,0:T(8,128)(2,1)S(1)}, bf16[128,256]{1,0:T(8,128)(2,1)S(1)}, u32[]{:S(2)}, u32[]{:S(2)}) collective-permute-start(bf16[128,256]{1,0:T(8,128)(2,1)S(1)} %get-tuple-element.31), channel_id=1, source_target_pairs={{0,508},{1,509},{2,510},{3,511},{4,8},{5,9},{6,10},{7,11},{8,4},{9... | collective-permute-start | bytes 196616 | tf_op jit(solution)/shard_map/ppermute | solution.py:31
  71.1 5.4 %collective-permute-start.12 = (bf16[128,256]{1,0:T(8,128)(2,1)S(1)}, bf16[128,256]{1,0:T(8,128)(2,1)S(1)}, u32[]{:S(2)}, u32[]{:S(2)}) collective-permute-start(bf16[128,256]{1,0:T(8,128)(2,1)S(1)} %get-tuple-element.31), channel_id=1, source_target_pairs={{0,4},{1,5},{2,6},{3,7},{4,0},{5,1},{6,2},{7,3},{8,12},{9,13},{10,... | collective-permute-start | bytes 196616 | tf_op jit(solution)/shard_map/ppermute | solution.py:31
  76.5 3.4 %collective-permute-start.11 = (bf16[128,256]{1,0:T(8,128)(2,1)S(1)}, bf16[128,256]{1,0:T(8,128)(2,1)S(1)}, u32[]{:S(2)}, u32[]{:S(2)}) collective-permute-start(bf16[128,256]{1,0:T(8,128)(2,1)S(1)} %get-tuple-element.31), channel_id=1, source_target_pairs={{0,510},{1,511},{2,4},{3,5},{4,2},{5,3},{6,8},{7,9},{8,6},{9,7},{1... | collective-permute-start | bytes 196616 | tf_op jit(solution)/shard_map/ppermute | solution.py:31
  79.9 0.0 collective-permute-done.15.rest_15_
  79.9 1.9 %collective-permute-start.10 = (bf16[128,256]{1,0:T(8,128)(2,1)S(1)}, bf16[128,256]{1,0:T(8,128)(2,1)S(1)}, u32[]{:S(2)}, u32[]{:S(2)}) collective-permute-start(bf16[128,256]{1,0:T(8,128)(2,1)S(1)} %get-tuple-element.31), channel_id=1, source_target_pairs={{0,2},{1,3},{2,0},{3,1},{4,6},{5,7},{6,4},{7,5},{8,10},{9,11},{10,... | collective-permute-start | bytes 196616 | tf_op jit(solution)/shard_map/ppermute | solution.py:31
  81.8 0.0 collective-permute-done.14.rest_14_
  81.8 6.9 %collective-permute-start.9 = (bf16[128,256]{1,0:T(8,128)(2,1)S(1)}, bf16[128,256]{1,0:T(8,128)(2,1)S(1)}, u32[]{:S(2)}, u32[]{:S(2)}) collective-permute-start(bf16[128,256]{1,0:T(8,128)(2,1)S(1)} %get-tuple-element.31), channel_id=1, source_target_pairs={{0,511},{1,2},{2,1},{3,4},{4,3},{5,6},{6,5},{7,8},{8,7},{9,10},{10... | collective-permute-start | bytes 196616 | tf_op jit(solution)/shard_map/ppermute | solution.py:31
  88.7 0.0 collective-permute-done.13.rest_13_
  88.7 2.8 %collective-permute-start.8 = (bf16[128,256]{1,0:T(8,128)(2,1)S(1)}, bf16[128,256]{1,0:T(8,128)(2,1)S(1)}, u32[]{:S(2)}, u32[]{:S(2)}) collective-permute-start(bf16[128,256]{1,0:T(8,128)(2,1)S(1)} %get-tuple-element.31), channel_id=1, source_target_pairs={{0,1},{1,0},{2,3},{3,2},{4,5},{5,4},{6,7},{7,6},{8,9},{9,8},{10,11... | collective-permute-start | bytes 196616 | tf_op jit(solution)/shard_map/ppermute | solution.py:31
  91.5 0.0 collective-permute-done.12.rest_12_
  91.5 0.0 collective-permute-done.11.rest_11_
  91.5 0.0 collective-permute-done.10.rest_10_
  91.5 0.0 collective-permute-done.9.rest_9_
  91.5 0.8 collective-permute-done.8.rest_8_
  92.4 0.0 copy-done.1
  92.4 0.0 copy-done.3
  92.4 0.0 copy-done.5
  92.4 7.1 %finish.1 = (bf16[1024,128]{1,0:T(8,128)(2,1)}, f32[128,128]{1,0:T(8,128)}) custom-call(s32[48]{0:T(128)S(1)} %copy-done.8, s32[1,8]{1,0:T(1,128)S(1)} %copy-done.9, bf16[1024,128]{1,0:T(8,128)(2,1)S(1)} %copy-done.3, bf16[48,128,128]{2,1,0:T(8,128)(2,1)S(1)} %copy-done.1, f32[8,128]{1,0:T(8,128)S(1)} %bitcast.5, bf16[1024,128]{1,0:T(8,128)(2,1)S(1)} %copy-done.5, ...), custom_call_target="tpu_custom_call" | custom-call | tf_op jit(solution)/shard_map/finish/pallas_call | solution.py:173
Async XLA Ops:
  0.6 56.9 %copy-start.9 = (s32[1,8]{1,0:T(1,128)S(1)}, s32[1,8]{1,0:T(1,128)}, u32[]{:S(2)}) copy-start(s32[1,8]{1,0:T(1,128)} %adj_ref.3) | copy-start | bytes 100
  0.6 1.4 %copy-start = (bf16[48,128,128]{2,1,0:T(8,128)(2,1)S(1)}, bf16[48,128,128]{2,1,0:T(8,128)(2,1)}, u32[]{:S(2)}) copy-start(bf16[48,128,128]{2,1,0:T(8,128)(2,1)} %tiles_ref.3) | copy-start | bytes 4718596
  2.1 0.9 copy-start.2
  3.0 0.9 copy-start.4
  4.0 0.7 copy-start.6
  4.7 0.7 copy-start.7
  5.4 0.7 copy-start.8
  9.5 26.4 %collective-permute-start = (bf16[256,640]{1,0:T(8,128)(2,1)S(1)}, bf16[256,640]{1,0:T(8,128)(2,1)S(1)}, u32[]{:S(2)}, u32[]{:S(2)}) collective-permute-start(bf16[256,640]{1,0:T(8,128)(2,1)S(1)} %get-tuple-element.19.rest_0_), channel_id=1, source_target_pairs={{0,1},{1,0},{2,3},{3,2},{4,5},{5,4},{6,7},{7,6},{8,9},{9,8},{10,11... | collective-permute-start | bytes 983048 | tf_op jit(solution)/shard_map/ppermute | solution.py:31
  18.3 23.2 %collective-permute-start.1 = (bf16[256,640]{1,0:T(8,128)(2,1)S(1)}, bf16[256,640]{1,0:T(8,128)(2,1)S(1)}, u32[]{:S(2)}, u32[]{:S(2)}) collective-permute-start(bf16[256,640]{1,0:T(8,128)(2,1)S(1)} %get-tuple-element.20.rest_1_), channel_id=1, source_target_pairs={{0,511},{1,2},{2,1},{3,4},{4,3},{5,6},{6,5},{7,8},{8,7},{9,10},{10... | collective-permute-start | bytes 983048 | tf_op jit(solution)/shard_map/ppermute | solution.py:31
  20.2 23.6 %collective-permute-start.2 = (bf16[256,640]{1,0:T(8,128)(2,1)S(1)}, bf16[256,640]{1,0:T(8,128)(2,1)S(1)}, u32[]{:S(2)}, u32[]{:S(2)}) collective-permute-start(bf16[256,640]{1,0:T(8,128)(2,1)S(1)} %get-tuple-element.21.rest_2_), channel_id=1, source_target_pairs={{0,2},{1,3},{2,0},{3,1},{4,6},{5,7},{6,4},{7,5},{8,10},{9,11},{10,... | collective-permute-start | bytes 983048 | tf_op jit(solution)/shard_map/ppermute | solution.py:31
  22.2 25.3 %collective-permute-start.3 = (bf16[256,640]{1,0:T(8,128)(2,1)S(1)}, bf16[256,640]{1,0:T(8,128)(2,1)S(1)}, u32[]{:S(2)}, u32[]{:S(2)}) collective-permute-start(bf16[256,640]{1,0:T(8,128)(2,1)S(1)} %get-tuple-element.22.rest_3_), channel_id=1, source_target_pairs={{0,510},{1,511},{2,4},{3,5},{4,2},{5,3},{6,8},{7,9},{8,6},{9,7},{1... | collective-permute-start | bytes 983048 | tf_op jit(solution)/shard_map/ppermute | solution.py:31
  33.9 21.7 %collective-permute-start.4 = (bf16[256,640]{1,0:T(8,128)(2,1)S(1)}, bf16[256,640]{1,0:T(8,128)(2,1)S(1)}, u32[]{:S(2)}, u32[]{:S(2)}) collective-permute-start(bf16[256,640]{1,0:T(8,128)(2,1)S(1)} %get-tuple-element.23.rest_4_), channel_id=1, source_target_pairs={{0,4},{1,5},{2,6},{3,7},{4,0},{5,1},{6,2},{7,3},{8,12},{9,13},{10,... | collective-permute-start | bytes 983048 | tf_op jit(solution)/shard_map/ppermute | solution.py:31
  35.9 19.8 %collective-permute-start.5 = (bf16[256,640]{1,0:T(8,128)(2,1)S(1)}, bf16[256,640]{1,0:T(8,128)(2,1)S(1)}, u32[]{:S(2)}, u32[]{:S(2)}) collective-permute-start(bf16[256,640]{1,0:T(8,128)(2,1)S(1)} %get-tuple-element.24.rest_5_), channel_id=1, source_target_pairs={{0,508},{1,509},{2,510},{3,511},{4,8},{5,9},{6,10},{7,11},{8,4},{9... | collective-permute-start | bytes 983048 | tf_op jit(solution)/shard_map/ppermute | solution.py:31
  41.6 14.6 %collective-permute-start.6 = (bf16[256,640]{1,0:T(8,128)(2,1)S(1)}, bf16[256,640]{1,0:T(8,128)(2,1)S(1)}, u32[]{:S(2)}, u32[]{:S(2)}) collective-permute-start(bf16[256,640]{1,0:T(8,128)(2,1)S(1)} %get-tuple-element.25.rest_6_), channel_id=1, source_target_pairs={{0,8},{1,9},{2,10},{3,11},{4,12},{5,13},{6,14},{7,15},{8,0},{9,1},... | collective-permute-start | bytes 983048 | tf_op jit(solution)/shard_map/ppermute | solution.py:31
  43.9 13.6 %collective-permute-start.7 = (bf16[256,640]{1,0:T(8,128)(2,1)S(1)}, bf16[256,640]{1,0:T(8,128)(2,1)S(1)}, u32[]{:S(2)}, u32[]{:S(2)}) collective-permute-start(bf16[256,640]{1,0:T(8,128)(2,1)S(1)} %get-tuple-element.26.rest_7_), channel_id=1, source_target_pairs={{0,504},{1,505},{2,506},{3,507},{4,508},{5,509},{6,510},{7,511},{8... | collective-permute-start | bytes 983048 | tf_op jit(solution)/shard_map/ppermute | solution.py:31
  57.5 34.9 %copy-start.1 = (bf16[48,128,128]{2,1,0:T(8,128)(2,1)S(1)}, bf16[48,128,128]{2,1,0:T(8,128)(2,1)}, u32[]{:S(2)}) copy-start(bf16[48,128,128]{2,1,0:T(8,128)(2,1)} %tiles_ref.3) | copy-start | bytes 4718596
  57.5 34.9 %copy-start.3 = (bf16[1024,128]{1,0:T(8,128)(2,1)S(1)}, bf16[1024,128]{1,0:T(8,128)(2,1)}, u32[]{:S(2)}) copy-start(bf16[1024,128]{1,0:T(8,128)(2,1)} %z_ref.3) | copy-start | bytes 786436
  57.5 34.9 %copy-start.5 = (bf16[1024,128]{1,0:T(8,128)(2,1)S(1)}, bf16[1024,128]{1,0:T(8,128)(2,1)}, u32[]{:S(2)}) copy-start(bf16[1024,128]{1,0:T(8,128)(2,1)} %rhs_ref.3) | copy-start | bytes 786436
  59.2 20.7 %collective-permute-start.15 = (bf16[128,256]{1,0:T(8,128)(2,1)S(1)}, bf16[128,256]{1,0:T(8,128)(2,1)S(1)}, u32[]{:S(2)}, u32[]{:S(2)}) collective-permute-start(bf16[128,256]{1,0:T(8,128)(2,1)S(1)} %get-tuple-element.31), channel_id=1, source_target_pairs={{0,504},{1,505},{2,506},{3,507},{4,508},{5,509},{6,510},{7,511},{8... | collective-permute-start | bytes 196616 | tf_op jit(solution)/shard_map/ppermute | solution.py:31
  66.6 15.2 %collective-permute-start.14 = (bf16[128,256]{1,0:T(8,128)(2,1)S(1)}, bf16[128,256]{1,0:T(8,128)(2,1)S(1)}, u32[]{:S(2)}, u32[]{:S(2)}) collective-permute-start(bf16[128,256]{1,0:T(8,128)(2,1)S(1)} %get-tuple-element.31), channel_id=1, source_target_pairs={{0,8},{1,9},{2,10},{3,11},{4,12},{5,13},{6,14},{7,15},{8,0},{9,1},... | collective-permute-start | bytes 196616 | tf_op jit(solution)/shard_map/ppermute | solution.py:31
  68.5 20.2 %collective-permute-start.13 = (bf16[128,256]{1,0:T(8,128)(2,1)S(1)}, bf16[128,256]{1,0:T(8,128)(2,1)S(1)}, u32[]{:S(2)}, u32[]{:S(2)}) collective-permute-start(bf16[128,256]{1,0:T(8,128)(2,1)S(1)} %get-tuple-element.31), channel_id=1, source_target_pairs={{0,508},{1,509},{2,510},{3,511},{4,8},{5,9},{6,10},{7,11},{8,4},{9... | collective-permute-start | bytes 196616 | tf_op jit(solution)/shard_map/ppermute | solution.py:31
  71.1 20.4 %collective-permute-start.12 = (bf16[128,256]{1,0:T(8,128)(2,1)S(1)}, bf16[128,256]{1,0:T(8,128)(2,1)S(1)}, u32[]{:S(2)}, u32[]{:S(2)}) collective-permute-start(bf16[128,256]{1,0:T(8,128)(2,1)S(1)} %get-tuple-element.31), channel_id=1, source_target_pairs={{0,4},{1,5},{2,6},{3,7},{4,0},{5,1},{6,2},{7,3},{8,12},{9,13},{10,... | collective-permute-start | bytes 196616 | tf_op jit(solution)/shard_map/ppermute | solution.py:31
  76.5 15.0 %collective-permute-start.11 = (bf16[128,256]{1,0:T(8,128)(2,1)S(1)}, bf16[128,256]{1,0:T(8,128)(2,1)S(1)}, u32[]{:S(2)}, u32[]{:S(2)}) collective-permute-start(bf16[128,256]{1,0:T(8,128)(2,1)S(1)} %get-tuple-element.31), channel_id=1, source_target_pairs={{0,510},{1,511},{2,4},{3,5},{4,2},{5,3},{6,8},{7,9},{8,6},{9,7},{1... | collective-permute-start | bytes 196616 | tf_op jit(solution)/shard_map/ppermute | solution.py:31
  79.9 11.7 %collective-permute-start.10 = (bf16[128,256]{1,0:T(8,128)(2,1)S(1)}, bf16[128,256]{1,0:T(8,128)(2,1)S(1)}, u32[]{:S(2)}, u32[]{:S(2)}) collective-permute-start(bf16[128,256]{1,0:T(8,128)(2,1)S(1)} %get-tuple-element.31), channel_id=1, source_target_pairs={{0,2},{1,3},{2,0},{3,1},{4,6},{5,7},{6,4},{7,5},{8,10},{9,11},{10,... | collective-permute-start | bytes 196616 | tf_op jit(solution)/shard_map/ppermute | solution.py:31
  81.8 9.7 %collective-permute-start.9 = (bf16[128,256]{1,0:T(8,128)(2,1)S(1)}, bf16[128,256]{1,0:T(8,128)(2,1)S(1)}, u32[]{:S(2)}, u32[]{:S(2)}) collective-permute-start(bf16[128,256]{1,0:T(8,128)(2,1)S(1)} %get-tuple-element.31), channel_id=1, source_target_pairs={{0,511},{1,2},{2,1},{3,4},{4,3},{5,6},{6,5},{7,8},{8,7},{9,10},{10... | collective-permute-start | bytes 196616 | tf_op jit(solution)/shard_map/ppermute | solution.py:31
  88.7 3.7 %collective-permute-start.8 = (bf16[128,256]{1,0:T(8,128)(2,1)S(1)}, bf16[128,256]{1,0:T(8,128)(2,1)S(1)}, u32[]{:S(2)}, u32[]{:S(2)}) collective-permute-start(bf16[128,256]{1,0:T(8,128)(2,1)S(1)} %get-tuple-element.31), channel_id=1, source_target_pairs={{0,1},{1,0},{2,3},{3,2},{4,5},{5,4},{6,7},{7,6},{8,9},{9,8},{10,11... | collective-permute-start | bytes 196616 | tf_op jit(solution)/shard_map/ppermute | solution.py:31

commit v2 on v1

v2 whole, which is shorter than its diff:
```python
import functools

import jax
import jax.numpy as jnp
from jax import lax
from jax.experimental import pallas as pl
from jax.experimental.pallas import tpu as pltpu
from jax.sharding import PartitionSpec as P

BLK = 128
TPR = 6
NB = 8
OV = 512
NLOC = 1024
K = 128
TAIL = K * K // OV
CHEB_CENTER = 2.5
CHEB_HALF = 1.5
RHO_FIRST = CHEB_HALF / CHEB_CENTER
RHO_SECOND = 1.0 / (2.0 * CHEB_CENTER / CHEB_HALF - RHO_FIRST)
F32 = jnp.float32
BF16 = jnp.bfloat16
VMEM = pl.BlockSpec(memory_space=pltpu.VMEM)
SMEM = pl.BlockSpec(memory_space=pltpu.SMEM)
HBM = pl.BlockSpec(memory_space=pltpu.HBM)
NT = (((1,), (1,)), ((), ()))
STEPS = ((2, 0), (2, 1), (1, 0), (1, 1), (0, 1), (3, 0), (3, 1), (0, 0))
INSIDE = STEPS.index((0, 0))
ACROSS = STEPS.index((0, 1))


def permute(block, target):
    n = lax.axis_size("sub")
    return lax.ppermute(block, "sub", [(i, target(i) % n) for i in range(n)])


def swapped(block, power, colour):
    o = 1 << power
    return permute(block, lambda i: i + o if (i // o) % 2 == colour else i - o)


def core_swap(block):
    return permute(block, lambda i: i ^ 1)


def both_ways(block, chips):
    return permute(block, lambda i: i + 2 * chips if i % 2 == 0 else i - 2 * chips)


def bit(me, power):
    return lax.rem(lax.div(me, 1 << power), 2)


def slot_of(step, me):
    power, colour = STEPS[step]
    return power + 4 * (bit(me, power) if colour == 0 else 1 - bit(me, power))


def near_step_is_first(power, me):
    return bit(me, power) != bit(me, 0)


def split(x):
    hi = x.astype(BF16)
    return hi, (x - hi.astype(F32)).astype(BF16)


def column(diag_ref, b):
    return jnp.broadcast_to(diag_ref[b : b + 1, :], (BLK, BLK)).T


def tile_row(cols_ref, tiles_ref, v_ref, b):
    acc = None
    for t in range(TPR * b, TPR * (b + 1)):
        rows = pl.ds(pl.multiple_of(cols_ref[t] * BLK, BLK), BLK)
        term = jnp.dot(tiles_ref[t], v_ref[rows, :], preferred_element_type=F32)
        acc = term if acc is None else acc + term
    return acc


def picks(margin_ref, slot):
    rows = margin_ref[pl.ds(slot, 1), :]
    ids = lax.broadcasted_iota(jnp.int32, (NLOC, OV), 0)
    return jnp.where(ids == rows, 1.0, 0.0).astype(BF16)


def prepare(cols_in, z_in, tiles_in, diag_in, rhs_in, margin_in, *rest):
    payloads, (own_ref, coarse_ref) = rest[:8], rest[8:10]
    cols_ref, z_ref, tiles_ref, diag_ref, rhs_ref, margin_ref, zit, im_rhs, sems = rest[10:]
    me = lax.axis_index("sub")
    pairs = [(cols_in, cols_ref), (z_in, z_ref), (diag_in, diag_ref)]
    pairs += [(tiles_in.at[pl.ds(TPR * b, TPR)], tiles_ref.at[pl.ds(TPR * b, TPR)]) for b in range(NB)]
    pairs += [(rhs_in, rhs_ref), (margin_in, margin_ref)]
    copies = [pltpu.make_async_copy(src, dst, sems.at[i]) for i, (src, dst) in enumerate(pairs)]
    for copy in copies:
        copy.start()
    for copy in copies[:3]:
        copy.wait()
    for b in range(NB):
        copies[3 + b].wait()
        rows = slice(b * BLK, (b + 1) * BLK)
        z = z_ref[rows, :]
        image = (column(diag_ref, b) * z.astype(F32) + tile_row(cols_ref, tiles_ref, z_ref, b)).astype(BF16)
        zit[:K, rows] = z.T
        zit[K:, rows] = image.T
        im_rhs[rows, :K] = image
    copies[-2].wait()
    copies[-1].wait()
    im_rhs[:, K:] = rhs_ref[...]
    both = jnp.dot(zit[:K, :], im_rhs[...], preferred_element_type=F32)
    own_ref[...] = both[:, :K]
    coarse = both[:, K:]
    coarse_ref[...] = coarse
    first = (coarse / CHEB_CENTER).astype(BF16)
    for step, out in enumerate(payloads):
        onehot = picks(margin_ref, slot_of(step, me))
        out[: 2 * K, :] = jnp.dot(zit[...], onehot, preferred_element_type=F32).astype(BF16)
        for q in range(OV // K):
            out[2 * K :, q * K : (q + 1) * K] = first[q * TAIL : (q + 1) * TAIL, :]


dot = functools.partial(jnp.dot, preferred_element_type=F32)


def iterate(adj_ref, own_ref, coarse_ref, *rest):
    mine, theirs = rest[:8], rest[8:16]
    ehi_ref, elo_ref, send_ref, v_ref = rest[16:]
    me = lax.axis_index("sub")
    coarse = coarse_ref[...]
    first = coarse / CHEB_CENTER
    ehi_ref[:, :K], elo_ref[:, :K] = split(own_ref[...])
    v_ref[:K, :], first_lo = split(first)
    for step in range(8):
        block = lax.dot_general(mine[step][: 2 * K, :], theirs[step][: 2 * K, :], NT, preferred_element_type=F32)
        weight = adj_ref[0, slot_of(step, me)].astype(F32) * 0.5
        at = (step + 1) * K
        ehi_ref[:, at : at + K], elo_ref[:, at : at + K] = split((block[:K, K:] + block[K:, :K]) * weight)
        for q in range(OV // K):
            v_ref[at + q * TAIL : at + (q + 1) * TAIL, :] = theirs[step][2 * K :, q * K : (q + 1) * K]
    image = dot(ehi_ref[...], v_ref[...]) + dot(elo_ref[...], v_ref[...]) + dot(ehi_ref[:, :K], first_lo)
    second = RHO_SECOND * RHO_FIRST * first + (2.0 * RHO_SECOND / CHEB_HALF) * (coarse - image)
    send_ref[:, :K], send_ref[:, K:] = split(first + second)


def arrive(adj_ref, margin_ref, slot, basis, coeffs):
    corr = lax.dot_general(coeffs, basis, (((0,), (0,)), ((), ())), preferred_element_type=F32).astype(BF16)
    corr = corr * adj_ref[0, slot].astype(BF16)
    return lax.dot_general(picks(margin_ref, slot), corr, NT, preferred_element_type=F32)


def merge_chip(adj_ref, z_ref, margin_ref, send_ref, other_ref, basis_ref, out_ref):
    me = lax.axis_index("sub")
    local = dot(z_ref[...], send_ref[:, :K]).astype(BF16).astype(F32)
    out_ref[...] = local + arrive(adj_ref, margin_ref, slot_of(INSIDE, me), basis_ref[:K, :], other_ref[:, :K])


def pick_basis(refs, power, near, me):
    a, b = STEPS.index((power, 0)), STEPS.index((power, 1))
    take_a = near_step_is_first(power, me) == near
    slot = jnp.where(take_a, slot_of(a, me), slot_of(b, me))
    return jnp.where(take_a, refs[a][:K, :], refs[b][:K, :]), slot, jnp.where(take_a, a, b)


def merge_near(adj_ref, margin_ref, summed_ref, one_ref, two_ref, four_ref, *rest):
    theirs, out_ref = rest[:8], rest[8]
    me = lax.axis_index("sub")
    acc = summed_ref[...]
    acc += arrive(adj_ref, margin_ref, slot_of(ACROSS, me), theirs[ACROSS][:K, :], one_ref[K:, :K])
    for power, ref in ((1, one_ref), (2, two_ref), (3, four_ref)):
        basis, slot, _ = pick_basis(theirs, power, True, me)
        acc += arrive(adj_ref, margin_ref, slot, basis, ref[:K, :K])
    out_ref[...] = acc


def finish(cols_ref, adj_ref, tiles_ref, diag_ref, rhs_ref, margin_ref, coarse_ref, ehi_ref, elo_ref, summed_ref, send_ref, other_ref, one_ref, two_ref, four_ref, far_ref, *rest):
    theirs = rest[:8]
    fine_ref, coarse_out, v_ref, merged = rest[8:]
    me = lax.axis_index("sub")
    acc = summed_ref[...]
    v_ref[:K, :] = send_ref[...]
    v_ref[(INSIDE + 1) * K : (INSIDE + 2) * K, :] = other_ref[...]
    v_ref[(ACROSS + 1) * K : (ACROSS + 2) * K, :] = one_ref[K:, :]
    for power, ref in ((1, one_ref), (2, two_ref), (3, four_ref)):
        far = far_ref[(power - 1) * K : power * K, :]
        basis, slot, step = pick_basis(theirs, power, False, me)
        acc += arrive(adj_ref, margin_ref, slot, basis, far[:, :K])
        near_step = STEPS.index((power, 0)) + STEPS.index((power, 1)) - step
        v_ref[pl.ds(pl.multiple_of((step + 1) * K, K), K), :] = far
        v_ref[pl.ds(pl.multiple_of((near_step + 1) * K, K), K), :] = ref[:K, :]
    merged[...] = acc.astype(BF16)
    both = dot(ehi_ref[...], v_ref[...])
    coarse_out[...] = coarse_ref[...] - (both[:, :K] + (both[:, K:] + dot(elo_ref[...], v_ref[:, :K])))
    for b in range(NB):
        rows = slice(b * BLK, (b + 1) * BLK)
        image = column(diag_ref, b) * merged[rows, :].astype(F32) + tile_row(cols_ref, tiles_ref, merged, b)
        fine_ref[rows, :] = (rhs_ref[rows, :].astype(F32) - image).astype(BF16)


def arr(shape, dtype):
    return jax.ShapeDtypeStruct(shape, dtype)


def call(kernel, name, in_specs, outs, scratch, flops, limit=32):
    return pl.pallas_call(
        kernel,
        name=name,
        in_specs=in_specs,
        out_specs=[VMEM] * len(outs),
        out_shape=outs,
        scratch_shapes=scratch,
        compiler_params=pltpu.CompilerParams(vmem_limit_bytes=limit * 1024 * 1024),
        cost_estimate=pl.CostEstimate(flops=flops, bytes_accessed=2**20, transcendentals=0),
    )


def per_device(deflation, op_tiles, tile_cols, diag_coef, fine_rhs, adjacency, margin_rows):
    diag = diag_coef.reshape(NB, BLK)
    margin = margin_rows[0]
    *payloads, own, coarse = call(
        prepare,
        "prepare",
        [HBM] * 6,
        [arr((2 * K + TAIL, OV), BF16)] * 8 + [arr((K, K), F32)] * 2,
        [
            pltpu.SMEM((TPR * NB,), jnp.int32),
            pltpu.VMEM((NLOC, K), BF16),
            pltpu.VMEM((TPR * NB, BLK, BLK), BF16),
            pltpu.VMEM((NB, BLK), F32),
            pltpu.VMEM((NLOC, K), BF16),
            pltpu.VMEM((8, OV), jnp.int32),
            pltpu.VMEM((2 * K, NLOC), BF16),
            pltpu.VMEM((NLOC, 2 * K), BF16),
            pltpu.SemaphoreType.DMA((NB + 5,)),
        ],
        3 * 10**9,
    )(*(pltpu.with_memory_space_constraint(x, pltpu.HBM) for x in (tile_cols, deflation, op_tiles, diag, fine_rhs, margin)))
    theirs = [swapped(block, *step) for block, step in zip(payloads, STEPS)]
    ehi, elo, send = call(
        iterate,
        "iterate",
        [SMEM] + [VMEM] * 18,
        [arr((K, 9 * K), BF16)] * 2 + [arr((K, 2 * K), BF16)],
        [pltpu.VMEM((9 * K, K), BF16)],
        10**9,
    )(adjacency, own, coarse, *payloads, *theirs)
    other = core_swap(send)
    pair = jnp.concatenate([send, other])
    one, two, four = (both_ways(pair, chips) for chips in (1, 2, 4))
    summed = call(
        merge_chip, "merge_chip", [SMEM] + [VMEM] * 5, [arr((NLOC, K), F32)], [], 10**9
    )(adjacency, deflation, margin, send, other, theirs[INSIDE])[0]
    hand_over, summed = lax.optimization_barrier((jnp.concatenate([one[K:], two[K:], four[K:]]), summed))
    far = core_swap(hand_over)
    summed = call(
        merge_near, "merge_near", [SMEM] + [VMEM] * 13, [arr((NLOC, K), F32)], [], 2 * 10**9
    )(adjacency, margin, summed, one, two, four, *theirs)[0]
    return tuple(
        call(
            finish,
            "finish",
            [SMEM] * 2 + [VMEM] * 22,
            [arr((NLOC, K), BF16), arr((K, K), F32)],
            [pltpu.VMEM((9 * K, 2 * K), BF16), pltpu.VMEM((NLOC, K), BF16)],
            3 * 10**9,
        )(tile_cols, adjacency, op_tiles, diag, fine_rhs, margin, coarse, ehi, elo, summed, send, other, one, two, four, far, *theirs)
    )


def solution(mesh):
    return jax.shard_map(
        per_device,
        mesh=mesh,
        in_specs=(P("sub", None), P("sub", None, None), P("sub"), P("sub"), P("sub", None), P("sub", None), P("sub", None, None)),
        out_specs=(P("sub", None), P("sub", None)),
        check_vma=False,
    )
```

time: 100 us -> 85.8 us (0.86)
  starting transfers between devices: 70.1 us -> 63.2 us
  waiting for transfers between devices: 10.8 us -> 4.85 us
  local copies, waits for them, and re-layouts: 5.38 us -> 0.07 us
  Pallas kernels: 12.2 us -> 16.2 us
    ppermute x16 -> x13, starting transfers between devices: 70.1 us -> 63.2 us  [permute(): return lax.ppermute(block, 'sub', [(i, target(i) % n) for i in range(n)])]
    ppermute x16 -> x13, waiting for transfers between devices: 10.8 us -> 4.85 us  [permute(): return lax.ppermute(block, 'sub', [(i, target(i) % n) for i in range(n)])]
    unnamed x20 -> x15, local copies, waits for them, and re-layouts: 5.38 us -> 0.04 us
    pallas_call x3 -> x5, Pallas kernels: 12.2 us -> 16.2 us  [the longest x1 6.06 us: per_device(): call(prepare, 'prepare', [HBM] * 6, [arr((2 * K + TAIL, OV), BF16)] * 8 +...]
  transfers between devices with their start and end apart: 16 -> 13, of which waited for: 4 -> 5; matrix products, arithmetic and copies ran while one was open for 0% -> 0% of each run, Pallas kernels for 0% -> 5%
where the time goes in v2:
time: 85.8 us; the launch traced here: 85.3 us
  starting transfers between devices  63.2 us (74%)
  Pallas kernels  16.2 us (19%)
  waiting for transfers between devices  4.85 us (6%)
  between operations  0.93 us (1%)
    ppermute x13, starting transfers between devices, permute(): return lax.ppermute(block, 'sub', [(i, target(i) % n) for i in range(n)])  63.2 us
    pallas_call x1, Pallas kernels, per_device(): call(prepare, 'prepare', [HBM] * 6, [arr((2 * K + TAIL, OV), BF16)] * 8 +...  6.06 us
    ppermute x13, waiting for transfers between devices, permute(): return lax.ppermute(block, 'sub', [(i, target(i) % n) for i in range(n)])  4.85 us
    pallas_call x1, Pallas kernels, per_device(): call(finish, 'finish', [SMEM] * 2 + [VMEM] * 22, [arr((NLOC, K), BF16), a...  4.07 us
    pallas_call x1, Pallas kernels, per_device(): call(merge_near, 'merge_near', [SMEM] + [VMEM] * 13, [arr((NLOC, K), F32)...  3.26 us
  transfers between devices with their start and end apart: 13, of which 5 were waited for; matrix products, arithmetic and copies ran while one was open for 0% of the time, Pallas kernels for 5%

profile of v2, /device:TPU:1, one launch (start us, length us, event | category | flops | bytes accessed | tf_op | source)
XLA Modules:
  0.0 85.3 jit_solution(15018854568954710238)
XLA Ops:
  0.6 0.0 copy-start
  0.6 6.1 %prepare.1 = (bf16[288,512]{1,0:T(8,128)(2,1)S(1)}, bf16[288,512]{1,0:T(8,128)(2,1)S(1)}, bf16[288,512]{1,0:T(8,128)(2,1)S(1)}, bf16[288,512]{1,0:T(8,128)(2,1)S...) custom-call(s32[48]{0:T(128)} %cols_ref.1, ...), custom_call_target="tpu_custom_call" | custom-call | flops 3000000000 | bytes 1048576 | tf_op jit(solution)/shard_map/prepare/pallas_call | solution.py:219
  6.7 5.5 %collective-permute-start = (bf16[288,512]{1,0:T(8,128)(2,1)S(1)}, bf16[288,512]{1,0:T(8,128)(2,1)S(1)}, u32[]{:S(2)}, u32[]{:S(2)}) collective-permute-start(bf16[288,512]{1,0:T(8,128)(2,1)S(1)} %get-tuple-element.19.rest_0_), channel_id=1, source_target_pairs={{0,4},{1,5},{2,6},{3,7},{4,0},{5,1},{6,2},{7,3},{8,12},{9,13},{10,... | collective-permute-start | bytes 884744 | tf_op jit(solution)/shard_map/ppermute | solution.py:34
  12.2 13.5 %collective-permute-start.1 = (bf16[288,512]{1,0:T(8,128)(2,1)S(1)}, bf16[288,512]{1,0:T(8,128)(2,1)S(1)}, u32[]{:S(2)}, u32[]{:S(2)}) collective-permute-start(bf16[288,512]{1,0:T(8,128)(2,1)S(1)} %get-tuple-element.20.rest_1_), channel_id=1, source_target_pairs={{0,508},{1,509},{2,510},{3,511},{4,8},{5,9},{6,10},{7,11},{8,4},{9... | collective-permute-start | bytes 884744 | tf_op jit(solution)/shard_map/ppermute | solution.py:34
  25.7 3.1 %collective-permute-start.2 = (bf16[288,512]{1,0:T(8,128)(2,1)S(1)}, bf16[288,512]{1,0:T(8,128)(2,1)S(1)}, u32[]{:S(2)}, u32[]{:S(2)}) collective-permute-start(bf16[288,512]{1,0:T(8,128)(2,1)S(1)} %get-tuple-element.21.rest_2_), channel_id=1, source_target_pairs={{0,2},{1,3},{2,0},{3,1},{4,6},{5,7},{6,4},{7,5},{8,10},{9,11},{10,... | collective-permute-start | bytes 884744 | tf_op jit(solution)/shard_map/ppermute | solution.py:34
  28.8 1.9 %collective-permute-start.3 = (bf16[288,512]{1,0:T(8,128)(2,1)S(1)}, bf16[288,512]{1,0:T(8,128)(2,1)S(1)}, u32[]{:S(2)}, u32[]{:S(2)}) collective-permute-start(bf16[288,512]{1,0:T(8,128)(2,1)S(1)} %get-tuple-element.22.rest_3_), channel_id=1, source_target_pairs={{0,510},{1,511},{2,4},{3,5},{4,2},{5,3},{6,8},{7,9},{8,6},{9,7},{1... | collective-permute-start | bytes 884744 | tf_op jit(solution)/shard_map/ppermute | solution.py:34
  30.8 3.6 %collective-permute-start.4 = (bf16[288,512]{1,0:T(8,128)(2,1)S(1)}, bf16[288,512]{1,0:T(8,128)(2,1)S(1)}, u32[]{:S(2)}, u32[]{:S(2)}) collective-permute-start(bf16[288,512]{1,0:T(8,128)(2,1)S(1)} %get-tuple-element.23.rest_4_), channel_id=1, source_target_pairs={{0,511},{1,2},{2,1},{3,4},{4,3},{5,6},{6,5},{7,8},{8,7},{9,10},{10... | collective-permute-start | bytes 884744 | tf_op jit(solution)/shard_map/ppermute | solution.py:34
  34.4 0.0 collective-permute-done.rest_8_.rest_0_
  34.4 1.9 %collective-permute-start.5 = (bf16[288,512]{1,0:T(8,128)(2,1)S(1)}, bf16[288,512]{1,0:T(8,128)(2,1)S(1)}, u32[]{:S(2)}, u32[]{:S(2)}) collective-permute-start(bf16[288,512]{1,0:T(8,128)(2,1)S(1)} %get-tuple-element.24.rest_5_), channel_id=1, source_target_pairs={{0,8},{1,9},{2,10},{3,11},{4,12},{5,13},{6,14},{7,15},{8,0},{9,1},... | collective-permute-start | bytes 884744 | tf_op jit(solution)/shard_map/ppermute | solution.py:34
  36.3 0.0 collective-permute-done.1.rest_9_.rest_1_
  36.3 5.5 %collective-permute-start.6 = (bf16[288,512]{1,0:T(8,128)(2,1)S(1)}, bf16[288,512]{1,0:T(8,128)(2,1)S(1)}, u32[]{:S(2)}, u32[]{:S(2)}) collective-permute-start(bf16[288,512]{1,0:T(8,128)(2,1)S(1)} %get-tuple-element.25.rest_6_), channel_id=1, source_target_pairs={{0,504},{1,505},{2,506},{3,507},{4,508},{5,509},{6,510},{7,511},{8... | collective-permute-start | bytes 884744 | tf_op jit(solution)/shard_map/ppermute | solution.py:34
  41.8 0.0 collective-permute-done.2.rest_10_.rest_2_
  41.8 5.2 %collective-permute-start.7 = (bf16[288,512]{1,0:T(8,128)(2,1)S(1)}, bf16[288,512]{1,0:T(8,128)(2,1)S(1)}, u32[]{:S(2)}, u32[]{:S(2)}) collective-permute-start(bf16[288,512]{1,0:T(8,128)(2,1)S(1)} %get-tuple-element.26.rest_7_), channel_id=1, source_target_pairs={{0,1},{1,0},{2,3},{3,2},{4,5},{5,4},{6,7},{7,6},{8,9},{9,8},{10,11... | collective-permute-start | bytes 884744 | tf_op jit(solution)/shard_map/ppermute | solution.py:34
  47.0 0.0 collective-permute-done.3.rest_11_.rest_3_
  47.0 0.0 collective-permute-done.4.rest_12_.rest_4_
  47.0 0.0 collective-permute-done.5.rest_13_.rest_5_
  47.0 1.0 %collective-permute-done.6.rest_14_.rest_6_ = bf16[288,512]{1,0:T(8,128)(2,1)S(1)} collective-permute-done((bf16[288,512]{1,0:T(8,128)(2,1)S(1)}, bf16[288,512]{1,0:T(8,128)(2,1)S(1)}, u32[]{:S(2)}, u32[]{:S(2)}) %collective-permute-start.6) | collective-permute-done | bytes 294944 | tf_op jit(solution)/shard_map/ppermute | solution.py:34
  48.1 0.1 collective-permute-done.7.rest_15_.basis_ref.rest_7_
  48.2 0.0 copy-done
  48.2 0.0 copy-start.2
  48.2 0.0 copy-start.4
  48.2 1.6 %iterate.1 = (bf16[128,1152]{1,0:T(8,128)(2,1)S(1)}, bf16[128,1152]{1,0:T(8,128)(2,1)S(1)}, bf16[128,256]{1,0:T(8,128)(2,1)S(1)}) custom-call(s32[1,8]{1,0:T(1,128)S(1)} %copy-done, f32[128,128]{1,0:T(8,128)S(1)} %get-tuple-element.18.own_ref, f32[128,128]{1,0:T(8,128)S(1)} %get-tuple-element.17.coarse_ref, bf16[288,512]{1,0:T(8,128)(2,1)S(1)} %get-tuple-element.19.rest_0_, ...), custom_call_target="tpu_custom_call" | custom-call | flops 1000000000 | bytes 1048576 | tf_op jit(solution)/shard_map/iterate/pallas_call | solution.py:238
  49.8 7.6 %collective-permute-start.8 = (bf16[128,256]{1,0:T(8,128)(2,1)S(1)}, bf16[128,256]{1,0:T(8,128)(2,1)S(1)}, u32[]{:S(2)}, u32[]{:S(2)}) collective-permute-start(bf16[128,256]{1,0:T(8,128)(2,1)S(1)} %get-tuple-element.29.send_ref), channel_id=1, source_target_pairs={{0,1},{1,0},{2,3},{3,2},{4,5},{5,4},{6,7},{7,6},{8,9},{9,8},{10,11... | collective-permute-start | bytes 196616 | tf_op jit(solution)/shard_map/ppermute | solution.py:34
  57.5 0.9 %collective-permute-done.8.other_ref = bf16[128,256]{1,0:T(8,128)(2,1)S(1)} collective-permute-done((bf16[128,256]{1,0:T(8,128)(2,1)S(1)}, bf16[128,256]{1,0:T(8,128)(2,1)S(1)}, u32[]{:S(2)}, u32[]{:S(2)}) %collective-permute-start.8) | collective-permute-done | bytes 65568 | tf_op jit(solution)/shard_map/ppermute | solution.py:34
  58.3 4.1 %collective-permute-start.11 = (bf16[256,256]{1,0:T(8,128)(2,1)S(1)}, bf16[256,256]{1,0:T(8,128)(2,1)S(1)}, u32[]{:S(2)}, u32[]{:S(2)}) collective-permute-start(bf16[256,256]{1,0:T(8,128)(2,1)S(1)} %constant_dynamic-update-slice_fusion), channel_id=1, source_target_pairs={{0,8},{1,505},{2,10},{3,507},{4,12},{5,509},{6,14},{7,511},{8,16},... | collective-permute-start | bytes 393224 | tf_op jit(solution)/shard_map/ppermute | solution.py:34
  62.4 4.9 %collective-permute-start.10 = (bf16[256,256]{1,0:T(8,128)(2,1)S(1)}, bf16[256,256]{1,0:T(8,128)(2,1)S(1)}, u32[]{:S(2)}, u32[]{:S(2)}) collective-permute-start(bf16[256,256]{1,0:T(8,128)(2,1)S(1)} %constant_dynamic-update-slice_fusion), channel_id=1, source_target_pairs={{0,4},{1,509},{2,6},{3,511},{4,8},{5,1},{6,10},{7,3},{8,12},{9,5},... | collective-permute-start | bytes 393224 | tf_op jit(solution)/shard_map/ppermute | solution.py:34
  67.3 1.9 %collective-permute-start.9 = (bf16[256,256]{1,0:T(8,128)(2,1)S(1)}, bf16[256,256]{1,0:T(8,128)(2,1)S(1)}, u32[]{:S(2)}, u32[]{:S(2)}) collective-permute-start(bf16[256,256]{1,0:T(8,128)(2,1)S(1)} %constant_dynamic-update-slice_fusion), channel_id=1, source_target_pairs={{0,2},{1,511},{2,4},{3,1},{4,6},{5,3},{6,8},{7,5},{8,10},{9,7},{10... | collective-permute-start | bytes 393224 | tf_op jit(solution)/shard_map/ppermute | solution.py:34
  69.3 0.0 copy-done.2
  69.3 0.0 copy-done.4
  69.3 1.2 %merge_chip.1.summed_ref = f32[1024,128]{1,0:T(8,128)S(1)} custom-call(s32[1,8]{1,0:T(1,128)S(1)} %copy-done, bf16[1024,128]{1,0:T(8,128)(2,1)S(1)} %copy-done.2, s32[8,512]{1,0:T(8,128)S(1)} %bitcast.3, bf16[128,256]{1,0:T(8,128)(2,1)S(1)} %get-tuple-element.29.send_ref, bf16[128,256]{1,0:T(8,128)(2,1)S(1)} %collective-permute-done.8.other_ref, ...), custom_call_target="tpu_custom_call" | custom-call | flops 1000000000 | bytes 1048576 | tf_op jit(solution)/shard_map/merge_chip/pallas_call | solution.py:249
  70.5 0.0 collective-permute-done.11.four_ref
  70.5 2.3 %collective-permute-done.10.two_ref = bf16[256,256]{1,0:T(8,128)(2,1)S(1)} collective-permute-done((bf16[256,256]{1,0:T(8,128)(2,1)S(1)}, bf16[256,256]{1,0:T(8,128)(2,1)S(1)}, u32[]{:S(2)}, u32[]{:S(2)}) %collective-permute-start.10) | collective-permute-done | bytes 131104 | tf_op jit(solution)/shard_map/ppermute | solution.py:34
  72.8 0.5 collective-permute-done.9.one_ref
  73.4 0.0 copy-start.1
  73.4 0.0 copy-start.3
  73.4 0.0 copy-start.5
  73.4 0.0 copy-start.6
  73.4 4.5 %collective-permute-start.12 = (bf16[384,256]{1,0:T(8,128)(2,1)S(1)}, bf16[384,256]{1,0:T(8,128)(2,1)S(1)}, u32[]{:S(2)}, u32[]{:S(2)}) collective-permute-start(bf16[384,256]{1,0:T(8,128)(2,1)S(1)} %pad_maximum_fusion), channel_id=1, source_target_pairs={{0,1},{1,0},{2,3},{3,2},{4,5},{5,4},{6,7},{7,6},{8,9},{9,8},{10,11... | collective-permute-start | bytes 589832 | tf_op jit(solution)/shard_map/ppermute | solution.py:34
  77.9 3.3 %merge_near.1.summed_ref = f32[1024,128]{1,0:T(8,128)S(1)} custom-call(s32[1,8]{1,0:T(1,128)S(1)} %copy-done, s32[8,512]{1,0:T(8,128)S(1)} %bitcast.4, f32[1024,128]{1,0:T(8,128)S(1)} %merge_chip.1.summed_ref, bf16[256,256]{1,0:T(8,128)(2,1)S(1)} %collective-permute-done.9.one_ref, bf16[256,256]{1,0:T(8,128)(2,1)S(1)} %collective-permute-done.10.two_ref, ...), custom_call_target="tpu_custom_call" | custom-call | flops 2000000000 | bytes 1048576 | tf_op jit(solution)/shard_map/merge_near/pallas_call | solution.py:254
  81.1 0.0 collective-permute-done.12.far_ref
  81.2 0.0 copy-done.1
  81.2 0.0 copy-done.3
  81.2 0.0 copy-done.5
  81.2 0.0 copy-done.6
  81.2 4.1 %finish.1 = (bf16[1024,128]{1,0:T(8,128)(2,1)}, f32[128,128]{1,0:T(8,128)}) custom-call(s32[48]{0:T(128)S(1)} %copy-done.6, s32[1,8]{1,0:T(1,128)S(1)} %copy-done, bf16[48,128,128]{2,1,0:T(8,128)(2,1)S(1)} %copy-done.1, f32[8,128]{1,0:T(8,128)S(1)} %bitcast.7, bf16[1024,128]{1,0:T(8,128)(2,1)S(1)} %copy-done.3, s32[8,512]{1,0:T(8,128)S(1)} %bitcast.5, ...), custom_call_target="tpu_custom_call" | custom-call | flops 3000000000 | bytes 1048576 | tf_op jit(solution)/shard_map/finish/pallas_call | solution.py:258
  (6 shorter events, 0.0 us)
Async XLA Ops:
  0.6 47.6 %copy-start = (s32[1,8]{1,0:T(1,128)S(1)}, s32[1,8]{1,0:T(1,128)}, u32[]{:S(2)}) copy-start(s32[1,8]{1,0:T(1,128)} %adj_ref.7) | copy-start | bytes 100
  6.7 27.6 %collective-permute-start = (bf16[288,512]{1,0:T(8,128)(2,1)S(1)}, bf16[288,512]{1,0:T(8,128)(2,1)S(1)}, u32[]{:S(2)}, u32[]{:S(2)}) collective-permute-start(bf16[288,512]{1,0:T(8,128)(2,1)S(1)} %get-tuple-element.19.rest_0_), channel_id=1, source_target_pairs={{0,4},{1,5},{2,6},{3,7},{4,0},{5,1},{6,2},{7,3},{8,12},{9,13},{10,... | collective-permute-start | bytes 884744 | tf_op jit(solution)/shard_map/ppermute | solution.py:34
  12.2 24.1 %collective-permute-start.1 = (bf16[288,512]{1,0:T(8,128)(2,1)S(1)}, bf16[288,512]{1,0:T(8,128)(2,1)S(1)}, u32[]{:S(2)}, u32[]{:S(2)}) collective-permute-start(bf16[288,512]{1,0:T(8,128)(2,1)S(1)} %get-tuple-element.20.rest_1_), channel_id=1, source_target_pairs={{0,508},{1,509},{2,510},{3,511},{4,8},{5,9},{6,10},{7,11},{8,4},{9... | collective-permute-start | bytes 884744 | tf_op jit(solution)/shard_map/ppermute | solution.py:34
  25.7 16.1 %collective-permute-start.2 = (bf16[288,512]{1,0:T(8,128)(2,1)S(1)}, bf16[288,512]{1,0:T(8,128)(2,1)S(1)}, u32[]{:S(2)}, u32[]{:S(2)}) collective-permute-start(bf16[288,512]{1,0:T(8,128)(2,1)S(1)} %get-tuple-element.21.rest_2_), channel_id=1, source_target_pairs={{0,2},{1,3},{2,0},{3,1},{4,6},{5,7},{6,4},{7,5},{8,10},{9,11},{10,... | collective-permute-start | bytes 884744 | tf_op jit(solution)/shard_map/ppermute | solution.py:34
  28.8 18.2 %collective-permute-start.3 = (bf16[288,512]{1,0:T(8,128)(2,1)S(1)}, bf16[288,512]{1,0:T(8,128)(2,1)S(1)}, u32[]{:S(2)}, u32[]{:S(2)}) collective-permute-start(bf16[288,512]{1,0:T(8,128)(2,1)S(1)} %get-tuple-element.22.rest_3_), channel_id=1, source_target_pairs={{0,510},{1,511},{2,4},{3,5},{4,2},{5,3},{6,8},{7,9},{8,6},{9,7},{1... | collective-permute-start | bytes 884744 | tf_op jit(solution)/shard_map/ppermute | solution.py:34
  30.8 16.2 %collective-permute-start.4 = (bf16[288,512]{1,0:T(8,128)(2,1)S(1)}, bf16[288,512]{1,0:T(8,128)(2,1)S(1)}, u32[]{:S(2)}, u32[]{:S(2)}) collective-permute-start(bf16[288,512]{1,0:T(8,128)(2,1)S(1)} %get-tuple-element.23.rest_4_), channel_id=1, source_target_pairs={{0,511},{1,2},{2,1},{3,4},{4,3},{5,6},{6,5},{7,8},{8,7},{9,10},{10... | collective-permute-start | bytes 884744 | tf_op jit(solution)/shard_map/ppermute | solution.py:34
  34.4 12.7 %collective-permute-start.5 = (bf16[288,512]{1,0:T(8,128)(2,1)S(1)}, bf16[288,512]{1,0:T(8,128)(2,1)S(1)}, u32[]{:S(2)}, u32[]{:S(2)}) collective-permute-start(bf16[288,512]{1,0:T(8,128)(2,1)S(1)} %get-tuple-element.24.rest_5_), channel_id=1, source_target_pairs={{0,8},{1,9},{2,10},{3,11},{4,12},{5,13},{6,14},{7,15},{8,0},{9,1},... | collective-permute-start | bytes 884744 | tf_op jit(solution)/shard_map/ppermute | solution.py:34
  36.3 11.8 %collective-permute-start.6 = (bf16[288,512]{1,0:T(8,128)(2,1)S(1)}, bf16[288,512]{1,0:T(8,128)(2,1)S(1)}, u32[]{:S(2)}, u32[]{:S(2)}) collective-permute-start(bf16[288,512]{1,0:T(8,128)(2,1)S(1)} %get-tuple-element.25.rest_6_), channel_id=1, source_target_pairs={{0,504},{1,505},{2,506},{3,507},{4,508},{5,509},{6,510},{7,511},{8... | collective-permute-start | bytes 884744 | tf_op jit(solution)/shard_map/ppermute | solution.py:34
  41.8 6.4 %collective-permute-start.7 = (bf16[288,512]{1,0:T(8,128)(2,1)S(1)}, bf16[288,512]{1,0:T(8,128)(2,1)S(1)}, u32[]{:S(2)}, u32[]{:S(2)}) collective-permute-start(bf16[288,512]{1,0:T(8,128)(2,1)S(1)} %get-tuple-element.26.rest_7_), channel_id=1, source_target_pairs={{0,1},{1,0},{2,3},{3,2},{4,5},{5,4},{6,7},{7,6},{8,9},{9,8},{10,11... | collective-permute-start | bytes 884744 | tf_op jit(solution)/shard_map/ppermute | solution.py:34
  48.2 21.1 %copy-start.2 = (bf16[1024,128]{1,0:T(8,128)(2,1)S(1)}, bf16[1024,128]{1,0:T(8,128)(2,1)}, u32[]{:S(2)}) copy-start(bf16[1024,128]{1,0:T(8,128)(2,1)} %z_ref.1) | copy-start | bytes 786436
  48.2 21.1 %copy-start.4 = (s32[1,8,512]{2,1,0:T(8,128)S(1)}, s32[1,8,512]{2,1,0:T(8,128)}, u32[]{:S(2)}) copy-start(s32[1,8,512]{2,1,0:T(8,128)} %param.13) | copy-start | bytes 49156
  49.8 8.5 %collective-permute-start.8 = (bf16[128,256]{1,0:T(8,128)(2,1)S(1)}, bf16[128,256]{1,0:T(8,128)(2,1)S(1)}, u32[]{:S(2)}, u32[]{:S(2)}) collective-permute-start(bf16[128,256]{1,0:T(8,128)(2,1)S(1)} %get-tuple-element.29.send_ref), channel_id=1, source_target_pairs={{0,1},{1,0},{2,3},{3,2},{4,5},{5,4},{6,7},{7,6},{8,9},{9,8},{10,11... | collective-permute-start | bytes 196616 | tf_op jit(solution)/shard_map/ppermute | solution.py:34
  58.3 12.2 %collective-permute-start.11 = (bf16[256,256]{1,0:T(8,128)(2,1)S(1)}, bf16[256,256]{1,0:T(8,128)(2,1)S(1)}, u32[]{:S(2)}, u32[]{:S(2)}) collective-permute-start(bf16[256,256]{1,0:T(8,128)(2,1)S(1)} %constant_dynamic-update-slice_fusion), channel_id=1, source_target_pairs={{0,8},{1,505},{2,10},{3,507},{4,12},{5,509},{6,14},{7,511},{8,16},... | collective-permute-start | bytes 393224 | tf_op jit(solution)/shard_map/ppermute | solution.py:34
  62.4 10.4 %collective-permute-start.10 = (bf16[256,256]{1,0:T(8,128)(2,1)S(1)}, bf16[256,256]{1,0:T(8,128)(2,1)S(1)}, u32[]{:S(2)}, u32[]{:S(2)}) collective-permute-start(bf16[256,256]{1,0:T(8,128)(2,1)S(1)} %constant_dynamic-update-slice_fusion), channel_id=1, source_target_pairs={{0,4},{1,509},{2,6},{3,511},{4,8},{5,1},{6,10},{7,3},{8,12},{9,5},... | collective-permute-start | bytes 393224 | tf_op jit(solution)/shard_map/ppermute | solution.py:34
  67.3 6.0 %collective-permute-start.9 = (bf16[256,256]{1,0:T(8,128)(2,1)S(1)}, bf16[256,256]{1,0:T(8,128)(2,1)S(1)}, u32[]{:S(2)}, u32[]{:S(2)}) collective-permute-start(bf16[256,256]{1,0:T(8,128)(2,1)S(1)} %constant_dynamic-update-slice_fusion), channel_id=1, source_target_pairs={{0,2},{1,511},{2,4},{3,1},{4,6},{5,3},{6,8},{7,5},{8,10},{9,7},{10... | collective-permute-start | bytes 393224 | tf_op jit(solution)/shard_map/ppermute | solution.py:34
  73.4 7.8 %copy-start.1 = (bf16[48,128,128]{2,1,0:T(8,128)(2,1)S(1)}, bf16[48,128,128]{2,1,0:T(8,128)(2,1)}, u32[]{:S(2)}) copy-start(bf16[48,128,128]{2,1,0:T(8,128)(2,1)} %tiles_ref.1) | copy-start | bytes 4718596
  73.4 7.8 %copy-start.3 = (bf16[1024,128]{1,0:T(8,128)(2,1)S(1)}, bf16[1024,128]{1,0:T(8,128)(2,1)}, u32[]{:S(2)}) copy-start(bf16[1024,128]{1,0:T(8,128)(2,1)} %rhs_ref.1) | copy-start | bytes 786436
  73.4 7.8 %copy-start.5 = (f32[1024]{0:T(1024)S(1)}, f32[1024]{0:T(1024)}, u32[]{:S(2)}) copy-start(f32[1024]{0:T(1024)} %param.10) | copy-start | bytes 12292
  73.4 7.8 %copy-start.6 = (s32[48]{0:T(128)S(1)}, s32[48]{0:T(128)}, u32[]{:S(2)}) copy-start(s32[48]{0:T(128)} %cols_ref.1) | copy-start | bytes 580
  73.4 7.7 %collective-permute-start.12 = (bf16[384,256]{1,0:T(8,128)(2,1)S(1)}, bf16[384,256]{1,0:T(8,128)(2,1)S(1)}, u32[]{:S(2)}, u32[]{:S(2)}) collective-permute-start(bf16[384,256]{1,0:T(8,128)(2,1)S(1)} %pad_maximum_fusion), channel_id=1, source_target_pairs={{0,1},{1,0},{2,3},{3,2},{4,5},{5,4},{6,7},{7,6},{8,9},{9,8},{10,11... | collective-permute-start | bytes 589832 | tf_op jit(solution)/shard_map/ppermute | solution.py:34

commit v3 on v2

--- a/solution.py
+++ b/solution.py
@@ -24,7 +24,8 @@
 SMEM = pl.BlockSpec(memory_space=pltpu.SMEM)
 HBM = pl.BlockSpec(memory_space=pltpu.HBM)
 NT = (((1,), (1,)), ((), ()))
-STEPS = ((2, 0), (2, 1), (1, 0), (1, 1), (0, 1), (3, 0), (3, 1), (0, 0))
+STEPS = ((0, 0), (2, 0), (2, 1), (3, 0), (1, 0), (1, 1), (3, 1), (0, 1))
+EARLY = 6
 INSIDE = STEPS.index((0, 0))
 ACROSS = STEPS.index((0, 1))
 
@@ -122,22 +123,42 @@
 dot = functools.partial(jnp.dot, preferred_element_type=F32)
 
 
-def iterate(adj_ref, own_ref, coarse_ref, *rest):
-    mine, theirs = rest[:8], rest[8:16]
-    ehi_ref, elo_ref, send_ref, v_ref = rest[16:]
+def pair_block(mine, theirs, adj_ref, step, me):
+    block = lax.dot_general(mine[: 2 * K, :], theirs[: 2 * K, :], NT, preferred_element_type=F32)
+    weight = adj_ref[0, slot_of(step, me)].astype(F32) * 0.5
+    return split((block[:K, K:] + block[K:, :K]) * weight)
+
+
+def take_first(theirs, v_ref, at):
+    for q in range(OV // K):
+        v_ref[at + q * TAIL : at + (q + 1) * TAIL, :] = theirs[2 * K :, q * K : (q + 1) * K]
+
+
+def iterate_early(adj_ref, own_ref, coarse_ref, *rest):
+    mine, theirs = rest[:EARLY], rest[EARLY : 2 * EARLY]
+    ehi_ref, elo_ref, image_ref, v_ref = rest[2 * EARLY :]
+    me = lax.axis_index("sub")
+    ehi_ref[:, :K], elo_ref[:, :K] = split(own_ref[...])
+    v_ref[:K, :], first_lo = split(coarse_ref[...] / CHEB_CENTER)
+    for step in range(EARLY):
+        at = (step + 1) * K
+        ehi_ref[:, at : at + K], elo_ref[:, at : at + K] = pair_block(mine[step], theirs[step], adj_ref, step, me)
+        take_first(theirs[step], v_ref, at)
+    image_ref[...] = dot(ehi_ref[...], v_ref[...]) + dot(elo_ref[...], v_ref[...]) + dot(ehi_ref[:, :K], first_lo)
+
+
+def iterate(adj_ref, coarse_ref, image_ref, *rest):
+    late = 8 - EARLY
+    mine, theirs = rest[:late], rest[late : 2 * late]
+    ehi_ref, elo_ref, send_ref, v_ref = rest[2 * late :]
     me = lax.axis_index("sub")
     coarse = coarse_ref[...]
     first = coarse / CHEB_CENTER
-    ehi_ref[:, :K], elo_ref[:, :K] = split(own_ref[...])
-    v_ref[:K, :], first_lo = split(first)
-    for step in range(8):
-        block = lax.dot_general(mine[step][: 2 * K, :], theirs[step][: 2 * K, :], NT, preferred_element_type=F32)
-        weight = adj_ref[0, slot_of(step, me)].astype(F32) * 0.5
-        at = (step + 1) * K
-        ehi_ref[:, at : at + K], elo_ref[:, at : at + K] = split((block[:K, K:] + block[K:, :K]) * weight)
-        for q in range(OV // K):
-            v_ref[at + q * TAIL : at + (q + 1) * TAIL, :] = theirs[step][2 * K :, q * K : (q + 1) * K]
-    image = dot(ehi_ref[...], v_ref[...]) + dot(elo_ref[...], v_ref[...]) + dot(ehi_ref[:, :K], first_lo)
+    for i in range(late):
+        at = i * K
+        ehi_ref[:, at : at + K], elo_ref[:, at : at + K] = pair_block(mine[i], theirs[i], adj_ref, EARLY + i, me)
+        take_first(theirs[i], v_ref, at)
+    image = image_ref[...] + (dot(ehi_ref[...], v_ref[...]) + dot(elo_ref[...], v_ref[...]))
     second = RHO_SECOND * RHO_FIRST * first + (2.0 * RHO_SECOND / CHEB_HALF) * (coarse - image)
     send_ref[:, :K], send_ref[:, K:] = split(first + second)
 
@@ -154,25 +175,27 @@
     out_ref[...] = local + arrive(adj_ref, margin_ref, slot_of(INSIDE, me), basis_ref[:K, :], other_ref[:, :K])
 
 
-def pick_basis(refs, power, near, me):
+def pick_basis(power, a_ref, b_ref, near, me):
     a, b = STEPS.index((power, 0)), STEPS.index((power, 1))
     take_a = near_step_is_first(power, me) == near
     slot = jnp.where(take_a, slot_of(a, me), slot_of(b, me))
-    return jnp.where(take_a, refs[a][:K, :], refs[b][:K, :]), slot, jnp.where(take_a, a, b)
-
-
-def merge_near(adj_ref, margin_ref, summed_ref, one_ref, two_ref, four_ref, *rest):
-    theirs, out_ref = rest[:8], rest[8]
-    me = lax.axis_index("sub")
-    acc = summed_ref[...]
-    acc += arrive(adj_ref, margin_ref, slot_of(ACROSS, me), theirs[ACROSS][:K, :], one_ref[K:, :K])
-    for power, ref in ((1, one_ref), (2, two_ref), (3, four_ref)):
-        basis, slot, _ = pick_basis(theirs, power, True, me)
-        acc += arrive(adj_ref, margin_ref, slot, basis, ref[:K, :K])
-    out_ref[...] = acc
-
-
-def finish(cols_ref, adj_ref, tiles_ref, diag_ref, rhs_ref, margin_ref, coarse_ref, ehi_ref, elo_ref, summed_ref, send_ref, other_ref, one_ref, two_ref, four_ref, far_ref, *rest):
+    return jnp.where(take_a, a_ref[:K, :], b_ref[:K, :]), slot, jnp.where(take_a, a, b)
+
+
+def merge_near(power, adj_ref, margin_ref, summed_ref, vectors_ref, a_ref, b_ref, out_ref):
+    me = lax.axis_index("sub")
+    basis, slot, _ = pick_basis(power, a_ref, b_ref, True, me)
+    out_ref[...] = summed_ref[...] + arrive(adj_ref, margin_ref, slot, basis, vectors_ref[:K, :K])
+
+
+def merge_next(adj_ref, margin_ref, summed_ref, vectors_ref, across_ref, a_ref, b_ref, out_ref):
+    me = lax.axis_index("sub")
+    acc = summed_ref[...] + arrive(adj_ref, margin_ref, slot_of(ACROSS, me), across_ref[:K, :], vectors_ref[K:, :K])
+    basis, slot, _ = pick_basis(1, a_ref, b_ref, True, me)
+    out_ref[...] = acc + arrive(adj_ref, margin_ref, slot, basis, vectors_ref[:K, :K])
+
+
+def finish(cols_ref, adj_ref, tiles_ref, diag_ref, rhs_ref, margin_ref, coarse_ref, ehi_early, elo_early, ehi_late, elo_late, summed_ref, send_ref, other_ref, one_ref, two_ref, four_ref, far_ref, *rest):
     theirs = rest[:8]
     fine_ref, coarse_out, v_ref, merged = rest[8:]
     me = lax.axis_index("sub")
@@ -182,14 +205,17 @@
     v_ref[(ACROSS + 1) * K : (ACROSS + 2) * K, :] = one_ref[K:, :]
     for power, ref in ((1, one_ref), (2, two_ref), (3, four_ref)):
         far = far_ref[(power - 1) * K : power * K, :]
-        basis, slot, step = pick_basis(theirs, power, False, me)
+        a, b = STEPS.index((power, 0)), STEPS.index((power, 1))
+        basis, slot, step = pick_basis(power, theirs[a], theirs[b], False, me)
         acc += arrive(adj_ref, margin_ref, slot, basis, far[:, :K])
-        near_step = STEPS.index((power, 0)) + STEPS.index((power, 1)) - step
+        near_step = a + b - step
         v_ref[pl.ds(pl.multiple_of((step + 1) * K, K), K), :] = far
         v_ref[pl.ds(pl.multiple_of((near_step + 1) * K, K), K), :] = ref[:K, :]
     merged[...] = acc.astype(BF16)
-    both = dot(ehi_ref[...], v_ref[...])
-    coarse_out[...] = coarse_ref[...] - (both[:, :K] + (both[:, K:] + dot(elo_ref[...], v_ref[:, :K])))
+    early, late = slice(0, (EARLY + 1) * K), slice((EARLY + 1) * K, 9 * K)
+    both = dot(ehi_early[...], v_ref[early, :]) + dot(ehi_late[...], v_ref[late, :])
+    small = dot(elo_early[...], v_ref[early, :K]) + dot(elo_late[...], v_ref[late, :K])
+    coarse_out[...] = coarse_ref[...] - (both[:, :K] + (both[:, K:] + small))
     for b in range(NB):
         rows = slice(b * BLK, (b + 1) * BLK)
         image = column(diag_ref, b) * merged[rows, :].astype(F32) + tile_row(cols_ref, tiles_ref, merged, b)
@@ -200,7 +226,7 @@
     return jax.ShapeDtypeStruct(shape, dtype)
 
 
-def call(kernel, name, in_specs, outs, scratch, flops, limit=32):
+def call(kernel, name, in_specs, outs, scratch, flops, limit=32, moved=2**20):
     return pl.pallas_call(
         kernel,
         name=name,
@@ -209,7 +235,7 @@
         out_shape=outs,
         scratch_shapes=scratch,
         compiler_params=pltpu.CompilerParams(vmem_limit_bytes=limit * 1024 * 1024),
-        cost_estimate=pl.CostEstimate(flops=flops, bytes_accessed=2**20, transcendentals=0),
+        cost_estimate=pl.CostEstimate(flops=flops, bytes_accessed=moved, transcendentals=0),
     )
 
 
@@ -235,34 +261,50 @@
         3 * 10**9,
     )(*(pltpu.with_memory_space_constraint(x, pltpu.HBM) for x in (tile_cols, deflation, op_tiles, diag, fine_rhs, margin)))
     theirs = [swapped(block, *step) for block, step in zip(payloads, STEPS)]
-    ehi, elo, send = call(
+    early = (EARLY + 1) * K
+    ehi_early, elo_early, image = call(
+        iterate_early,
+        "iterate_early",
+        [SMEM] + [VMEM] * (2 + 2 * EARLY),
+        [arr((K, early), BF16)] * 2 + [arr((K, K), F32)],
+        [pltpu.VMEM((early, K), BF16)],
+        10**9,
+    )(adjacency, own, coarse, *payloads[:EARLY], *theirs[:EARLY])
+    late = (8 - EARLY) * K
+    ehi_late, elo_late, send = call(
         iterate,
         "iterate",
-        [SMEM] + [VMEM] * 18,
-        [arr((K, 9 * K), BF16)] * 2 + [arr((K, 2 * K), BF16)],
-        [pltpu.VMEM((9 * K, K), BF16)],
+        [SMEM] + [VMEM] * (2 + 2 * (8 - EARLY)),
+        [arr((K, late), BF16)] * 2 + [arr((K, 2 * K), BF16)],
+        [pltpu.VMEM((late, K), BF16)],
         10**9,
-    )(adjacency, own, coarse, *payloads, *theirs)
+    )(adjacency, coarse, image, *payloads[EARLY:], *theirs[EARLY:])
     other = core_swap(send)
     pair = jnp.concatenate([send, other])
     one, two, four = (both_ways(pair, chips) for chips in (1, 2, 4))
     summed = call(
         merge_chip, "merge_chip", [SMEM] + [VMEM] * 5, [arr((NLOC, K), F32)], [], 10**9
     )(adjacency, deflation, margin, send, other, theirs[INSIDE])[0]
-    hand_over, summed = lax.optimization_barrier((jnp.concatenate([one[K:], two[K:], four[K:]]), summed))
+    near = {power: [theirs[STEPS.index((power, colour))] for colour in (0, 1)] for power in (1, 2, 3)}
+    for power, vectors in ((3, four), (2, two)):
+        summed = call(
+            functools.partial(merge_near, power), f"merge_{power}", [SMEM] + [VMEM] * 5, [arr((NLOC, K), F32)], [], 1, moved=1
+        )(adjacency, margin, summed, vectors, *near[power])[0]
+    one_late, summed = lax.optimization_barrier((one, summed))
+    hand_over = jnp.concatenate([one_late[K:], two[K:], four[K:]])
     far = core_swap(hand_over)
-    summed = call(
-        merge_near, "merge_near", [SMEM] + [VMEM] * 13, [arr((NLOC, K), F32)], [], 2 * 10**9
-    )(adjacency, margin, summed, one, two, four, *theirs)[0]
+    summed = call(merge_next, "merge_next", [SMEM] + [VMEM] * 6, [arr((NLOC, K), F32)], [], 10**9)(
+        adjacency, margin, summed, one, theirs[ACROSS], *near[1]
+    )[0]
     return tuple(
         call(
             finish,
             "finish",
-            [SMEM] * 2 + [VMEM] * 22,
+            [SMEM] * 2 + [VMEM] * 24,
             [arr((NLOC, K), BF16), arr((K, K), F32)],
             [pltpu.VMEM((9 * K, 2 * K), BF16), pltpu.VMEM((NLOC, K), BF16)],
             3 * 10**9,
-        )(tile_cols, adjacency, op_tiles, diag, fine_rhs, margin, coarse, ehi, elo, summed, send, other, one, two, four, far, *theirs)
+        )(tile_cols, adjacency, op_tiles, diag, fine_rhs, margin, coarse, ehi_early, elo_early, ehi_late, elo_late, summed, send, other, one, two, four, far, *theirs)
     )
 
 

time: 85.8 us -> 88.7 us (1.034)
  Pallas kernels: 16.2 us -> 18.2 us
  starting transfers between devices: 63.2 us -> 64.7 us
    pallas_call x3 -> x6, Pallas kernels: 8.95 us -> 11 us  [the longest x1 4.08 us: per_device(): call(finish, 'finish', [SMEM] * 2 + [VMEM] * 24, [arr((NLOC, K), BF16), a...]
    ppermute x13, starting transfers between devices: 63.2 us -> 64.7 us  [permute(): return lax.ppermute(block, 'sub', [(i, target(i) % n) for i in range(n)])]
  transfers between devices with their start and end apart: 13 -> 13, of which waited for: 5 -> 5; matrix products, arithmetic and copies ran while one was open for 0% -> 0% of each run, Pallas kernels for 5% -> 8%
where the time goes in v3:
time: 88.7 us; the launch traced here: 88.2 us
  starting transfers between devices  64.7 us (73%)
  Pallas kernels  18.2 us (21%)
  waiting for transfers between devices  4.35 us (5%)
  between operations  0.96 us (1%)
    ppermute x13, starting transfers between devices, permute(): return lax.ppermute(block, 'sub', [(i, target(i) % n) for i in range(n)])  64.7 us
    pallas_call x1, Pallas kernels, per_device(): call(prepare, 'prepare', [HBM] * 6, [arr((2 * K + TAIL, OV), BF16)] * 8 +...  5.98 us
    ppermute x13, waiting for transfers between devices, permute(): return lax.ppermute(block, 'sub', [(i, target(i) % n) for i in range(n)])  4.35 us
    pallas_call x1, Pallas kernels, per_device(): call(finish, 'finish', [SMEM] * 2 + [VMEM] * 24, [arr((NLOC, K), BF16), a...  4.08 us
    pallas_call x2, Pallas kernels, per_device(): call(functools.partial(merge_near, power), f'merge_{power}', [SMEM] + [VM...  2.31 us
    pallas_call x1, Pallas kernels, per_device(): call(merge_next, 'merge_next', [SMEM] + [VMEM] * 6, [arr((NLOC, K), F32)]...  2.08 us
  transfers between devices with their start and end apart: 13, of which 5 were waited for; matrix products, arithmetic and copies ran while one was open for 0% of the time, Pallas kernels for 8%

profile of v3, /device:TPU:1, one launch (start us, length us, event | category | flops | bytes accessed | tf_op | source)
XLA Modules:
  0.0 88.2 jit_solution(14860558117872948406)
XLA Ops:
  0.6 0.0 copy-start.1
  0.6 6.0 %prepare.1 = (bf16[288,512]{1,0:T(8,128)(2,1)S(1)}, bf16[288,512]{1,0:T(8,128)(2,1)S(1)}, bf16[288,512]{1,0:T(8,128)(2,1)S(1)}, bf16[288,512]{1,0:T(8,128)(2,1)S...) custom-call(s32[48]{0:T(128)} %cols_ref.1, ...), custom_call_target="tpu_custom_call" | custom-call | flops 3000000000 | bytes 1048576 | tf_op jit(solution)/shard_map/prepare/pallas_call | solution.py:245
  6.6 8.8 %collective-permute-start = (bf16[288,512]{1,0:T(8,128)(2,1)S(1)}, bf16[288,512]{1,0:T(8,128)(2,1)S(1)}, u32[]{:S(2)}, u32[]{:S(2)}) collective-permute-start(bf16[288,512]{1,0:T(8,128)(2,1)S(1)} %get-tuple-element.22.rest_0_), channel_id=1, source_target_pairs={{0,1},{1,0},{2,3},{3,2},{4,5},{5,4},{6,7},{7,6},{8,9},{9,8},{10,11... | collective-permute-start | bytes 884744 | tf_op jit(solution)/shard_map/ppermute | solution.py:35
  15.4 1.9 %collective-permute-start.1 = (bf16[288,512]{1,0:T(8,128)(2,1)S(1)}, bf16[288,512]{1,0:T(8,128)(2,1)S(1)}, u32[]{:S(2)}, u32[]{:S(2)}) collective-permute-start(bf16[288,512]{1,0:T(8,128)(2,1)S(1)} %get-tuple-element.23.rest_1_), channel_id=1, source_target_pairs={{0,4},{1,5},{2,6},{3,7},{4,0},{5,1},{6,2},{7,3},{8,12},{9,13},{10,... | collective-permute-start | bytes 884744 | tf_op jit(solution)/shard_map/ppermute | solution.py:35
  17.4 10.9 %collective-permute-start.2 = (bf16[288,512]{1,0:T(8,128)(2,1)S(1)}, bf16[288,512]{1,0:T(8,128)(2,1)S(1)}, u32[]{:S(2)}, u32[]{:S(2)}) collective-permute-start(bf16[288,512]{1,0:T(8,128)(2,1)S(1)} %get-tuple-element.24.rest_2_), channel_id=1, source_target_pairs={{0,508},{1,509},{2,510},{3,511},{4,8},{5,9},{6,10},{7,11},{8,4},{9... | collective-permute-start | bytes 884744 | tf_op jit(solution)/shard_map/ppermute | solution.py:35
  28.2 1.9 %collective-permute-start.3 = (bf16[288,512]{1,0:T(8,128)(2,1)S(1)}, bf16[288,512]{1,0:T(8,128)(2,1)S(1)}, u32[]{:S(2)}, u32[]{:S(2)}) collective-permute-start(bf16[288,512]{1,0:T(8,128)(2,1)S(1)} %get-tuple-element.25.rest_3_), channel_id=1, source_target_pairs={{0,8},{1,9},{2,10},{3,11},{4,12},{5,13},{6,14},{7,15},{8,0},{9,1},... | collective-permute-start | bytes 884744 | tf_op jit(solution)/shard_map/ppermute | solution.py:35
  30.2 3.1 %collective-permute-start.4 = (bf16[288,512]{1,0:T(8,128)(2,1)S(1)}, bf16[288,512]{1,0:T(8,128)(2,1)S(1)}, u32[]{:S(2)}, u32[]{:S(2)}) collective-permute-start(bf16[288,512]{1,0:T(8,128)(2,1)S(1)} %get-tuple-element.26.rest_4_), channel_id=1, source_target_pairs={{0,2},{1,3},{2,0},{3,1},{4,6},{5,7},{6,4},{7,5},{8,10},{9,11},{10,... | collective-permute-start | bytes 884744 | tf_op jit(solution)/shard_map/ppermute | solution.py:35
  33.3 0.0 collective-permute-done.rest_6_.basis_ref.rest_0_
  33.3 4.9 %collective-permute-start.5 = (bf16[288,512]{1,0:T(8,128)(2,1)S(1)}, bf16[288,512]{1,0:T(8,128)(2,1)S(1)}, u32[]{:S(2)}, u32[]{:S(2)}) collective-permute-start(bf16[288,512]{1,0:T(8,128)(2,1)S(1)} %get-tuple-element.27.rest_5_), channel_id=1, source_target_pairs={{0,510},{1,511},{2,4},{3,5},{4,2},{5,3},{6,8},{7,9},{8,6},{9,7},{1... | collective-permute-start | bytes 884744 | tf_op jit(solution)/shard_map/ppermute | solution.py:35
  38.2 0.0 collective-permute-done.1.rest_7_.a_ref.rest_1_
  38.2 3.4 %collective-permute-start.6 = (bf16[288,512]{1,0:T(8,128)(2,1)S(1)}, bf16[288,512]{1,0:T(8,128)(2,1)S(1)}, u32[]{:S(2)}, u32[]{:S(2)}) collective-permute-start(bf16[288,512]{1,0:T(8,128)(2,1)S(1)} %get-tuple-element.31.rest_0_), channel_id=1, source_target_pairs={{0,504},{1,505},{2,506},{3,507},{4,508},{5,509},{6,510},{7,511},{8... | collective-permute-start | bytes 884744 | tf_op jit(solution)/shard_map/ppermute | solution.py:35
  41.6 0.0 collective-permute-done.2.rest_8_.b_ref.rest_2_
  41.6 4.9 %collective-permute-start.7 = (bf16[288,512]{1,0:T(8,128)(2,1)S(1)}, bf16[288,512]{1,0:T(8,128)(2,1)S(1)}, u32[]{:S(2)}, u32[]{:S(2)}) collective-permute-start(bf16[288,512]{1,0:T(8,128)(2,1)S(1)} %get-tuple-element.32.rest_1_), channel_id=1, source_target_pairs={{0,511},{1,2},{2,1},{3,4},{4,3},{5,6},{6,5},{7,8},{8,7},{9,10},{10... | collective-permute-start | bytes 884744 | tf_op jit(solution)/shard_map/ppermute | solution.py:35
  46.5 0.0 collective-permute-done.3.rest_9_.a_ref.rest_3_
  46.5 0.0 collective-permute-done.4.rest_10_.a_ref.rest_4_
  46.5 1.8 %collective-permute-done.5.rest_11_.b_ref.rest_5_ = bf16[288,512]{1,0:T(8,128)(2,1)S(1)} collective-permute-done((bf16[288,512]{1,0:T(8,128)(2,1)S(1)}, bf16[288,512]{1,0:T(8,128)(2,1)S(1)}, u32[]{:S(2)}, u32[]{:S(2)}) %collective-permute-start.5) | collective-permute-done | bytes 294944 | tf_op jit(solution)/shard_map/ppermute | solution.py:35
  48.3 0.0 copy-done.1
  48.3 1.5 %iterate_early.1 = (bf16[128,896]{1,0:T(8,128)(2,1)S(1)}, bf16[128,896]{1,0:T(8,128)(2,1)S(1)}, f32[128,128]{1,0:T(8,128)S(1)}) custom-call(s32[1,8]{1,0:T(1,128)S(1)} %copy-done.1, f32[128,128]{1,0:T(8,128)S(1)} %get-tuple-element.21.own_ref, f32[128,128]{1,0:T(8,128)S(1)} %get-tuple-element.20.coarse_ref, bf16[288,512]{1,0:T(8,128)(2,1)S(1)} %get-tuple-element.22.rest_0_, ...), custom_call_target="tpu_custom_call" | custom-call | flops 1000000000 | bytes 1048576 | tf_op jit(solution)/shard_map/iterate_early/pallas_call | solution.py:265
  49.8 0.7 collective-permute-done.6.rest_2_.b_ref.rest_6_
  50.5 0.6 collective-permute-done.7.rest_3_.across_ref.rest_7_
  51.1 0.0 copy-start
  51.2 0.0 copy-start.3
  51.2 1.0 %iterate.1 = (bf16[128,256]{1,0:T(8,128)(2,1)S(1)}, bf16[128,256]{1,0:T(8,128)(2,1)S(1)}, bf16[128,256]{1,0:T(8,128)(2,1)S(1)}) custom-call(s32[1,8]{1,0:T(1,128)S(1)} %copy-done.1, f32[128,128]{1,0:T(8,128)S(1)} %get-tuple-element.20.coarse_ref, f32[128,128]{1,0:T(8,128)S(1)} %get-tuple-element.30.image_ref, ...), custom_call_target="tpu_custom_call" | custom-call | flops 1000000000 | bytes 1048576 | tf_op jit(solution)/shard_map/iterate/pallas_call | solution.py:274
  52.2 10.3 %collective-permute-start.8 = (bf16[128,256]{1,0:T(8,128)(2,1)S(1)}, bf16[128,256]{1,0:T(8,128)(2,1)S(1)}, u32[]{:S(2)}, u32[]{:S(2)}) collective-permute-start(bf16[128,256]{1,0:T(8,128)(2,1)S(1)} %get-tuple-element.35.send_ref), channel_id=1, source_target_pairs={{0,1},{1,0},{2,3},{3,2},{4,5},{5,4},{6,7},{7,6},{8,9},{9,8},{10,11... | collective-permute-start | bytes 196616 | tf_op jit(solution)/shard_map/ppermute | solution.py:35
  62.5 0.9 collective-permute-done.8.other_ref
  63.4 1.9 %collective-permute-start.10 = (bf16[256,256]{1,0:T(8,128)(2,1)S(1)}, bf16[256,256]{1,0:T(8,128)(2,1)S(1)}, u32[]{:S(2)}, u32[]{:S(2)}) collective-permute-start(bf16[256,256]{1,0:T(8,128)(2,1)S(1)} %constant_dynamic-update-slice_fusion), channel_id=1, source_target_pairs={{0,8},{1,505},{2,10},{3,507},{4,12},{5,509},{6,14},{7,511},{8,16},... | collective-permute-start | bytes 393224 | tf_op jit(solution)/shard_map/ppermute | solution.py:35
  65.3 1.9 %collective-permute-start.11 = (bf16[256,256]{1,0:T(8,128)(2,1)S(1)}, bf16[256,256]{1,0:T(8,128)(2,1)S(1)}, u32[]{:S(2)}, u32[]{:S(2)}) collective-permute-start(bf16[256,256]{1,0:T(8,128)(2,1)S(1)} %constant_dynamic-update-slice_fusion), channel_id=1, source_target_pairs={{0,4},{1,509},{2,6},{3,511},{4,8},{5,1},{6,10},{7,3},{8,12},{9,5},... | collective-permute-start | bytes 393224 | tf_op jit(solution)/shard_map/ppermute | solution.py:35
  67.2 4.6 %collective-permute-start.9 = (bf16[256,256]{1,0:T(8,128)(2,1)S(1)}, bf16[256,256]{1,0:T(8,128)(2,1)S(1)}, u32[]{:S(2)}, u32[]{:S(2)}) collective-permute-start(bf16[256,256]{1,0:T(8,128)(2,1)S(1)} %constant_dynamic-update-slice_fusion), channel_id=1, source_target_pairs={{0,2},{1,511},{2,4},{3,1},{4,6},{5,3},{6,8},{7,5},{8,10},{9,7},{10... | collective-permute-start | bytes 393224 | tf_op jit(solution)/shard_map/ppermute | solution.py:35
  71.8 0.0 copy-done
  71.8 0.0 copy-done.3
  71.8 1.2 %merge_chip.1.summed_ref = f32[1024,128]{1,0:T(8,128)S(1)} custom-call(s32[1,8]{1,0:T(1,128)S(1)} %copy-done.1, bf16[1024,128]{1,0:T(8,128)(2,1)S(1)} %copy-done.3, s32[8,512]{1,0:T(8,128)S(1)} %bitcast.3, bf16[128,256]{1,0:T(8,128)(2,1)S(1)} %get-tuple-element.35.send_ref, bf16[128,256]{1,0:T(8,128)(2,1)S(1)} %collective-permute-done.8.other_ref, ...), custom_call_target="tpu_custom_call" | custom-call | flops 1000000000 | bytes 1048576 | tf_op jit(solution)/shard_map/merge_chip/pallas_call | solution.py:285
  73.0 0.0 collective-permute-done.10.vectors_ref.four_ref
  73.0 1.2 %merge_3.1.summed_ref = f32[1024,128]{1,0:T(8,128)S(1)} custom-call(s32[1,8]{1,0:T(1,128)S(1)} %copy-done.1, s32[8,512]{1,0:T(8,128)S(1)} %bitcast.4, f32[1024,128]{1,0:T(8,128)S(1)} %merge_chip.1.summed_ref, bf16[256,256]{1,0:T(8,128)(2,1)S(1)} %collective-permute-done.10.vectors_ref.four_ref, ...), custom_call_target="tpu_custom_call" | custom-call | flops 1 | bytes 1 | tf_op jit(solution)/shard_map/merge_3/pallas_call | solution.py:290
  74.2 0.0 collective-permute-done.11.vectors_ref.two_ref
  74.2 1.2 %merge_2.1.summed_ref = f32[1024,128]{1,0:T(8,128)S(1)} custom-call(s32[1,8]{1,0:T(1,128)S(1)} %copy-done.1, s32[8,512]{1,0:T(8,128)S(1)} %bitcast.5, f32[1024,128]{1,0:T(8,128)S(1)} %merge_3.1.summed_ref, bf16[256,256]{1,0:T(8,128)(2,1)S(1)} %collective-permute-done.11.vectors_ref.two_ref, ...), custom_call_target="tpu_custom_call" | custom-call | flops 1 | bytes 1 | tf_op jit(solution)/shard_map/merge_2/pallas_call | solution.py:290
  75.4 0.3 collective-permute-done.9.vectors_ref.one_ref
  75.7 0.0 copy-start.2
  75.7 0.0 copy-start.4
  75.7 0.0 copy-start.5
  75.7 0.0 copy-start.6
  75.7 6.3 %collective-permute-start.12 = (bf16[384,256]{1,0:T(8,128)(2,1)S(1)}, bf16[384,256]{1,0:T(8,128)(2,1)S(1)}, u32[]{:S(2)}, u32[]{:S(2)}) collective-permute-start(bf16[384,256]{1,0:T(8,128)(2,1)S(1)} %pad_maximum_fusion), channel_id=1, source_target_pairs={{0,1},{1,0},{2,3},{3,2},{4,5},{5,4},{6,7},{7,6},{8,9},{9,8},{10,11... | collective-permute-start | bytes 589832 | tf_op jit(solution)/shard_map/ppermute | solution.py:35
  82.0 2.1 %merge_next.1.summed_ref = f32[1024,128]{1,0:T(8,128)S(1)} custom-call(s32[1,8]{1,0:T(1,128)S(1)} %copy-done.1, s32[8,512]{1,0:T(8,128)S(1)} %bitcast.6, f32[1024,128]{1,0:T(8,128)S(1)} %merge_2.1.summed_ref, bf16[256,256]{1,0:T(8,128)(2,1)S(1)} %collective-permute-done.9.vectors_ref.one_ref, ...), custom_call_target="tpu_custom_call" | custom-call | flops 1000000000 | bytes 1048576 | tf_op jit(solution)/shard_map/merge_next/pallas_call | solution.py:296
  84.1 0.0 collective-permute-done.12.far_ref
  84.1 0.0 copy-done.2
  84.1 0.0 copy-done.4
  84.1 0.0 copy-done.5
  84.1 0.0 copy-done.6
  84.2 4.1 %finish.1 = (bf16[1024,128]{1,0:T(8,128)(2,1)}, f32[128,128]{1,0:T(8,128)}) custom-call(s32[48]{0:T(128)S(1)} %copy-done.6, s32[1,8]{1,0:T(1,128)S(1)} %copy-done.1, bf16[48,128,128]{2,1,0:T(8,128)(2,1)S(1)} %copy-done.2, f32[8,128]{1,0:T(8,128)S(1)} %bitcast.9, bf16[1024,128]{1,0:T(8,128)(2,1)S(1)} %copy-done.4, s32[8,512]{1,0:T(8,128)S(1)} %bitcast.7, ...), custom_call_target="tpu_custom_call" | custom-call | flops 3000000000 | bytes 1048576 | tf_op jit(solution)/shard_map/finish/pallas_call | solution.py:300
  (6 shorter events, 0.0 us)
Async XLA Ops:
  0.6 47.7 %copy-start.1 = (s32[1,8]{1,0:T(1,128)S(1)}, s32[1,8]{1,0:T(1,128)}, u32[]{:S(2)}) copy-start(s32[1,8]{1,0:T(1,128)} %adj_ref.13) | copy-start | bytes 100
  6.6 26.7 %collective-permute-start = (bf16[288,512]{1,0:T(8,128)(2,1)S(1)}, bf16[288,512]{1,0:T(8,128)(2,1)S(1)}, u32[]{:S(2)}, u32[]{:S(2)}) collective-permute-start(bf16[288,512]{1,0:T(8,128)(2,1)S(1)} %get-tuple-element.22.rest_0_), channel_id=1, source_target_pairs={{0,1},{1,0},{2,3},{3,2},{4,5},{5,4},{6,7},{7,6},{8,9},{9,8},{10,11... | collective-permute-start | bytes 884744 | tf_op jit(solution)/shard_map/ppermute | solution.py:35
  15.4 22.8 %collective-permute-start.1 = (bf16[288,512]{1,0:T(8,128)(2,1)S(1)}, bf16[288,512]{1,0:T(8,128)(2,1)S(1)}, u32[]{:S(2)}, u32[]{:S(2)}) collective-permute-start(bf16[288,512]{1,0:T(8,128)(2,1)S(1)} %get-tuple-element.23.rest_1_), channel_id=1, source_target_pairs={{0,4},{1,5},{2,6},{3,7},{4,0},{5,1},{6,2},{7,3},{8,12},{9,13},{10,... | collective-permute-start | bytes 884744 | tf_op jit(solution)/shard_map/ppermute | solution.py:35
  17.4 24.2 %collective-permute-start.2 = (bf16[288,512]{1,0:T(8,128)(2,1)S(1)}, bf16[288,512]{1,0:T(8,128)(2,1)S(1)}, u32[]{:S(2)}, u32[]{:S(2)}) collective-permute-start(bf16[288,512]{1,0:T(8,128)(2,1)S(1)} %get-tuple-element.24.rest_2_), channel_id=1, source_target_pairs={{0,508},{1,509},{2,510},{3,511},{4,8},{5,9},{6,10},{7,11},{8,4},{9... | collective-permute-start | bytes 884744 | tf_op jit(solution)/shard_map/ppermute | solution.py:35
  28.2 18.2 %collective-permute-start.3 = (bf16[288,512]{1,0:T(8,128)(2,1)S(1)}, bf16[288,512]{1,0:T(8,128)(2,1)S(1)}, u32[]{:S(2)}, u32[]{:S(2)}) collective-permute-start(bf16[288,512]{1,0:T(8,128)(2,1)S(1)} %get-tuple-element.25.rest_3_), channel_id=1, source_target_pairs={{0,8},{1,9},{2,10},{3,11},{4,12},{5,13},{6,14},{7,15},{8,0},{9,1},... | collective-permute-start | bytes 884744 | tf_op jit(solution)/shard_map/ppermute | solution.py:35
  30.2 16.3 %collective-permute-start.4 = (bf16[288,512]{1,0:T(8,128)(2,1)S(1)}, bf16[288,512]{1,0:T(8,128)(2,1)S(1)}, u32[]{:S(2)}, u32[]{:S(2)}) collective-permute-start(bf16[288,512]{1,0:T(8,128)(2,1)S(1)} %get-tuple-element.26.rest_4_), channel_id=1, source_target_pairs={{0,2},{1,3},{2,0},{3,1},{4,6},{5,7},{6,4},{7,5},{8,10},{9,11},{10,... | collective-permute-start | bytes 884744 | tf_op jit(solution)/shard_map/ppermute | solution.py:35
  33.3 15.0 %collective-permute-start.5 = (bf16[288,512]{1,0:T(8,128)(2,1)S(1)}, bf16[288,512]{1,0:T(8,128)(2,1)S(1)}, u32[]{:S(2)}, u32[]{:S(2)}) collective-permute-start(bf16[288,512]{1,0:T(8,128)(2,1)S(1)} %get-tuple-element.27.rest_5_), channel_id=1, source_target_pairs={{0,510},{1,511},{2,4},{3,5},{4,2},{5,3},{6,8},{7,9},{8,6},{9,7},{1... | collective-permute-start | bytes 884744 | tf_op jit(solution)/shard_map/ppermute | solution.py:35
  38.2 12.3 %collective-permute-start.6 = (bf16[288,512]{1,0:T(8,128)(2,1)S(1)}, bf16[288,512]{1,0:T(8,128)(2,1)S(1)}, u32[]{:S(2)}, u32[]{:S(2)}) collective-permute-start(bf16[288,512]{1,0:T(8,128)(2,1)S(1)} %get-tuple-element.31.rest_0_), channel_id=1, source_target_pairs={{0,504},{1,505},{2,506},{3,507},{4,508},{5,509},{6,510},{7,511},{8... | collective-permute-start | bytes 884744 | tf_op jit(solution)/shard_map/ppermute | solution.py:35
  41.6 9.6 %collective-permute-start.7 = (bf16[288,512]{1,0:T(8,128)(2,1)S(1)}, bf16[288,512]{1,0:T(8,128)(2,1)S(1)}, u32[]{:S(2)}, u32[]{:S(2)}) collective-permute-start(bf16[288,512]{1,0:T(8,128)(2,1)S(1)} %get-tuple-element.32.rest_1_), channel_id=1, source_target_pairs={{0,511},{1,2},{2,1},{3,4},{4,3},{5,6},{6,5},{7,8},{8,7},{9,10},{10... | collective-permute-start | bytes 884744 | tf_op jit(solution)/shard_map/ppermute | solution.py:35
  51.1 20.6 %copy-start = (s32[1,8,512]{2,1,0:T(8,128)S(1)}, s32[1,8,512]{2,1,0:T(8,128)}, u32[]{:S(2)}) copy-start(s32[1,8,512]{2,1,0:T(8,128)} %param.13) | copy-start | bytes 49156
  51.2 20.7 %copy-start.3 = (bf16[1024,128]{1,0:T(8,128)(2,1)S(1)}, bf16[1024,128]{1,0:T(8,128)(2,1)}, u32[]{:S(2)}) copy-start(bf16[1024,128]{1,0:T(8,128)(2,1)} %z_ref.1) | copy-start | bytes 786436
  52.2 11.2 %collective-permute-start.8 = (bf16[128,256]{1,0:T(8,128)(2,1)S(1)}, bf16[128,256]{1,0:T(8,128)(2,1)S(1)}, u32[]{:S(2)}, u32[]{:S(2)}) collective-permute-start(bf16[128,256]{1,0:T(8,128)(2,1)S(1)} %get-tuple-element.35.send_ref), channel_id=1, source_target_pairs={{0,1},{1,0},{2,3},{3,2},{4,5},{5,4},{6,7},{7,6},{8,9},{9,8},{10,11... | collective-permute-start | bytes 196616 | tf_op jit(solution)/shard_map/ppermute | solution.py:35
  63.4 9.6 %collective-permute-start.10 = (bf16[256,256]{1,0:T(8,128)(2,1)S(1)}, bf16[256,256]{1,0:T(8,128)(2,1)S(1)}, u32[]{:S(2)}, u32[]{:S(2)}) collective-permute-start(bf16[256,256]{1,0:T(8,128)(2,1)S(1)} %constant_dynamic-update-slice_fusion), channel_id=1, source_target_pairs={{0,8},{1,505},{2,10},{3,507},{4,12},{5,509},{6,14},{7,511},{8,16},... | collective-permute-start | bytes 393224 | tf_op jit(solution)/shard_map/ppermute | solution.py:35
  65.3 8.9 %collective-permute-start.11 = (bf16[256,256]{1,0:T(8,128)(2,1)S(1)}, bf16[256,256]{1,0:T(8,128)(2,1)S(1)}, u32[]{:S(2)}, u32[]{:S(2)}) collective-permute-start(bf16[256,256]{1,0:T(8,128)(2,1)S(1)} %constant_dynamic-update-slice_fusion), channel_id=1, source_target_pairs={{0,4},{1,509},{2,6},{3,511},{4,8},{5,1},{6,10},{7,3},{8,12},{9,5},... | collective-permute-start | bytes 393224 | tf_op jit(solution)/shard_map/ppermute | solution.py:35
  67.2 8.4 %collective-permute-start.9 = (bf16[256,256]{1,0:T(8,128)(2,1)S(1)}, bf16[256,256]{1,0:T(8,128)(2,1)S(1)}, u32[]{:S(2)}, u32[]{:S(2)}) collective-permute-start(bf16[256,256]{1,0:T(8,128)(2,1)S(1)} %constant_dynamic-update-slice_fusion), channel_id=1, source_target_pairs={{0,2},{1,511},{2,4},{3,1},{4,6},{5,3},{6,8},{7,5},{8,10},{9,7},{10... | collective-permute-start | bytes 393224 | tf_op jit(solution)/shard_map/ppermute | solution.py:35
  75.7 8.4 %copy-start.2 = (bf16[48,128,128]{2,1,0:T(8,128)(2,1)S(1)}, bf16[48,128,128]{2,1,0:T(8,128)(2,1)}, u32[]{:S(2)}) copy-start(bf16[48,128,128]{2,1,0:T(8,128)(2,1)} %tiles_ref.1) | copy-start | bytes 4718596
  75.7 8.4 %copy-start.4 = (bf16[1024,128]{1,0:T(8,128)(2,1)S(1)}, bf16[1024,128]{1,0:T(8,128)(2,1)}, u32[]{:S(2)}) copy-start(bf16[1024,128]{1,0:T(8,128)(2,1)} %rhs_ref.1) | copy-start | bytes 786436
  75.7 8.4 %copy-start.5 = (f32[1024]{0:T(1024)S(1)}, f32[1024]{0:T(1024)}, u32[]{:S(2)}) copy-start(f32[1024]{0:T(1024)} %param.10) | copy-start | bytes 12292
  75.7 8.4 %copy-start.6 = (s32[48]{0:T(128)S(1)}, s32[48]{0:T(128)}, u32[]{:S(2)}) copy-start(s32[48]{0:T(128)} %cols_ref.1) | copy-start | bytes 580
  75.7 8.4 %collective-permute-start.12 = (bf16[384,256]{1,0:T(8,128)(2,1)S(1)}, bf16[384,256]{1,0:T(8,128)(2,1)S(1)}, u32[]{:S(2)}, u32[]{:S(2)}) collective-permute-start(bf16[384,256]{1,0:T(8,128)(2,1)S(1)} %pad_maximum_fusion), channel_id=1, source_target_pairs={{0,1},{1,0},{2,3},{3,2},{4,5},{5,4},{6,7},{7,6},{8,9},{9,8},{10,11... | collective-permute-start | bytes 589832 | tf_op jit(solution)/shard_map/ppermute | solution.py:35

commit v4 on v3

--- a/solution.py
+++ b/solution.py
@@ -24,7 +24,7 @@
 SMEM = pl.BlockSpec(memory_space=pltpu.SMEM)
 HBM = pl.BlockSpec(memory_space=pltpu.HBM)
 NT = (((1,), (1,)), ((), ()))
-STEPS = ((0, 0), (2, 0), (2, 1), (3, 0), (1, 0), (1, 1), (3, 1), (0, 1))
+STEPS = ((2, 0), (2, 1), (1, 0), (1, 1), (0, 1), (3, 0), (3, 1), (0, 0))
 EARLY = 6
 INSIDE = STEPS.index((0, 0))
 ACROSS = STEPS.index((0, 1))
@@ -87,37 +87,37 @@
 
 def prepare(cols_in, z_in, tiles_in, diag_in, rhs_in, margin_in, *rest):
     payloads, (own_ref, coarse_ref) = rest[:8], rest[8:10]
-    cols_ref, z_ref, tiles_ref, diag_ref, rhs_ref, margin_ref, zit, im_rhs, sems = rest[10:]
-    me = lax.axis_index("sub")
-    pairs = [(cols_in, cols_ref), (z_in, z_ref), (diag_in, diag_ref)]
+    cols_ref, z_ref, tiles_ref, diag_ref, rhs_ref, margin_ref, zit, images, sems = rest[10:]
+    me = lax.axis_index("sub")
+    pairs = [(z_in, z_ref), (rhs_in, rhs_ref), (cols_in, cols_ref), (diag_in, diag_ref)]
     pairs += [(tiles_in.at[pl.ds(TPR * b, TPR)], tiles_ref.at[pl.ds(TPR * b, TPR)]) for b in range(NB)]
-    pairs += [(rhs_in, rhs_ref), (margin_in, margin_ref)]
+    pairs += [(margin_in, margin_ref)]
     copies = [pltpu.make_async_copy(src, dst, sems.at[i]) for i, (src, dst) in enumerate(pairs)]
     for copy in copies:
         copy.start()
-    for copy in copies[:3]:
+    copies[0].wait()
+    for b in range(NB):
+        rows = slice(b * BLK, (b + 1) * BLK)
+        zit[:K, rows] = z_ref[rows, :].T
+    for copy in copies[1:4]:
+        copy.wait()
+    coarse = jnp.dot(zit[:K, :], rhs_ref[...], preferred_element_type=F32)
+    coarse_ref[...] = coarse
+    first = (coarse / CHEB_CENTER).astype(BF16)
+    for copy in copies[4:]:
         copy.wait()
     for b in range(NB):
-        copies[3 + b].wait()
         rows = slice(b * BLK, (b + 1) * BLK)
         z = z_ref[rows, :]
         image = (column(diag_ref, b) * z.astype(F32) + tile_row(cols_ref, tiles_ref, z_ref, b)).astype(BF16)
-        zit[:K, rows] = z.T
         zit[K:, rows] = image.T
-        im_rhs[rows, :K] = image
-    copies[-2].wait()
-    copies[-1].wait()
-    im_rhs[:, K:] = rhs_ref[...]
-    both = jnp.dot(zit[:K, :], im_rhs[...], preferred_element_type=F32)
-    own_ref[...] = both[:, :K]
-    coarse = both[:, K:]
-    coarse_ref[...] = coarse
-    first = (coarse / CHEB_CENTER).astype(BF16)
+        images[rows, :] = image
     for step, out in enumerate(payloads):
         onehot = picks(margin_ref, slot_of(step, me))
         out[: 2 * K, :] = jnp.dot(zit[...], onehot, preferred_element_type=F32).astype(BF16)
         for q in range(OV // K):
             out[2 * K :, q * K : (q + 1) * K] = first[q * TAIL : (q + 1) * TAIL, :]
+    own_ref[...] = jnp.dot(zit[:K, :], images[...], preferred_element_type=F32)
 
 
 dot = functools.partial(jnp.dot, preferred_element_type=F32)
@@ -169,6 +169,19 @@
     return lax.dot_general(picks(margin_ref, slot), corr, NT, preferred_element_type=F32)
 
 
+def corrections(adj_ref, pieces):
+    out = []
+    for slot, basis, coeffs in pieces:
+        corr = lax.dot_general(coeffs, basis, (((0,), (0,)), ((), ())), preferred_element_type=F32).astype(BF16)
+        out.append(corr * adj_ref[0, slot].astype(BF16))
+    return out
+
+
+def scatter(margin_ref, slots, corrs):
+    onehot = jnp.concatenate([picks(margin_ref, slot) for slot in slots], axis=1)
+    return lax.dot_general(onehot, jnp.concatenate(corrs, axis=1), NT, preferred_element_type=F32)
+
+
 def merge_chip(adj_ref, z_ref, margin_ref, send_ref, other_ref, basis_ref, out_ref):
     me = lax.axis_index("sub")
     local = dot(z_ref[...], send_ref[:, :K]).astype(BF16).astype(F32)
@@ -190,16 +203,17 @@
 
 def merge_next(adj_ref, margin_ref, summed_ref, vectors_ref, across_ref, a_ref, b_ref, out_ref):
     me = lax.axis_index("sub")
-    acc = summed_ref[...] + arrive(adj_ref, margin_ref, slot_of(ACROSS, me), across_ref[:K, :], vectors_ref[K:, :K])
     basis, slot, _ = pick_basis(1, a_ref, b_ref, True, me)
-    out_ref[...] = acc + arrive(adj_ref, margin_ref, slot, basis, vectors_ref[:K, :K])
+    slots = (slot_of(ACROSS, me), slot)
+    corrs = corrections(adj_ref, ((slots[0], across_ref[:K, :], vectors_ref[K:, :K]), (slot, basis, vectors_ref[:K, :K])))
+    out_ref[...] = summed_ref[...] + scatter(margin_ref, slots, corrs)
 
 
 def finish(cols_ref, adj_ref, tiles_ref, diag_ref, rhs_ref, margin_ref, coarse_ref, ehi_early, elo_early, ehi_late, elo_late, summed_ref, send_ref, other_ref, one_ref, two_ref, four_ref, far_ref, *rest):
     theirs = rest[:8]
     fine_ref, coarse_out, v_ref, merged = rest[8:]
     me = lax.axis_index("sub")
-    acc = summed_ref[...]
+    pieces = []
     v_ref[:K, :] = send_ref[...]
     v_ref[(INSIDE + 1) * K : (INSIDE + 2) * K, :] = other_ref[...]
     v_ref[(ACROSS + 1) * K : (ACROSS + 2) * K, :] = one_ref[K:, :]
@@ -207,11 +221,12 @@
         far = far_ref[(power - 1) * K : power * K, :]
         a, b = STEPS.index((power, 0)), STEPS.index((power, 1))
         basis, slot, step = pick_basis(power, theirs[a], theirs[b], False, me)
-        acc += arrive(adj_ref, margin_ref, slot, basis, far[:, :K])
+        pieces.append((slot, basis, far[:, :K]))
         near_step = a + b - step
         v_ref[pl.ds(pl.multiple_of((step + 1) * K, K), K), :] = far
         v_ref[pl.ds(pl.multiple_of((near_step + 1) * K, K), K), :] = ref[:K, :]
-    merged[...] = acc.astype(BF16)
+    added = scatter(margin_ref, [p[0] for p in pieces], corrections(adj_ref, pieces))
+    merged[...] = (summed_ref[...] + added).astype(BF16)
     early, late = slice(0, (EARLY + 1) * K), slice((EARLY + 1) * K, 9 * K)
     both = dot(ehi_early[...], v_ref[early, :]) + dot(ehi_late[...], v_ref[late, :])
     small = dot(elo_early[...], v_ref[early, :K]) + dot(elo_late[...], v_ref[late, :K])
@@ -255,7 +270,7 @@
             pltpu.VMEM((NLOC, K), BF16),
             pltpu.VMEM((8, OV), jnp.int32),
             pltpu.VMEM((2 * K, NLOC), BF16),
-            pltpu.VMEM((NLOC, 2 * K), BF16),
+            pltpu.VMEM((NLOC, K), BF16),
             pltpu.SemaphoreType.DMA((NB + 5,)),
         ],
         3 * 10**9,

time: 88.7 us -> 81 us (0.913)
  Pallas kernels: 18.2 us -> 15.2 us
  starting transfers between devices: 64.7 us -> 62.1 us
  waiting for transfers between devices: 4.35 us -> 2.02 us
    ppermute x13, starting transfers between devices: 64.7 us -> 62.1 us  [permute(): return lax.ppermute(block, 'sub', [(i, target(i) % n) for i in range(n)])]
    ppermute x13, waiting for transfers between devices: 4.35 us -> 2.02 us  [permute(): return lax.ppermute(block, 'sub', [(i, target(i) % n) for i in range(n)])]
    pallas_call x1, Pallas kernels: 5.98 us -> 4.64 us  [per_device(): call(prepare, 'prepare', [HBM] * 6, [arr((2 * K + TAIL, OV), BF16)] * 8 +...]
    pallas_call x1, Pallas kernels: 4.08 us -> 3.1 us  [per_device(): call(finish, 'finish', [SMEM] * 2 + [VMEM] * 24, [arr((NLOC, K), BF16), a...]
  transfers between devices with their start and end apart: 13 -> 13, of which waited for: 5 -> 2; matrix products, arithmetic and copies ran while one was open for 0% -> 0% of each run, Pallas kernels for 8% -> 8%
where the time goes in v4:
time: 81 us; the launch traced here: 80.5 us
  starting transfers between devices  62.1 us (77%)
  Pallas kernels  15.2 us (19%)
  waiting for transfers between devices  2.02 us (2%)
  between operations  1.01 us (1%)
    ppermute x13, starting transfers between devices, permute(): return lax.ppermute(block, 'sub', [(i, target(i) % n) for i in range(n)])  62.1 us
    pallas_call x1, Pallas kernels, per_device(): call(prepare, 'prepare', [HBM] * 6, [arr((2 * K + TAIL, OV), BF16)] * 8 +...  4.64 us
    pallas_call x1, Pallas kernels, per_device(): call(finish, 'finish', [SMEM] * 2 + [VMEM] * 24, [arr((NLOC, K), BF16), a...  3.1 us
    pallas_call x2, Pallas kernels, per_device(): call(functools.partial(merge_near, power), f'merge_{power}', [SMEM] + [VM...  2.32 us
    ppermute x13, waiting for transfers between devices, permute(): return lax.ppermute(block, 'sub', [(i, target(i) % n) for i in range(n)])  2.02 us
  transfers between devices with their start and end apart: 13, of which 2 were waited for; matrix products, arithmetic and copies ran while one was open for 0% of the time, Pallas kernels for 8%

profile of v4, /device:TPU:1, one launch (start us, length us, event | category | flops | bytes accessed | tf_op | source)
XLA Modules:
  0.0 80.5 jit_solution(17828858619936716082)
XLA Ops:
  0.6 0.0 copy-start.1
  0.6 4.6 %prepare.1 = (bf16[288,512]{1,0:T(8,128)(2,1)S(1)}, bf16[288,512]{1,0:T(8,128)(2,1)S(1)}, bf16[288,512]{1,0:T(8,128)(2,1)S(1)}, bf16[288,512]{1,0:T(8,128)(2,1)S...) custom-call(s32[48]{0:T(128)} %cols_ref.1, ...), custom_call_target="tpu_custom_call" | custom-call | flops 3000000000 | bytes 1048576 | tf_op jit(solution)/shard_map/prepare/pallas_call | solution.py:260
  5.3 5.5 %collective-permute-start = (bf16[288,512]{1,0:T(8,128)(2,1)S(1)}, bf16[288,512]{1,0:T(8,128)(2,1)S(1)}, u32[]{:S(2)}, u32[]{:S(2)}) collective-permute-start(bf16[288,512]{1,0:T(8,128)(2,1)S(1)} %get-tuple-element.22.rest_0_), channel_id=1, source_target_pairs={{0,4},{1,5},{2,6},{3,7},{4,0},{5,1},{6,2},{7,3},{8,12},{9,13},{10,... | collective-permute-start | bytes 884744 | tf_op jit(solution)/shard_map/ppermute | solution.py:35
  10.8 13.5 %collective-permute-start.1 = (bf16[288,512]{1,0:T(8,128)(2,1)S(1)}, bf16[288,512]{1,0:T(8,128)(2,1)S(1)}, u32[]{:S(2)}, u32[]{:S(2)}) collective-permute-start(bf16[288,512]{1,0:T(8,128)(2,1)S(1)} %get-tuple-element.23.rest_1_), channel_id=1, source_target_pairs={{0,508},{1,509},{2,510},{3,511},{4,8},{5,9},{6,10},{7,11},{8,4},{9... | collective-permute-start | bytes 884744 | tf_op jit(solution)/shard_map/ppermute | solution.py:35
  24.3 3.1 %collective-permute-start.2 = (bf16[288,512]{1,0:T(8,128)(2,1)S(1)}, bf16[288,512]{1,0:T(8,128)(2,1)S(1)}, u32[]{:S(2)}, u32[]{:S(2)}) collective-permute-start(bf16[288,512]{1,0:T(8,128)(2,1)S(1)} %get-tuple-element.24.rest_2_), channel_id=1, source_target_pairs={{0,2},{1,3},{2,0},{3,1},{4,6},{5,7},{6,4},{7,5},{8,10},{9,11},{10,... | collective-permute-start | bytes 884744 | tf_op jit(solution)/shard_map/ppermute | solution.py:35
  27.4 1.9 %collective-permute-start.3 = (bf16[288,512]{1,0:T(8,128)(2,1)S(1)}, bf16[288,512]{1,0:T(8,128)(2,1)S(1)}, u32[]{:S(2)}, u32[]{:S(2)}) collective-permute-start(bf16[288,512]{1,0:T(8,128)(2,1)S(1)} %get-tuple-element.25.rest_3_), channel_id=1, source_target_pairs={{0,510},{1,511},{2,4},{3,5},{4,2},{5,3},{6,8},{7,9},{8,6},{9,7},{1... | collective-permute-start | bytes 884744 | tf_op jit(solution)/shard_map/ppermute | solution.py:35
  29.4 3.6 %collective-permute-start.4 = (bf16[288,512]{1,0:T(8,128)(2,1)S(1)}, bf16[288,512]{1,0:T(8,128)(2,1)S(1)}, u32[]{:S(2)}, u32[]{:S(2)}) collective-permute-start(bf16[288,512]{1,0:T(8,128)(2,1)S(1)} %get-tuple-element.26.rest_4_), channel_id=1, source_target_pairs={{0,511},{1,2},{2,1},{3,4},{4,3},{5,6},{6,5},{7,8},{8,7},{9,10},{10... | collective-permute-start | bytes 884744 | tf_op jit(solution)/shard_map/ppermute | solution.py:35
  32.9 0.0 collective-permute-done.rest_6_.a_ref.rest_0_
  32.9 1.9 %collective-permute-start.5 = (bf16[288,512]{1,0:T(8,128)(2,1)S(1)}, bf16[288,512]{1,0:T(8,128)(2,1)S(1)}, u32[]{:S(2)}, u32[]{:S(2)}) collective-permute-start(bf16[288,512]{1,0:T(8,128)(2,1)S(1)} %get-tuple-element.27.rest_5_), channel_id=1, source_target_pairs={{0,8},{1,9},{2,10},{3,11},{4,12},{5,13},{6,14},{7,15},{8,0},{9,1},... | collective-permute-start | bytes 884744 | tf_op jit(solution)/shard_map/ppermute | solution.py:35
  34.9 0.0 collective-permute-done.1.rest_7_.b_ref.rest_1_
  34.9 5.5 %collective-permute-start.6 = (bf16[288,512]{1,0:T(8,128)(2,1)S(1)}, bf16[288,512]{1,0:T(8,128)(2,1)S(1)}, u32[]{:S(2)}, u32[]{:S(2)}) collective-permute-start(bf16[288,512]{1,0:T(8,128)(2,1)S(1)} %get-tuple-element.31.rest_0_), channel_id=1, source_target_pairs={{0,504},{1,505},{2,506},{3,507},{4,508},{5,509},{6,510},{7,511},{8... | collective-permute-start | bytes 884744 | tf_op jit(solution)/shard_map/ppermute | solution.py:35
  40.4 0.0 collective-permute-done.2.rest_8_.a_ref.rest_2_
  40.4 5.2 %collective-permute-start.7 = (bf16[288,512]{1,0:T(8,128)(2,1)S(1)}, bf16[288,512]{1,0:T(8,128)(2,1)S(1)}, u32[]{:S(2)}, u32[]{:S(2)}) collective-permute-start(bf16[288,512]{1,0:T(8,128)(2,1)S(1)} %get-tuple-element.32.rest_1_), channel_id=1, source_target_pairs={{0,1},{1,0},{2,3},{3,2},{4,5},{5,4},{6,7},{7,6},{8,9},{9,8},{10,11... | collective-permute-start | bytes 884744 | tf_op jit(solution)/shard_map/ppermute | solution.py:35
  45.6 0.0 collective-permute-done.3.rest_9_.b_ref.rest_3_
  45.6 0.0 collective-permute-done.4.rest_10_.across_ref.rest_4_
  45.6 0.0 collective-permute-done.5.rest_11_.a_ref.rest_5_
  45.6 0.0 copy-done.1
  45.6 1.5 %iterate_early.1 = (bf16[128,896]{1,0:T(8,128)(2,1)S(1)}, bf16[128,896]{1,0:T(8,128)(2,1)S(1)}, f32[128,128]{1,0:T(8,128)S(1)}) custom-call(s32[1,8]{1,0:T(1,128)S(1)} %copy-done.1, f32[128,128]{1,0:T(8,128)S(1)} %get-tuple-element.21.own_ref, f32[128,128]{1,0:T(8,128)S(1)} %get-tuple-element.20.coarse_ref, bf16[288,512]{1,0:T(8,128)(2,1)S(1)} %get-tuple-element.22.rest_0_, ...), custom_call_target="tpu_custom_call" | custom-call | flops 1000000000 | bytes 1048576 | tf_op jit(solution)/shard_map/iterate_early/pallas_call | solution.py:280
  47.1 0.0 collective-permute-done.6.rest_2_.b_ref.rest_6_
  47.1 0.0 collective-permute-done.7.rest_3_.basis_ref.rest_7_
  47.1 0.0 copy-start
  47.1 0.0 copy-start.3
  47.2 1.0 %iterate.1 = (bf16[128,256]{1,0:T(8,128)(2,1)S(1)}, bf16[128,256]{1,0:T(8,128)(2,1)S(1)}, bf16[128,256]{1,0:T(8,128)(2,1)S(1)}) custom-call(s32[1,8]{1,0:T(1,128)S(1)} %copy-done.1, f32[128,128]{1,0:T(8,128)S(1)} %get-tuple-element.20.coarse_ref, f32[128,128]{1,0:T(8,128)S(1)} %get-tuple-element.30.image_ref, ...), custom_call_target="tpu_custom_call" | custom-call | flops 1000000000 | bytes 1048576 | tf_op jit(solution)/shard_map/iterate/pallas_call | solution.py:289
  48.2 7.2 %collective-permute-start.8 = (bf16[128,256]{1,0:T(8,128)(2,1)S(1)}, bf16[128,256]{1,0:T(8,128)(2,1)S(1)}, u32[]{:S(2)}, u32[]{:S(2)}) collective-permute-start(bf16[128,256]{1,0:T(8,128)(2,1)S(1)} %get-tuple-element.35.send_ref), channel_id=1, source_target_pairs={{0,1},{1,0},{2,3},{3,2},{4,5},{5,4},{6,7},{7,6},{8,9},{9,8},{10,11... | collective-permute-start | bytes 196616 | tf_op jit(solution)/shard_map/ppermute | solution.py:35
  55.4 0.9 %collective-permute-done.8.other_ref = bf16[128,256]{1,0:T(8,128)(2,1)S(1)} collective-permute-done((bf16[128,256]{1,0:T(8,128)(2,1)S(1)}, bf16[128,256]{1,0:T(8,128)(2,1)S(1)}, u32[]{:S(2)}, u32[]{:S(2)}) %collective-permute-start.8) | collective-permute-done | bytes 65568 | tf_op jit(solution)/shard_map/ppermute | solution.py:35
  56.3 4.1 %collective-permute-start.10 = (bf16[256,256]{1,0:T(8,128)(2,1)S(1)}, bf16[256,256]{1,0:T(8,128)(2,1)S(1)}, u32[]{:S(2)}, u32[]{:S(2)}) collective-permute-start(bf16[256,256]{1,0:T(8,128)(2,1)S(1)} %constant_dynamic-update-slice_fusion), channel_id=1, source_target_pairs={{0,8},{1,505},{2,10},{3,507},{4,12},{5,509},{6,14},{7,511},{8,16},... | collective-permute-start | bytes 393224 | tf_op jit(solution)/shard_map/ppermute | solution.py:35
  60.4 4.9 %collective-permute-start.11 = (bf16[256,256]{1,0:T(8,128)(2,1)S(1)}, bf16[256,256]{1,0:T(8,128)(2,1)S(1)}, u32[]{:S(2)}, u32[]{:S(2)}) collective-permute-start(bf16[256,256]{1,0:T(8,128)(2,1)S(1)} %constant_dynamic-update-slice_fusion), channel_id=1, source_target_pairs={{0,4},{1,509},{2,6},{3,511},{4,8},{5,1},{6,10},{7,3},{8,12},{9,5},... | collective-permute-start | bytes 393224 | tf_op jit(solution)/shard_map/ppermute | solution.py:35
  65.3 1.9 %collective-permute-start.9 = (bf16[256,256]{1,0:T(8,128)(2,1)S(1)}, bf16[256,256]{1,0:T(8,128)(2,1)S(1)}, u32[]{:S(2)}, u32[]{:S(2)}) collective-permute-start(bf16[256,256]{1,0:T(8,128)(2,1)S(1)} %constant_dynamic-update-slice_fusion), channel_id=1, source_target_pairs={{0,2},{1,511},{2,4},{3,1},{4,6},{5,3},{6,8},{7,5},{8,10},{9,7},{10... | collective-permute-start | bytes 393224 | tf_op jit(solution)/shard_map/ppermute | solution.py:35
  67.2 0.0 copy-done
  67.2 0.0 copy-done.3
  67.3 1.2 %merge_chip.1.summed_ref = f32[1024,128]{1,0:T(8,128)S(1)} custom-call(s32[1,8]{1,0:T(1,128)S(1)} %copy-done.1, bf16[1024,128]{1,0:T(8,128)(2,1)S(1)} %copy-done.3, s32[8,512]{1,0:T(8,128)S(1)} %bitcast.3, bf16[128,256]{1,0:T(8,128)(2,1)S(1)} %get-tuple-element.35.send_ref, bf16[128,256]{1,0:T(8,128)(2,1)S(1)} %collective-permute-done.8.other_ref, ...), custom_call_target="tpu_custom_call" | custom-call | flops 1000000000 | bytes 1048576 | tf_op jit(solution)/shard_map/merge_chip/pallas_call | solution.py:300
  68.5 0.0 collective-permute-done.10.vectors_ref.four_ref
  68.5 1.2 %merge_3.1.summed_ref = f32[1024,128]{1,0:T(8,128)S(1)} custom-call(s32[1,8]{1,0:T(1,128)S(1)} %copy-done.1, s32[8,512]{1,0:T(8,128)S(1)} %bitcast.4, f32[1024,128]{1,0:T(8,128)S(1)} %merge_chip.1.summed_ref, bf16[256,256]{1,0:T(8,128)(2,1)S(1)} %collective-permute-done.10.vectors_ref.four_ref, ...), custom_call_target="tpu_custom_call" | custom-call | flops 1 | bytes 1 | tf_op jit(solution)/shard_map/merge_3/pallas_call | solution.py:305
  69.6 1.1 %collective-permute-done.11.vectors_ref.two_ref = bf16[256,256]{1,0:T(8,128)(2,1)S(1)} collective-permute-done((bf16[256,256]{1,0:T(8,128)(2,1)S(1)}, bf16[256,256]{1,0:T(8,128)(2,1)S(1)}, u32[]{:S(2)}, u32[]{:S(2)}) %collective-permute-start.11) | collective-permute-done | bytes 131104 | tf_op jit(solution)/shard_map/ppermute | solution.py:35
  70.8 1.2 %merge_2.1.summed_ref = f32[1024,128]{1,0:T(8,128)S(1)} custom-call(s32[1,8]{1,0:T(1,128)S(1)} %copy-done.1, s32[8,512]{1,0:T(8,128)S(1)} %bitcast.5, f32[1024,128]{1,0:T(8,128)S(1)} %merge_3.1.summed_ref, bf16[256,256]{1,0:T(8,128)(2,1)S(1)} %collective-permute-done.11.vectors_ref.two_ref, bf16[288,512]{1,0:T(8,128)(2,1)S(1)} %collective-permute-done.rest_6_.a_ref.rest_0_, ...), custom_call_target="tpu_custom_call" | custom-call | flops 1 | bytes 1 | tf_op jit(solution)/shard_map/merge_2/pallas_call | solution.py:305
  71.9 0.0 collective-permute-done.9.vectors_ref.one_ref
  72.0 0.0 copy-start.2
  72.0 0.0 copy-start.4
  72.0 0.0 copy-start.5
  72.0 0.0 copy-start.6
  72.0 3.8 %collective-permute-start.12 = (bf16[384,256]{1,0:T(8,128)(2,1)S(1)}, bf16[384,256]{1,0:T(8,128)(2,1)S(1)}, u32[]{:S(2)}, u32[]{:S(2)}) collective-permute-start(bf16[384,256]{1,0:T(8,128)(2,1)S(1)} %pad_maximum_fusion), channel_id=1, source_target_pairs={{0,1},{1,0},{2,3},{3,2},{4,5},{5,4},{6,7},{7,6},{8,9},{9,8},{10,11... | collective-permute-start | bytes 589832 | tf_op jit(solution)/shard_map/ppermute | solution.py:35
  75.9 1.4 %merge_next.1.summed_ref = f32[1024,128]{1,0:T(8,128)S(1)} custom-call(s32[1,8]{1,0:T(1,128)S(1)} %copy-done.1, s32[8,512]{1,0:T(8,128)S(1)} %bitcast.6, f32[1024,128]{1,0:T(8,128)S(1)} %merge_2.1.summed_ref, bf16[256,256]{1,0:T(8,128)(2,1)S(1)} %collective-permute-done.9.vectors_ref.one_ref, ...), custom_call_target="tpu_custom_call" | custom-call | flops 1000000000 | bytes 1048576 | tf_op jit(solution)/shard_map/merge_next/pallas_call | solution.py:311
  77.3 0.0 collective-permute-done.12.far_ref
  77.3 0.0 copy-done.2
  77.4 0.0 copy-done.4
  77.4 0.0 copy-done.5
  77.4 0.0 copy-done.6
  77.4 3.1 %finish.1 = (bf16[1024,128]{1,0:T(8,128)(2,1)}, f32[128,128]{1,0:T(8,128)}) custom-call(s32[48]{0:T(128)S(1)} %copy-done.6, s32[1,8]{1,0:T(1,128)S(1)} %copy-done.1, bf16[48,128,128]{2,1,0:T(8,128)(2,1)S(1)} %copy-done.2, f32[8,128]{1,0:T(8,128)S(1)} %bitcast.9, bf16[1024,128]{1,0:T(8,128)(2,1)S(1)} %copy-done.4, s32[8,512]{1,0:T(8,128)S(1)} %bitcast.7, ...), custom_call_target="tpu_custom_call" | custom-call | flops 3000000000 | bytes 1048576 | tf_op jit(solution)/shard_map/finish/pallas_call | solution.py:315
  (6 shorter events, 0.0 us)
Async XLA Ops:
  0.6 45.0 %copy-start.1 = (s32[1,8]{1,0:T(1,128)S(1)}, s32[1,8]{1,0:T(1,128)}, u32[]{:S(2)}) copy-start(s32[1,8]{1,0:T(1,128)} %adj_ref.13) | copy-start | bytes 100
  5.3 27.6 %collective-permute-start = (bf16[288,512]{1,0:T(8,128)(2,1)S(1)}, bf16[288,512]{1,0:T(8,128)(2,1)S(1)}, u32[]{:S(2)}, u32[]{:S(2)}) collective-permute-start(bf16[288,512]{1,0:T(8,128)(2,1)S(1)} %get-tuple-element.22.rest_0_), channel_id=1, source_target_pairs={{0,4},{1,5},{2,6},{3,7},{4,0},{5,1},{6,2},{7,3},{8,12},{9,13},{10,... | collective-permute-start | bytes 884744 | tf_op jit(solution)/shard_map/ppermute | solution.py:35
  10.8 24.1 %collective-permute-start.1 = (bf16[288,512]{1,0:T(8,128)(2,1)S(1)}, bf16[288,512]{1,0:T(8,128)(2,1)S(1)}, u32[]{:S(2)}, u32[]{:S(2)}) collective-permute-start(bf16[288,512]{1,0:T(8,128)(2,1)S(1)} %get-tuple-element.23.rest_1_), channel_id=1, source_target_pairs={{0,508},{1,509},{2,510},{3,511},{4,8},{5,9},{6,10},{7,11},{8,4},{9... | collective-permute-start | bytes 884744 | tf_op jit(solution)/shard_map/ppermute | solution.py:35
  24.3 16.1 %collective-permute-start.2 = (bf16[288,512]{1,0:T(8,128)(2,1)S(1)}, bf16[288,512]{1,0:T(8,128)(2,1)S(1)}, u32[]{:S(2)}, u32[]{:S(2)}) collective-permute-start(bf16[288,512]{1,0:T(8,128)(2,1)S(1)} %get-tuple-element.24.rest_2_), channel_id=1, source_target_pairs={{0,2},{1,3},{2,0},{3,1},{4,6},{5,7},{6,4},{7,5},{8,10},{9,11},{10,... | collective-permute-start | bytes 884744 | tf_op jit(solution)/shard_map/ppermute | solution.py:35
  27.4 18.2 %collective-permute-start.3 = (bf16[288,512]{1,0:T(8,128)(2,1)S(1)}, bf16[288,512]{1,0:T(8,128)(2,1)S(1)}, u32[]{:S(2)}, u32[]{:S(2)}) collective-permute-start(bf16[288,512]{1,0:T(8,128)(2,1)S(1)} %get-tuple-element.25.rest_3_), channel_id=1, source_target_pairs={{0,510},{1,511},{2,4},{3,5},{4,2},{5,3},{6,8},{7,9},{8,6},{9,7},{1... | collective-permute-start | bytes 884744 | tf_op jit(solution)/shard_map/ppermute | solution.py:35
  29.4 16.3 %collective-permute-start.4 = (bf16[288,512]{1,0:T(8,128)(2,1)S(1)}, bf16[288,512]{1,0:T(8,128)(2,1)S(1)}, u32[]{:S(2)}, u32[]{:S(2)}) collective-permute-start(bf16[288,512]{1,0:T(8,128)(2,1)S(1)} %get-tuple-element.26.rest_4_), channel_id=1, source_target_pairs={{0,511},{1,2},{2,1},{3,4},{4,3},{5,6},{6,5},{7,8},{8,7},{9,10},{10... | collective-permute-start | bytes 884744 | tf_op jit(solution)/shard_map/ppermute | solution.py:35
  32.9 12.7 %collective-permute-start.5 = (bf16[288,512]{1,0:T(8,128)(2,1)S(1)}, bf16[288,512]{1,0:T(8,128)(2,1)S(1)}, u32[]{:S(2)}, u32[]{:S(2)}) collective-permute-start(bf16[288,512]{1,0:T(8,128)(2,1)S(1)} %get-tuple-element.27.rest_5_), channel_id=1, source_target_pairs={{0,8},{1,9},{2,10},{3,11},{4,12},{5,13},{6,14},{7,15},{8,0},{9,1},... | collective-permute-start | bytes 884744 | tf_op jit(solution)/shard_map/ppermute | solution.py:35
  34.9 12.2 %collective-permute-start.6 = (bf16[288,512]{1,0:T(8,128)(2,1)S(1)}, bf16[288,512]{1,0:T(8,128)(2,1)S(1)}, u32[]{:S(2)}, u32[]{:S(2)}) collective-permute-start(bf16[288,512]{1,0:T(8,128)(2,1)S(1)} %get-tuple-element.31.rest_0_), channel_id=1, source_target_pairs={{0,504},{1,505},{2,506},{3,507},{4,508},{5,509},{6,510},{7,511},{8... | collective-permute-start | bytes 884744 | tf_op jit(solution)/shard_map/ppermute | solution.py:35
  40.4 6.7 %collective-permute-start.7 = (bf16[288,512]{1,0:T(8,128)(2,1)S(1)}, bf16[288,512]{1,0:T(8,128)(2,1)S(1)}, u32[]{:S(2)}, u32[]{:S(2)}) collective-permute-start(bf16[288,512]{1,0:T(8,128)(2,1)S(1)} %get-tuple-element.32.rest_1_), channel_id=1, source_target_pairs={{0,1},{1,0},{2,3},{3,2},{4,5},{5,4},{6,7},{7,6},{8,9},{9,8},{10,11... | collective-permute-start | bytes 884744 | tf_op jit(solution)/shard_map/ppermute | solution.py:35
  47.1 20.1 %copy-start = (s32[1,8,512]{2,1,0:T(8,128)S(1)}, s32[1,8,512]{2,1,0:T(8,128)}, u32[]{:S(2)}) copy-start(s32[1,8,512]{2,1,0:T(8,128)} %param.13) | copy-start | bytes 49156
  47.1 20.1 %copy-start.3 = (bf16[1024,128]{1,0:T(8,128)(2,1)S(1)}, bf16[1024,128]{1,0:T(8,128)(2,1)}, u32[]{:S(2)}) copy-start(bf16[1024,128]{1,0:T(8,128)(2,1)} %z_ref.1) | copy-start | bytes 786436
  48.2 8.1 %collective-permute-start.8 = (bf16[128,256]{1,0:T(8,128)(2,1)S(1)}, bf16[128,256]{1,0:T(8,128)(2,1)S(1)}, u32[]{:S(2)}, u32[]{:S(2)}) collective-permute-start(bf16[128,256]{1,0:T(8,128)(2,1)S(1)} %get-tuple-element.35.send_ref), channel_id=1, source_target_pairs={{0,1},{1,0},{2,3},{3,2},{4,5},{5,4},{6,7},{7,6},{8,9},{9,8},{10,11... | collective-permute-start | bytes 196616 | tf_op jit(solution)/shard_map/ppermute | solution.py:35
  56.3 12.2 %collective-permute-start.10 = (bf16[256,256]{1,0:T(8,128)(2,1)S(1)}, bf16[256,256]{1,0:T(8,128)(2,1)S(1)}, u32[]{:S(2)}, u32[]{:S(2)}) collective-permute-start(bf16[256,256]{1,0:T(8,128)(2,1)S(1)} %constant_dynamic-update-slice_fusion), channel_id=1, source_target_pairs={{0,8},{1,505},{2,10},{3,507},{4,12},{5,509},{6,14},{7,511},{8,16},... | collective-permute-start | bytes 393224 | tf_op jit(solution)/shard_map/ppermute | solution.py:35
  60.4 10.4 %collective-permute-start.11 = (bf16[256,256]{1,0:T(8,128)(2,1)S(1)}, bf16[256,256]{1,0:T(8,128)(2,1)S(1)}, u32[]{:S(2)}, u32[]{:S(2)}) collective-permute-start(bf16[256,256]{1,0:T(8,128)(2,1)S(1)} %constant_dynamic-update-slice_fusion), channel_id=1, source_target_pairs={{0,4},{1,509},{2,6},{3,511},{4,8},{5,1},{6,10},{7,3},{8,12},{9,5},... | collective-permute-start | bytes 393224 | tf_op jit(solution)/shard_map/ppermute | solution.py:35
  65.3 6.6 %collective-permute-start.9 = (bf16[256,256]{1,0:T(8,128)(2,1)S(1)}, bf16[256,256]{1,0:T(8,128)(2,1)S(1)}, u32[]{:S(2)}, u32[]{:S(2)}) collective-permute-start(bf16[256,256]{1,0:T(8,128)(2,1)S(1)} %constant_dynamic-update-slice_fusion), channel_id=1, source_target_pairs={{0,2},{1,511},{2,4},{3,1},{4,6},{5,3},{6,8},{7,5},{8,10},{9,7},{10... | collective-permute-start | bytes 393224 | tf_op jit(solution)/shard_map/ppermute | solution.py:35
  72.0 5.3 %copy-start.2 = (bf16[48,128,128]{2,1,0:T(8,128)(2,1)S(1)}, bf16[48,128,128]{2,1,0:T(8,128)(2,1)}, u32[]{:S(2)}) copy-start(bf16[48,128,128]{2,1,0:T(8,128)(2,1)} %tiles_ref.1) | copy-start | bytes 4718596
  72.0 5.3 %copy-start.4 = (bf16[1024,128]{1,0:T(8,128)(2,1)S(1)}, bf16[1024,128]{1,0:T(8,128)(2,1)}, u32[]{:S(2)}) copy-start(bf16[1024,128]{1,0:T(8,128)(2,1)} %rhs_ref.1) | copy-start | bytes 786436
  72.0 5.3 %copy-start.5 = (f32[1024]{0:T(1024)S(1)}, f32[1024]{0:T(1024)}, u32[]{:S(2)}) copy-start(f32[1024]{0:T(1024)} %param.10) | copy-start | bytes 12292
  72.0 5.3 %copy-start.6 = (s32[48]{0:T(128)S(1)}, s32[48]{0:T(128)}, u32[]{:S(2)}) copy-start(s32[48]{0:T(128)} %cols_ref.1) | copy-start | bytes 580
  72.0 5.3 %collective-permute-start.12 = (bf16[384,256]{1,0:T(8,128)(2,1)S(1)}, bf16[384,256]{1,0:T(8,128)(2,1)S(1)}, u32[]{:S(2)}, u32[]{:S(2)}) collective-permute-start(bf16[384,256]{1,0:T(8,128)(2,1)S(1)} %pad_maximum_fusion), channel_id=1, source_target_pairs={{0,1},{1,0},{2,3},{3,2},{4,5},{5,4},{6,7},{7,6},{8,9},{9,8},{10,11... | collective-permute-start | bytes 589832 | tf_op jit(solution)/shard_map/ppermute | solution.py:35

commit v5 on v4

--- a/solution.py
+++ b/solution.py
@@ -28,6 +28,10 @@
 EARLY = 6
 INSIDE = STEPS.index((0, 0))
 ACROSS = STEPS.index((0, 1))
+NEAR_2 = STEPS.index((1, 0))
+FAR_2 = STEPS.index((1, 1))
+REST = tuple(i for i in range(8) if i not in (INSIDE, ACROSS))
+ROWS = 2 * K + TAIL
 
 
 def permute(block, target):
@@ -54,11 +58,12 @@
 
 def slot_of(step, me):
     power, colour = STEPS[step]
-    return power + 4 * (bit(me, power) if colour == 0 else 1 - bit(me, power))
+    side = 1 - bit(me, 0) if power == 1 else bit(me, power)
+    return power + 4 * (side if colour == 0 else 1 - side)
 
 
 def near_step_is_first(power, me):
-    return bit(me, power) != bit(me, 0)
+    return power == 1 or bit(me, power) != bit(me, 0)
 
 
 def split(x):
@@ -86,8 +91,8 @@
 
 
 def prepare(cols_in, z_in, tiles_in, diag_in, rhs_in, margin_in, *rest):
-    payloads, (own_ref, coarse_ref) = rest[:8], rest[8:10]
-    cols_ref, z_ref, tiles_ref, diag_ref, rhs_ref, margin_ref, zit, images, sems = rest[10:]
+    inside_ref, own_ref, coarse_ref, zit = rest[:4]
+    cols_ref, z_ref, tiles_ref, diag_ref, rhs_ref, margin_ref, images, sems = rest[4:]
     me = lax.axis_index("sub")
     pairs = [(z_in, z_ref), (rhs_in, rhs_ref), (cols_in, cols_ref), (diag_in, diag_ref)]
     pairs += [(tiles_in.at[pl.ds(TPR * b, TPR)], tiles_ref.at[pl.ds(TPR * b, TPR)]) for b in range(NB)]
@@ -112,12 +117,23 @@
         image = (column(diag_ref, b) * z.astype(F32) + tile_row(cols_ref, tiles_ref, z_ref, b)).astype(BF16)
         zit[K:, rows] = image.T
         images[rows, :] = image
-    for step, out in enumerate(payloads):
-        onehot = picks(margin_ref, slot_of(step, me))
-        out[: 2 * K, :] = jnp.dot(zit[...], onehot, preferred_element_type=F32).astype(BF16)
-        for q in range(OV // K):
-            out[2 * K :, q * K : (q + 1) * K] = first[q * TAIL : (q + 1) * TAIL, :]
+    for i, step in enumerate((INSIDE, ACROSS)):
+        gather(inside_ref, i * ROWS, zit, margin_ref, slot_of(step, me), first)
     own_ref[...] = jnp.dot(zit[:K, :], images[...], preferred_element_type=F32)
+
+
+def gather(out, at, zit, margin_ref, slot, first):
+    rows = jnp.dot(zit[...], picks(margin_ref, slot), preferred_element_type=F32).astype(BF16)
+    out[at : at + 2 * K, :] = rows
+    for q in range(OV // K):
+        out[at + 2 * K : at + ROWS, q * K : (q + 1) * K] = first[q * TAIL : (q + 1) * TAIL, :]
+
+
+def prepare_rest(margin_ref, zit, coarse_ref, *payloads):
+    me = lax.axis_index("sub")
+    first = (coarse_ref[...] / CHEB_CENTER).astype(BF16)
+    for step, out in zip(REST, payloads):
+        gather(out, 0, zit, margin_ref, slot_of(step, me), first)
 
 
 dot = functools.partial(jnp.dot, preferred_element_type=F32)
@@ -191,6 +207,8 @@
 def pick_basis(power, a_ref, b_ref, near, me):
     a, b = STEPS.index((power, 0)), STEPS.index((power, 1))
     take_a = near_step_is_first(power, me) == near
+    if isinstance(take_a, bool):
+        return (a_ref if take_a else b_ref)[:K, :], slot_of(a if take_a else b, me), a if take_a else b
     slot = jnp.where(take_a, slot_of(a, me), slot_of(b, me))
     return jnp.where(take_a, a_ref[:K, :], b_ref[:K, :]), slot, jnp.where(take_a, a, b)
 
@@ -257,11 +275,11 @@
 def per_device(deflation, op_tiles, tile_cols, diag_coef, fine_rhs, adjacency, margin_rows):
     diag = diag_coef.reshape(NB, BLK)
     margin = margin_rows[0]
-    *payloads, own, coarse = call(
+    sent_inside, own, coarse, zit = call(
         prepare,
         "prepare",
         [HBM] * 6,
-        [arr((2 * K + TAIL, OV), BF16)] * 8 + [arr((K, K), F32)] * 2,
+        [arr((2 * ROWS, OV), BF16)] + [arr((K, K), F32)] * 2 + [arr((2 * K, NLOC), BF16)],
         [
             pltpu.SMEM((TPR * NB,), jnp.int32),
             pltpu.VMEM((NLOC, K), BF16),
@@ -269,13 +287,32 @@
             pltpu.VMEM((NB, BLK), F32),
             pltpu.VMEM((NLOC, K), BF16),
             pltpu.VMEM((8, OV), jnp.int32),
-            pltpu.VMEM((2 * K, NLOC), BF16),
             pltpu.VMEM((NLOC, K), BF16),
             pltpu.SemaphoreType.DMA((NB + 5,)),
         ],
         3 * 10**9,
     )(*(pltpu.with_memory_space_constraint(x, pltpu.HBM) for x in (tile_cols, deflation, op_tiles, diag, fine_rhs, margin)))
-    theirs = [swapped(block, *step) for block, step in zip(payloads, STEPS)]
+    others = call(
+        prepare_rest,
+        "prepare_rest",
+        [VMEM] * 3,
+        [arr((ROWS, OV), BF16)] * len(REST),
+        [],
+        8 * 10**9,
+    )(margin, zit, coarse)
+    payloads = [None] * 8
+    for step, block in zip(REST, others):
+        payloads[step] = block
+    payloads[INSIDE], payloads[ACROSS] = sent_inside[:ROWS], sent_inside[ROWS:]
+    theirs = [None] * 8
+    inside = core_swap(sent_inside)
+    theirs[STEPS.index((2, 0))] = swapped(payloads[STEPS.index((2, 0))], 2, 0)
+    theirs[STEPS.index((2, 1))] = swapped(payloads[STEPS.index((2, 1))], 2, 1)
+    forth = both_ways(jnp.concatenate([payloads[FAR_2], inside[ROWS:]]), 1)
+    theirs[FAR_2] = both_ways(payloads[NEAR_2], -1)
+    theirs[STEPS.index((3, 0))] = swapped(payloads[STEPS.index((3, 0))], 3, 0)
+    theirs[STEPS.index((3, 1))] = swapped(payloads[STEPS.index((3, 1))], 3, 1)
+    theirs[INSIDE], theirs[NEAR_2], theirs[ACROSS] = inside[:ROWS], forth[:ROWS], forth[ROWS:]
     early = (EARLY + 1) * K
     ehi_early, elo_early, image = call(
         iterate_early,

time: 81 us -> 80.2 us (level)
  starting transfers between devices: 62.1 us -> 53.2 us
  waiting for transfers between devices: 2.02 us -> 9.91 us
    ppermute x13 -> x12, starting transfers between devices: 62.1 us -> 53.2 us  [permute(): return lax.ppermute(block, 'sub', [(i, target(i) % n) for i in range(n)])]
    ppermute x13 -> x12, waiting for transfers between devices: 2.02 us -> 9.91 us  [permute(): return lax.ppermute(block, 'sub', [(i, target(i) % n) for i in range(n)])]
    pallas_call x1 -> x2, Pallas kernels: 4.64 us -> 4.83 us  [the longest x1 2.91 us: per_device(): call(prepare, 'prepare', [HBM] * 6, [arr((2 * ROWS, OV), BF16)] + [arr((K...]
  transfers between devices with their start and end apart: 13 -> 12, of which waited for: 2 -> 5; matrix products, arithmetic and copies ran while one was open for 0% -> 0% of each run, Pallas kernels for 8% -> 10%
where the time goes in v5:
time: 80.2 us; the launch traced here: 79.7 us
  starting transfers between devices  53.2 us (66%)
  Pallas kernels  15.4 us (19%)
  waiting for transfers between devices  9.91 us (12%)
  between operations  0.98 us (1%)
    ppermute x12, starting transfers between devices, permute(): return lax.ppermute(block, 'sub', [(i, target(i) % n) for i in range(n)])  53.2 us
    ppermute x12, waiting for transfers between devices, permute(): return lax.ppermute(block, 'sub', [(i, target(i) % n) for i in range(n)])  9.91 us
    pallas_call x1, Pallas kernels, per_device(): call(finish, 'finish', [SMEM] * 2 + [VMEM] * 24, [arr((NLOC, K), BF16), a...  3.11 us
    pallas_call x1, Pallas kernels, per_device(): call(prepare, 'prepare', [HBM] * 6, [arr((2 * ROWS, OV), BF16)] + [arr((K...  2.91 us
    pallas_call x2, Pallas kernels, per_device(): call(functools.partial(merge_near, power), f'merge_{power}', [SMEM] + [VM...  2.31 us
    pallas_call x1, Pallas kernels, per_device(): call(prepare_rest, 'prepare_rest', [VMEM] * 3, [arr((ROWS, OV), BF16)] *...  1.92 us
  transfers between devices with their start and end apart: 12, of which 5 were waited for; matrix products, arithmetic and copies ran while one was open for 0% of the time, Pallas kernels for 10%

profile of v5, /device:TPU:1, one launch (start us, length us, event | category | flops | bytes accessed | tf_op | source)
XLA Modules:
  0.0 79.7 jit_solution(11292577826337548664)
XLA Ops:
  0.6 0.0 copy-start
  0.6 2.9 %prepare.1 = (bf16[576,512]{1,0:T(8,128)(2,1)S(1)}, f32[128,128]{1,0:T(8,128)S(1)}, f32[128,128]{1,0:T(8,128)S(1)}, bf16[256,1024]{1,0:T(8,128)(2,1)S(1)}) custom-call(s32[48]{0:T(128)} %cols_ref.1, bf16[1024,128]{1,0:T(8,128)(2,1)} %z_ref.1, bf16[48,128,128]{2,1,0:T(8,128)(2,1)} %tiles_ref.1, f32[8,128]{1,0:T(8,128)} %bitcast.9, bf16[1024,128]{1,0:T(8,128)(2,1)} %rhs_ref.1, ...), custom_call_target="tpu_custom_call" | custom-call | flops 3000000000 | bytes 1048576 | tf_op jit(solution)/shard_map/prepare/pallas_call | solution.py:278
  3.6 8.8 %collective-permute-start.2 = (bf16[576,512]{1,0:T(8,128)(2,1)S(1)}, bf16[576,512]{1,0:T(8,128)(2,1)S(1)}, u32[]{:S(2)}, u32[]{:S(2)}) collective-permute-start(bf16[576,512]{1,0:T(8,128)(2,1)S(1)} %get-tuple-element.27), channel_id=1, source_target_pairs={{0,1},{1,0},{2,3},{3,2},{4,5},{5,4},{6,7},{7,6},{8,9},{9,8},{10,11... | collective-permute-start | bytes 1769480 | tf_op jit(solution)/shard_map/ppermute | solution.py:39
  12.3 0.0 copy-done
  12.4 1.9 %prepare_rest.1 = (bf16[288,512]{1,0:T(8,128)(2,1)S(1)}, bf16[288,512]{1,0:T(8,128)(2,1)S(1)}, bf16[288,512]{1,0:T(8,128)(2,1)S(1)}, bf16[288,512]{1,0:T(8,128)(...) custom-call(s32[8,512]{1,0:T(8,128)S(1)} %bitcast.3, bf16[256,1024]{1,0:T(8,128)(2,1)S(1)} %get-tuple-element.22.zit, ...), custom_call_target="tpu_custom_call" | custom-call | flops 8000000000 | bytes 1048576 | tf_op jit(solution)/shard_map/prepare_rest/pallas_call | solution.py:295
  14.3 0.0 collective-permute-done.2
  14.4 10.4 %collective-permute-start.3 = (bf16[576,512]{1,0:T(8,128)(2,1)S(1)}, bf16[576,512]{1,0:T(8,128)(2,1)S(1)}, u32[]{:S(2)}, u32[]{:S(2)}) collective-permute-start(bf16[576,512]{1,0:T(8,128)(2,1)S(1)} %pad_maximum_fusion), channel_id=1, source_target_pairs={{0,2},{1,511},{2,4},{3,1},{4,6},{5,3},{6,8},{7,5},{8,10},{9,7},{10... | collective-permute-start | bytes 1769480 | tf_op jit(solution)/shard_map/ppermute | solution.py:39
  24.8 1.9 %collective-permute-start = (bf16[288,512]{1,0:T(8,128)(2,1)S(1)}, bf16[288,512]{1,0:T(8,128)(2,1)S(1)}, u32[]{:S(2)}, u32[]{:S(2)}) collective-permute-start(bf16[288,512]{1,0:T(8,128)(2,1)S(1)} %get-tuple-element.23.rest_0_), channel_id=1, source_target_pairs={{0,4},{1,5},{2,6},{3,7},{4,0},{5,1},{6,2},{7,3},{8,12},{9,13},{10,... | collective-permute-start | bytes 884744 | tf_op jit(solution)/shard_map/ppermute | solution.py:39
  26.7 5.7 %collective-permute-start.1 = (bf16[288,512]{1,0:T(8,128)(2,1)S(1)}, bf16[288,512]{1,0:T(8,128)(2,1)S(1)}, u32[]{:S(2)}, u32[]{:S(2)}) collective-permute-start(bf16[288,512]{1,0:T(8,128)(2,1)S(1)} %get-tuple-element.24.rest_1_), channel_id=1, source_target_pairs={{0,508},{1,509},{2,510},{3,511},{4,8},{5,9},{6,10},{7,11},{8,4},{9... | collective-permute-start | bytes 884744 | tf_op jit(solution)/shard_map/ppermute | solution.py:39
  32.4 1.9 %collective-permute-start.4 = (bf16[288,512]{1,0:T(8,128)(2,1)S(1)}, bf16[288,512]{1,0:T(8,128)(2,1)S(1)}, u32[]{:S(2)}, u32[]{:S(2)}) collective-permute-start(bf16[288,512]{1,0:T(8,128)(2,1)S(1)} %get-tuple-element.25.rest_2_), channel_id=1, source_target_pairs={{0,510},{1,3},{2,0},{3,5},{4,2},{5,7},{6,4},{7,9},{8,6},{9,11},{10... | collective-permute-start | bytes 884744 | tf_op jit(solution)/shard_map/ppermute | solution.py:39
  34.3 0.0 copy-start.1
  34.3 2.3 %collective-permute-start.5 = (bf16[288,512]{1,0:T(8,128)(2,1)S(1)}, bf16[288,512]{1,0:T(8,128)(2,1)S(1)}, u32[]{:S(2)}, u32[]{:S(2)}) collective-permute-start(bf16[288,512]{1,0:T(8,128)(2,1)S(1)} %get-tuple-element.28.rest_5_), channel_id=1, source_target_pairs={{0,8},{1,9},{2,10},{3,11},{4,12},{5,13},{6,14},{7,15},{8,0},{9,1},... | collective-permute-start | bytes 884744 | tf_op jit(solution)/shard_map/ppermute | solution.py:39
  36.7 0.0 collective-permute-done.3
  36.7 3.6 %collective-permute-start.6 = (bf16[288,512]{1,0:T(8,128)(2,1)S(1)}, bf16[288,512]{1,0:T(8,128)(2,1)S(1)}, u32[]{:S(2)}, u32[]{:S(2)}) collective-permute-start(bf16[288,512]{1,0:T(8,128)(2,1)S(1)} %get-tuple-element.32.rest_0_), channel_id=1, source_target_pairs={{0,504},{1,505},{2,506},{3,507},{4,508},{5,509},{6,510},{7,511},{8... | collective-permute-start | bytes 884744 | tf_op jit(solution)/shard_map/ppermute | solution.py:39
  40.4 1.3 %collective-permute-done.rest_6_.a_ref.rest_0_ = bf16[288,512]{1,0:T(8,128)(2,1)S(1)} collective-permute-done((bf16[288,512]{1,0:T(8,128)(2,1)S(1)}, bf16[288,512]{1,0:T(8,128)(2,1)S(1)}, u32[]{:S(2)}, u32[]{:S(2)}) %collective-permute-start) | collective-permute-done | bytes 294944 | tf_op jit(solution)/shard_map/ppermute | solution.py:39
  41.7 0.0 collective-permute-done.1.rest_7_.b_ref.rest_1_
  41.7 3.5 %collective-permute-done.4.rest_9_.b_ref.rest_3_ = bf16[288,512]{1,0:T(8,128)(2,1)S(1)} collective-permute-done((bf16[288,512]{1,0:T(8,128)(2,1)S(1)}, bf16[288,512]{1,0:T(8,128)(2,1)S(1)}, u32[]{:S(2)}, u32[]{:S(2)}) %collective-permute-start.4) | collective-permute-done | bytes 294944 | tf_op jit(solution)/shard_map/ppermute | solution.py:39
  45.3 0.0 collective-permute-done.5.rest_11_.a_ref.rest_5_
  45.3 0.0 copy-done.1
  45.3 1.4 %iterate_early.1 = (bf16[128,896]{1,0:T(8,128)(2,1)S(1)}, bf16[128,896]{1,0:T(8,128)(2,1)S(1)}, f32[128,128]{1,0:T(8,128)S(1)}) custom-call(s32[1,8]{1,0:T(1,128)S(1)} %copy-done.1, f32[128,128]{1,0:T(8,128)S(1)} %get-tuple-element.21.own_ref, f32[128,128]{1,0:T(8,128)S(1)} %get-tuple-element.20.coarse_ref, bf16[288,512]{1,0:T(8,128)(2,1)S(1)} %get-tuple-element.23.rest_0_, ...), custom_call_target="tpu_custom_call" | custom-call | flops 1000000000 | bytes 1048576 | tf_op jit(solution)/shard_map/iterate_early/pallas_call | solution.py:317
  46.7 3.4 %collective-permute-done.6.rest_2_.b_ref.rest_6_ = bf16[288,512]{1,0:T(8,128)(2,1)S(1)} collective-permute-done((bf16[288,512]{1,0:T(8,128)(2,1)S(1)}, bf16[288,512]{1,0:T(8,128)(2,1)S(1)}, u32[]{:S(2)}, u32[]{:S(2)}) %collective-permute-start.6) | collective-permute-done | bytes 294944 | tf_op jit(solution)/shard_map/ppermute | solution.py:39
  50.2 0.0 copy-start.3
  50.2 1.0 %iterate.1 = (bf16[128,256]{1,0:T(8,128)(2,1)S(1)}, bf16[128,256]{1,0:T(8,128)(2,1)S(1)}, bf16[128,256]{1,0:T(8,128)(2,1)S(1)}) custom-call(s32[1,8]{1,0:T(1,128)S(1)} %copy-done.1, f32[128,128]{1,0:T(8,128)S(1)} %get-tuple-element.20.coarse_ref, f32[128,128]{1,0:T(8,128)S(1)} %get-tuple-element.31.image_ref, ...), custom_call_target="tpu_custom_call" | custom-call | flops 1000000000 | bytes 1048576 | tf_op jit(solution)/shard_map/iterate/pallas_call | solution.py:326
  51.2 2.2 %collective-permute-start.7 = (bf16[128,256]{1,0:T(8,128)(2,1)S(1)}, bf16[128,256]{1,0:T(8,128)(2,1)S(1)}, u32[]{:S(2)}, u32[]{:S(2)}) collective-permute-start(bf16[128,256]{1,0:T(8,128)(2,1)S(1)} %get-tuple-element.35.send_ref), channel_id=1, source_target_pairs={{0,1},{1,0},{2,3},{3,2},{4,5},{5,4},{6,7},{7,6},{8,9},{9,8},{10,11... | collective-permute-start | bytes 196616 | tf_op jit(solution)/shard_map/ppermute | solution.py:39
  53.4 0.9 %collective-permute-done.7.other_ref = bf16[128,256]{1,0:T(8,128)(2,1)S(1)} collective-permute-done((bf16[128,256]{1,0:T(8,128)(2,1)S(1)}, bf16[128,256]{1,0:T(8,128)(2,1)S(1)}, u32[]{:S(2)}, u32[]{:S(2)}) %collective-permute-start.7) | collective-permute-done | bytes 65568 | tf_op jit(solution)/shard_map/ppermute | solution.py:39
  54.4 6.7 %collective-permute-start.9 = (bf16[256,256]{1,0:T(8,128)(2,1)S(1)}, bf16[256,256]{1,0:T(8,128)(2,1)S(1)}, u32[]{:S(2)}, u32[]{:S(2)}) collective-permute-start(bf16[256,256]{1,0:T(8,128)(2,1)S(1)} %constant_dynamic-update-slice_fusion), channel_id=1, source_target_pairs={{0,8},{1,505},{2,10},{3,507},{4,12},{5,509},{6,14},{7,511},{8,16},... | collective-permute-start | bytes 393224 | tf_op jit(solution)/shard_map/ppermute | solution.py:39
  61.1 3.4 %collective-permute-start.10 = (bf16[256,256]{1,0:T(8,128)(2,1)S(1)}, bf16[256,256]{1,0:T(8,128)(2,1)S(1)}, u32[]{:S(2)}, u32[]{:S(2)}) collective-permute-start(bf16[256,256]{1,0:T(8,128)(2,1)S(1)} %constant_dynamic-update-slice_fusion), channel_id=1, source_target_pairs={{0,4},{1,509},{2,6},{3,511},{4,8},{5,1},{6,10},{7,3},{8,12},{9,5},... | collective-permute-start | bytes 393224 | tf_op jit(solution)/shard_map/ppermute | solution.py:39
  64.5 2.9 %collective-permute-start.8 = (bf16[256,256]{1,0:T(8,128)(2,1)S(1)}, bf16[256,256]{1,0:T(8,128)(2,1)S(1)}, u32[]{:S(2)}, u32[]{:S(2)}) collective-permute-start(bf16[256,256]{1,0:T(8,128)(2,1)S(1)} %constant_dynamic-update-slice_fusion), channel_id=1, source_target_pairs={{0,2},{1,511},{2,4},{3,1},{4,6},{5,3},{6,8},{7,5},{8,10},{9,7},{10... | collective-permute-start | bytes 393224 | tf_op jit(solution)/shard_map/ppermute | solution.py:39
  67.5 0.0 copy-done.3
  67.5 1.2 %merge_chip.1.summed_ref = f32[1024,128]{1,0:T(8,128)S(1)} custom-call(s32[1,8]{1,0:T(1,128)S(1)} %copy-done.1, bf16[1024,128]{1,0:T(8,128)(2,1)S(1)} %copy-done.3, s32[8,512]{1,0:T(8,128)S(1)} %bitcast.4, bf16[128,256]{1,0:T(8,128)(2,1)S(1)} %get-tuple-element.35.send_ref, bf16[128,256]{1,0:T(8,128)(2,1)S(1)} %collective-permute-done.7.other_ref, ...), custom_call_target="tpu_custom_call" | custom-call | flops 1000000000 | bytes 1048576 | tf_op jit(solution)/shard_map/merge_chip/pallas_call | solution.py:337
  68.7 0.0 collective-permute-done.9.vectors_ref.four_ref
  68.7 1.2 %merge_3.1.summed_ref = f32[1024,128]{1,0:T(8,128)S(1)} custom-call(s32[1,8]{1,0:T(1,128)S(1)} %copy-done.1, s32[8,512]{1,0:T(8,128)S(1)} %bitcast.5, f32[1024,128]{1,0:T(8,128)S(1)} %merge_chip.1.summed_ref, bf16[256,256]{1,0:T(8,128)(2,1)S(1)} %collective-permute-done.9.vectors_ref.four_ref, ...), custom_call_target="tpu_custom_call" | custom-call | flops 1 | bytes 1 | tf_op jit(solution)/shard_map/merge_3/pallas_call | solution.py:342
  69.8 0.6 collective-permute-done.10.vectors_ref.two_ref
  70.5 1.2 %merge_2.1.summed_ref = f32[1024,128]{1,0:T(8,128)S(1)} custom-call(s32[1,8]{1,0:T(1,128)S(1)} %copy-done.1, s32[8,512]{1,0:T(8,128)S(1)} %bitcast.6, f32[1024,128]{1,0:T(8,128)S(1)} %merge_3.1.summed_ref, bf16[256,256]{1,0:T(8,128)(2,1)S(1)} %collective-permute-done.10.vectors_ref.two_ref, bf16[288,512]{1,0:T(8,128)(2,1)S(1)} %collective-permute-done.rest_6_.a_ref.rest_0_, ...), custom_call_target="tpu_custom_call" | custom-call | flops 1 | bytes 1 | tf_op jit(solution)/shard_map/merge_2/pallas_call | solution.py:342
  71.6 0.0 collective-permute-done.8.vectors_ref.one_ref
  71.7 0.0 copy-start.2
  71.7 0.0 copy-start.4
  71.7 0.0 copy-start.5
  71.7 0.0 copy-start.6
  71.8 3.3 %collective-permute-start.11 = (bf16[384,256]{1,0:T(8,128)(2,1)S(1)}, bf16[384,256]{1,0:T(8,128)(2,1)S(1)}, u32[]{:S(2)}, u32[]{:S(2)}) collective-permute-start(bf16[384,256]{1,0:T(8,128)(2,1)S(1)} %pad_maximum_fusion.1), channel_id=1, source_target_pairs={{0,1},{1,0},{2,3},{3,2},{4,5},{5,4},{6,7},{7,6},{8,9},{9,8},{10,11... | collective-permute-start | bytes 589832 | tf_op jit(solution)/shard_map/ppermute | solution.py:39
  75.1 1.4 %merge_next.1.summed_ref = f32[1024,128]{1,0:T(8,128)S(1)} custom-call(s32[1,8]{1,0:T(1,128)S(1)} %copy-done.1, s32[8,512]{1,0:T(8,128)S(1)} %bitcast.7, f32[1024,128]{1,0:T(8,128)S(1)} %merge_2.1.summed_ref, bf16[256,256]{1,0:T(8,128)(2,1)S(1)} %collective-permute-done.8.vectors_ref.one_ref, ...), custom_call_target="tpu_custom_call" | custom-call | flops 1000000000 | bytes 1048576 | tf_op jit(solution)/shard_map/merge_next/pallas_call | solution.py:348
  76.5 0.0 collective-permute-done.11.far_ref
  76.5 0.0 copy-done.2
  76.6 0.0 copy-done.4
  76.6 0.0 copy-done.5
  76.6 0.0 copy-done.6
  76.6 3.1 %finish.1 = (bf16[1024,128]{1,0:T(8,128)(2,1)}, f32[128,128]{1,0:T(8,128)}) custom-call(s32[48]{0:T(128)S(1)} %copy-done.6, s32[1,8]{1,0:T(1,128)S(1)} %copy-done.1, bf16[48,128,128]{2,1,0:T(8,128)(2,1)S(1)} %copy-done.2, f32[8,128]{1,0:T(8,128)S(1)} %bitcast.10, bf16[1024,128]{1,0:T(8,128)(2,1)S(1)} %copy-done.4, s32[8,512]{1,0:T(8,128)S(1)} %bitcast.8, ...), custom_call_target="tpu_custom_call" | custom-call | flops 3000000000 | bytes 1048576 | tf_op jit(solution)/shard_map/finish/pallas_call | solution.py:352
  (10 shorter events, 0.2 us)
Async XLA Ops:
  0.6 11.7 %copy-start = (s32[1,8,512]{2,1,0:T(8,128)S(1)}, s32[1,8,512]{2,1,0:T(8,128)}, u32[]{:S(2)}) copy-start(s32[1,8,512]{2,1,0:T(8,128)} %param.13) | copy-start | bytes 49156
  3.6 10.7 %collective-permute-start.2 = (bf16[576,512]{1,0:T(8,128)(2,1)S(1)}, bf16[576,512]{1,0:T(8,128)(2,1)S(1)}, u32[]{:S(2)}, u32[]{:S(2)}) collective-permute-start(bf16[576,512]{1,0:T(8,128)(2,1)S(1)} %get-tuple-element.27), channel_id=1, source_target_pairs={{0,1},{1,0},{2,3},{3,2},{4,5},{5,4},{6,7},{7,6},{8,9},{9,8},{10,11... | collective-permute-start | bytes 1769480 | tf_op jit(solution)/shard_map/ppermute | solution.py:39
  14.4 22.3 %collective-permute-start.3 = (bf16[576,512]{1,0:T(8,128)(2,1)S(1)}, bf16[576,512]{1,0:T(8,128)(2,1)S(1)}, u32[]{:S(2)}, u32[]{:S(2)}) collective-permute-start(bf16[576,512]{1,0:T(8,128)(2,1)S(1)} %pad_maximum_fusion), channel_id=1, source_target_pairs={{0,2},{1,511},{2,4},{3,1},{4,6},{5,3},{6,8},{7,5},{8,10},{9,7},{10... | collective-permute-start | bytes 1769480 | tf_op jit(solution)/shard_map/ppermute | solution.py:39
  24.8 16.9 %collective-permute-start = (bf16[288,512]{1,0:T(8,128)(2,1)S(1)}, bf16[288,512]{1,0:T(8,128)(2,1)S(1)}, u32[]{:S(2)}, u32[]{:S(2)}) collective-permute-start(bf16[288,512]{1,0:T(8,128)(2,1)S(1)} %get-tuple-element.23.rest_0_), channel_id=1, source_target_pairs={{0,4},{1,5},{2,6},{3,7},{4,0},{5,1},{6,2},{7,3},{8,12},{9,13},{10,... | collective-permute-start | bytes 884744 | tf_op jit(solution)/shard_map/ppermute | solution.py:39
  26.7 15.0 %collective-permute-start.1 = (bf16[288,512]{1,0:T(8,128)(2,1)S(1)}, bf16[288,512]{1,0:T(8,128)(2,1)S(1)}, u32[]{:S(2)}, u32[]{:S(2)}) collective-permute-start(bf16[288,512]{1,0:T(8,128)(2,1)S(1)} %get-tuple-element.24.rest_1_), channel_id=1, source_target_pairs={{0,508},{1,509},{2,510},{3,511},{4,8},{5,9},{6,10},{7,11},{8,4},{9... | collective-permute-start | bytes 884744 | tf_op jit(solution)/shard_map/ppermute | solution.py:39
  32.4 12.9 %collective-permute-start.4 = (bf16[288,512]{1,0:T(8,128)(2,1)S(1)}, bf16[288,512]{1,0:T(8,128)(2,1)S(1)}, u32[]{:S(2)}, u32[]{:S(2)}) collective-permute-start(bf16[288,512]{1,0:T(8,128)(2,1)S(1)} %get-tuple-element.25.rest_2_), channel_id=1, source_target_pairs={{0,510},{1,3},{2,0},{3,5},{4,2},{5,7},{6,4},{7,9},{8,6},{9,11},{10... | collective-permute-start | bytes 884744 | tf_op jit(solution)/shard_map/ppermute | solution.py:39
  34.3 11.0 %copy-start.1 = (s32[1,8]{1,0:T(1,128)S(1)}, s32[1,8]{1,0:T(1,128)}, u32[]{:S(2)}) copy-start(s32[1,8]{1,0:T(1,128)} %adj_ref.13) | copy-start | bytes 100
  34.3 11.0 %collective-permute-start.5 = (bf16[288,512]{1,0:T(8,128)(2,1)S(1)}, bf16[288,512]{1,0:T(8,128)(2,1)S(1)}, u32[]{:S(2)}, u32[]{:S(2)}) collective-permute-start(bf16[288,512]{1,0:T(8,128)(2,1)S(1)} %get-tuple-element.28.rest_5_), channel_id=1, source_target_pairs={{0,8},{1,9},{2,10},{3,11},{4,12},{5,13},{6,14},{7,15},{8,0},{9,1},... | collective-permute-start | bytes 884744 | tf_op jit(solution)/shard_map/ppermute | solution.py:39
  36.7 13.5 %collective-permute-start.6 = (bf16[288,512]{1,0:T(8,128)(2,1)S(1)}, bf16[288,512]{1,0:T(8,128)(2,1)S(1)}, u32[]{:S(2)}, u32[]{:S(2)}) collective-permute-start(bf16[288,512]{1,0:T(8,128)(2,1)S(1)} %get-tuple-element.32.rest_0_), channel_id=1, source_target_pairs={{0,504},{1,505},{2,506},{3,507},{4,508},{5,509},{6,510},{7,511},{8... | collective-permute-start | bytes 884744 | tf_op jit(solution)/shard_map/ppermute | solution.py:39
  50.2 17.3 %copy-start.3 = (bf16[1024,128]{1,0:T(8,128)(2,1)S(1)}, bf16[1024,128]{1,0:T(8,128)(2,1)}, u32[]{:S(2)}) copy-start(bf16[1024,128]{1,0:T(8,128)(2,1)} %z_ref.1) | copy-start | bytes 786436
  51.2 3.1 %collective-permute-start.7 = (bf16[128,256]{1,0:T(8,128)(2,1)S(1)}, bf16[128,256]{1,0:T(8,128)(2,1)S(1)}, u32[]{:S(2)}, u32[]{:S(2)}) collective-permute-start(bf16[128,256]{1,0:T(8,128)(2,1)S(1)} %get-tuple-element.35.send_ref), channel_id=1, source_target_pairs={{0,1},{1,0},{2,3},{3,2},{4,5},{5,4},{6,7},{7,6},{8,9},{9,8},{10,11... | collective-permute-start | bytes 196616 | tf_op jit(solution)/shard_map/ppermute | solution.py:39
  54.4 14.3 %collective-permute-start.9 = (bf16[256,256]{1,0:T(8,128)(2,1)S(1)}, bf16[256,256]{1,0:T(8,128)(2,1)S(1)}, u32[]{:S(2)}, u32[]{:S(2)}) collective-permute-start(bf16[256,256]{1,0:T(8,128)(2,1)S(1)} %constant_dynamic-update-slice_fusion), channel_id=1, source_target_pairs={{0,8},{1,505},{2,10},{3,507},{4,12},{5,509},{6,14},{7,511},{8,16},... | collective-permute-start | bytes 393224 | tf_op jit(solution)/shard_map/ppermute | solution.py:39
  61.1 9.4 %collective-permute-start.10 = (bf16[256,256]{1,0:T(8,128)(2,1)S(1)}, bf16[256,256]{1,0:T(8,128)(2,1)S(1)}, u32[]{:S(2)}, u32[]{:S(2)}) collective-permute-start(bf16[256,256]{1,0:T(8,128)(2,1)S(1)} %constant_dynamic-update-slice_fusion), channel_id=1, source_target_pairs={{0,4},{1,509},{2,6},{3,511},{4,8},{5,1},{6,10},{7,3},{8,12},{9,5},... | collective-permute-start | bytes 393224 | tf_op jit(solution)/shard_map/ppermute | solution.py:39
  64.5 7.1 %collective-permute-start.8 = (bf16[256,256]{1,0:T(8,128)(2,1)S(1)}, bf16[256,256]{1,0:T(8,128)(2,1)S(1)}, u32[]{:S(2)}, u32[]{:S(2)}) collective-permute-start(bf16[256,256]{1,0:T(8,128)(2,1)S(1)} %constant_dynamic-update-slice_fusion), channel_id=1, source_target_pairs={{0,2},{1,511},{2,4},{3,1},{4,6},{5,3},{6,8},{7,5},{8,10},{9,7},{10... | collective-permute-start | bytes 393224 | tf_op jit(solution)/shard_map/ppermute | solution.py:39
  71.7 4.8 %copy-start.2 = (bf16[48,128,128]{2,1,0:T(8,128)(2,1)S(1)}, bf16[48,128,128]{2,1,0:T(8,128)(2,1)}, u32[]{:S(2)}) copy-start(bf16[48,128,128]{2,1,0:T(8,128)(2,1)} %tiles_ref.1) | copy-start | bytes 4718596
  71.7 4.8 %copy-start.4 = (bf16[1024,128]{1,0:T(8,128)(2,1)S(1)}, bf16[1024,128]{1,0:T(8,128)(2,1)}, u32[]{:S(2)}) copy-start(bf16[1024,128]{1,0:T(8,128)(2,1)} %rhs_ref.1) | copy-start | bytes 786436
  71.7 4.8 %copy-start.5 = (f32[1024]{0:T(1024)S(1)}, f32[1024]{0:T(1024)}, u32[]{:S(2)}) copy-start(f32[1024]{0:T(1024)} %param.10) | copy-start | bytes 12292
  71.7 4.8 %copy-start.6 = (s32[48]{0:T(128)S(1)}, s32[48]{0:T(128)}, u32[]{:S(2)}) copy-start(s32[48]{0:T(128)} %cols_ref.1) | copy-start | bytes 580
  71.8 4.8 %collective-permute-start.11 = (bf16[384,256]{1,0:T(8,128)(2,1)S(1)}, bf16[384,256]{1,0:T(8,128)(2,1)S(1)}, u32[]{:S(2)}, u32[]{:S(2)}) collective-permute-start(bf16[384,256]{1,0:T(8,128)(2,1)S(1)} %pad_maximum_fusion.1), channel_id=1, source_target_pairs={{0,1},{1,0},{2,3},{3,2},{4,5},{5,4},{6,7},{7,6},{8,9},{9,8},{10,11... | collective-permute-start | bytes 589832 | tf_op jit(solution)/shard_map/ppermute | solution.py:39

commit v6 on v5

--- a/solution.py
+++ b/solution.py
@@ -213,10 +213,14 @@
     return jnp.where(take_a, a_ref[:K, :], b_ref[:K, :]), slot, jnp.where(take_a, a, b)
 
 
-def merge_near(power, adj_ref, margin_ref, summed_ref, vectors_ref, a_ref, b_ref, out_ref):
-    me = lax.axis_index("sub")
-    basis, slot, _ = pick_basis(power, a_ref, b_ref, True, me)
-    out_ref[...] = summed_ref[...] + arrive(adj_ref, margin_ref, slot, basis, vectors_ref[:K, :K])
+def merge_near(adj_ref, margin_ref, summed_ref, two_ref, four_ref, a2_ref, b2_ref, a3_ref, b3_ref, out_ref):
+    me = lax.axis_index("sub")
+    pieces = []
+    for power, vectors_ref, a_ref, b_ref in ((2, two_ref, a2_ref, b2_ref), (3, four_ref, a3_ref, b3_ref)):
+        basis, slot, _ = pick_basis(power, a_ref, b_ref, True, me)
+        pieces.append((slot, basis, vectors_ref[:K, :K]))
+    added = scatter(margin_ref, [p[0] for p in pieces], corrections(adj_ref, pieces))
+    out_ref[...] = summed_ref[...] + added
 
 
 def merge_next(adj_ref, margin_ref, summed_ref, vectors_ref, across_ref, a_ref, b_ref, out_ref):
@@ -338,10 +342,9 @@
         merge_chip, "merge_chip", [SMEM] + [VMEM] * 5, [arr((NLOC, K), F32)], [], 10**9
     )(adjacency, deflation, margin, send, other, theirs[INSIDE])[0]
     near = {power: [theirs[STEPS.index((power, colour))] for colour in (0, 1)] for power in (1, 2, 3)}
-    for power, vectors in ((3, four), (2, two)):
-        summed = call(
-            functools.partial(merge_near, power), f"merge_{power}", [SMEM] + [VMEM] * 5, [arr((NLOC, K), F32)], [], 1, moved=1
-        )(adjacency, margin, summed, vectors, *near[power])[0]
+    summed = call(merge_near, "merge_near", [SMEM] + [VMEM] * 8, [arr((NLOC, K), F32)], [], 1, moved=1)(
+        adjacency, margin, summed, two, four, *near[2], *near[3]
+    )[0]
     one_late, summed = lax.optimization_barrier((one, summed))
     hand_over = jnp.concatenate([one_late[K:], two[K:], four[K:]])
     far = core_swap(hand_over)

time: 80.2 us -> 80.2 us (level)
  starting transfers between devices: 53.2 us -> 54.2 us
  Pallas kernels: 15.4 us -> 14.5 us
    ppermute x12, starting transfers between devices: 53.2 us -> 54.2 us  [permute(): return lax.ppermute(block, 'sub', [(i, target(i) % n) for i in range(n)])]
    pallas_call x2 -> x1, Pallas kernels: 2.31 us -> 1.44 us  [per_device(): call(merge_near, 'merge_near', [SMEM] + [VMEM] * 8, [arr((NLOC, K), F32)]...]
  transfers between devices with their start and end apart: 12 -> 12, of which waited for: 5 -> 5; matrix products, arithmetic and copies ran while one was open for 0% -> 0% of each run, Pallas kernels for 10% -> 9%
where the time goes in v6:
time: 80.2 us; the launch traced here: 79.7 us
  starting transfers between devices  54.2 us (68%)
  Pallas kernels  14.5 us (18%)
  waiting for transfers between devices  9.77 us (12%)
  between operations  0.97 us (1%)
    ppermute x12, starting transfers between devices, permute(): return lax.ppermute(block, 'sub', [(i, target(i) % n) for i in range(n)])  54.2 us
    ppermute x12, waiting for transfers between devices, permute(): return lax.ppermute(block, 'sub', [(i, target(i) % n) for i in range(n)])  9.77 us
    pallas_call x1, Pallas kernels, per_device(): call(finish, 'finish', [SMEM] * 2 + [VMEM] * 24, [arr((NLOC, K), BF16), a...  3.11 us
    pallas_call x1, Pallas kernels, per_device(): call(prepare, 'prepare', [HBM] * 6, [arr((2 * ROWS, OV), BF16)] + [arr((K...  2.91 us
    pallas_call x1, Pallas kernels, per_device(): call(prepare_rest, 'prepare_rest', [VMEM] * 3, [arr((ROWS, OV), BF16)] *...  1.92 us
  transfers between devices with their start and end apart: 12, of which 5 were waited for; matrix products, arithmetic and copies ran while one was open for 0% of the time, Pallas kernels for 9%

profile of v6, /device:TPU:1, one launch (start us, length us, event | category | flops | bytes accessed | tf_op | source)
XLA Modules:
  0.0 79.7 jit_solution(13504409434694099211)
XLA Ops:
  0.6 0.0 copy-start
  0.6 2.9 %prepare.1 = (bf16[576,512]{1,0:T(8,128)(2,1)S(1)}, f32[128,128]{1,0:T(8,128)S(1)}, f32[128,128]{1,0:T(8,128)S(1)}, bf16[256,1024]{1,0:T(8,128)(2,1)S(1)}) custom-call(s32[48]{0:T(128)} %cols_ref.1, bf16[1024,128]{1,0:T(8,128)(2,1)} %z_ref.1, bf16[48,128,128]{2,1,0:T(8,128)(2,1)} %tiles_ref.1, f32[8,128]{1,0:T(8,128)} %bitcast.8, bf16[1024,128]{1,0:T(8,128)(2,1)} %rhs_ref.1, ...), custom_call_target="tpu_custom_call" | custom-call | flops 3000000000 | bytes 1048576 | tf_op jit(solution)/shard_map/prepare/pallas_call | solution.py:282
  3.6 8.8 %collective-permute-start.2 = (bf16[576,512]{1,0:T(8,128)(2,1)S(1)}, bf16[576,512]{1,0:T(8,128)(2,1)S(1)}, u32[]{:S(2)}, u32[]{:S(2)}) collective-permute-start(bf16[576,512]{1,0:T(8,128)(2,1)S(1)} %get-tuple-element.27), channel_id=1, source_target_pairs={{0,1},{1,0},{2,3},{3,2},{4,5},{5,4},{6,7},{7,6},{8,9},{9,8},{10,11... | collective-permute-start | bytes 1769480 | tf_op jit(solution)/shard_map/ppermute | solution.py:39
  12.3 0.0 copy-done
  12.4 1.9 %prepare_rest.1 = (bf16[288,512]{1,0:T(8,128)(2,1)S(1)}, bf16[288,512]{1,0:T(8,128)(2,1)S(1)}, bf16[288,512]{1,0:T(8,128)(2,1)S(1)}, bf16[288,512]{1,0:T(8,128)(...) custom-call(s32[8,512]{1,0:T(8,128)S(1)} %bitcast.3, bf16[256,1024]{1,0:T(8,128)(2,1)S(1)} %get-tuple-element.22.zit, ...), custom_call_target="tpu_custom_call" | custom-call | flops 8000000000 | bytes 1048576 | tf_op jit(solution)/shard_map/prepare_rest/pallas_call | solution.py:299
  14.3 0.0 collective-permute-done.2
  14.4 10.4 %collective-permute-start.3 = (bf16[576,512]{1,0:T(8,128)(2,1)S(1)}, bf16[576,512]{1,0:T(8,128)(2,1)S(1)}, u32[]{:S(2)}, u32[]{:S(2)}) collective-permute-start(bf16[576,512]{1,0:T(8,128)(2,1)S(1)} %pad_maximum_fusion), channel_id=1, source_target_pairs={{0,2},{1,511},{2,4},{3,1},{4,6},{5,3},{6,8},{7,5},{8,10},{9,7},{10... | collective-permute-start | bytes 1769480 | tf_op jit(solution)/shard_map/ppermute | solution.py:39
  24.8 1.9 %collective-permute-start = (bf16[288,512]{1,0:T(8,128)(2,1)S(1)}, bf16[288,512]{1,0:T(8,128)(2,1)S(1)}, u32[]{:S(2)}, u32[]{:S(2)}) collective-permute-start(bf16[288,512]{1,0:T(8,128)(2,1)S(1)} %get-tuple-element.23.rest_0_), channel_id=1, source_target_pairs={{0,4},{1,5},{2,6},{3,7},{4,0},{5,1},{6,2},{7,3},{8,12},{9,13},{10,... | collective-permute-start | bytes 884744 | tf_op jit(solution)/shard_map/ppermute | solution.py:39
  26.7 5.7 %collective-permute-start.1 = (bf16[288,512]{1,0:T(8,128)(2,1)S(1)}, bf16[288,512]{1,0:T(8,128)(2,1)S(1)}, u32[]{:S(2)}, u32[]{:S(2)}) collective-permute-start(bf16[288,512]{1,0:T(8,128)(2,1)S(1)} %get-tuple-element.24.rest_1_), channel_id=1, source_target_pairs={{0,508},{1,509},{2,510},{3,511},{4,8},{5,9},{6,10},{7,11},{8,4},{9... | collective-permute-start | bytes 884744 | tf_op jit(solution)/shard_map/ppermute | solution.py:39
  32.4 1.9 %collective-permute-start.4 = (bf16[288,512]{1,0:T(8,128)(2,1)S(1)}, bf16[288,512]{1,0:T(8,128)(2,1)S(1)}, u32[]{:S(2)}, u32[]{:S(2)}) collective-permute-start(bf16[288,512]{1,0:T(8,128)(2,1)S(1)} %get-tuple-element.25.rest_2_), channel_id=1, source_target_pairs={{0,510},{1,3},{2,0},{3,5},{4,2},{5,7},{6,4},{7,9},{8,6},{9,11},{10... | collective-permute-start | bytes 884744 | tf_op jit(solution)/shard_map/ppermute | solution.py:39
  34.3 0.0 copy-start.1
  34.3 2.3 %collective-permute-start.5 = (bf16[288,512]{1,0:T(8,128)(2,1)S(1)}, bf16[288,512]{1,0:T(8,128)(2,1)S(1)}, u32[]{:S(2)}, u32[]{:S(2)}) collective-permute-start(bf16[288,512]{1,0:T(8,128)(2,1)S(1)} %get-tuple-element.28.rest_5_), channel_id=1, source_target_pairs={{0,8},{1,9},{2,10},{3,11},{4,12},{5,13},{6,14},{7,15},{8,0},{9,1},... | collective-permute-start | bytes 884744 | tf_op jit(solution)/shard_map/ppermute | solution.py:39
  36.7 0.0 collective-permute-done.3
  36.7 3.6 %collective-permute-start.6 = (bf16[288,512]{1,0:T(8,128)(2,1)S(1)}, bf16[288,512]{1,0:T(8,128)(2,1)S(1)}, u32[]{:S(2)}, u32[]{:S(2)}) collective-permute-start(bf16[288,512]{1,0:T(8,128)(2,1)S(1)} %get-tuple-element.32.rest_0_), channel_id=1, source_target_pairs={{0,504},{1,505},{2,506},{3,507},{4,508},{5,509},{6,510},{7,511},{8... | collective-permute-start | bytes 884744 | tf_op jit(solution)/shard_map/ppermute | solution.py:39
  40.4 1.3 %collective-permute-done.rest_6_.a2_ref.rest_0_ = bf16[288,512]{1,0:T(8,128)(2,1)S(1)} collective-permute-done((bf16[288,512]{1,0:T(8,128)(2,1)S(1)}, bf16[288,512]{1,0:T(8,128)(2,1)S(1)}, u32[]{:S(2)}, u32[]{:S(2)}) %collective-permute-start) | collective-permute-done | bytes 294944 | tf_op jit(solution)/shard_map/ppermute | solution.py:39
  41.7 0.0 collective-permute-done.1.rest_7_.b2_ref.rest_1_
  41.7 3.5 %collective-permute-done.4.rest_9_.b_ref.rest_3_ = bf16[288,512]{1,0:T(8,128)(2,1)S(1)} collective-permute-done((bf16[288,512]{1,0:T(8,128)(2,1)S(1)}, bf16[288,512]{1,0:T(8,128)(2,1)S(1)}, u32[]{:S(2)}, u32[]{:S(2)}) %collective-permute-start.4) | collective-permute-done | bytes 294944 | tf_op jit(solution)/shard_map/ppermute | solution.py:39
  45.3 0.0 collective-permute-done.5.rest_11_.a3_ref.rest_5_
  45.3 0.0 copy-done.1
  45.3 1.4 %iterate_early.1 = (bf16[128,896]{1,0:T(8,128)(2,1)S(1)}, bf16[128,896]{1,0:T(8,128)(2,1)S(1)}, f32[128,128]{1,0:T(8,128)S(1)}) custom-call(s32[1,8]{1,0:T(1,128)S(1)} %copy-done.1, f32[128,128]{1,0:T(8,128)S(1)} %get-tuple-element.21.own_ref, f32[128,128]{1,0:T(8,128)S(1)} %get-tuple-element.20.coarse_ref, bf16[288,512]{1,0:T(8,128)(2,1)S(1)} %get-tuple-element.23.rest_0_, ...), custom_call_target="tpu_custom_call" | custom-call | flops 1000000000 | bytes 1048576 | tf_op jit(solution)/shard_map/iterate_early/pallas_call | solution.py:321
  46.7 3.4 %collective-permute-done.6.rest_2_.b3_ref.rest_6_ = bf16[288,512]{1,0:T(8,128)(2,1)S(1)} collective-permute-done((bf16[288,512]{1,0:T(8,128)(2,1)S(1)}, bf16[288,512]{1,0:T(8,128)(2,1)S(1)}, u32[]{:S(2)}, u32[]{:S(2)}) %collective-permute-start.6) | collective-permute-done | bytes 294944 | tf_op jit(solution)/shard_map/ppermute | solution.py:39
  50.2 0.0 copy-start.3
  50.2 1.0 %iterate.1 = (bf16[128,256]{1,0:T(8,128)(2,1)S(1)}, bf16[128,256]{1,0:T(8,128)(2,1)S(1)}, bf16[128,256]{1,0:T(8,128)(2,1)S(1)}) custom-call(s32[1,8]{1,0:T(1,128)S(1)} %copy-done.1, f32[128,128]{1,0:T(8,128)S(1)} %get-tuple-element.20.coarse_ref, f32[128,128]{1,0:T(8,128)S(1)} %get-tuple-element.31.image_ref, ...), custom_call_target="tpu_custom_call" | custom-call | flops 1000000000 | bytes 1048576 | tf_op jit(solution)/shard_map/iterate/pallas_call | solution.py:330
  51.2 2.2 %collective-permute-start.7 = (bf16[128,256]{1,0:T(8,128)(2,1)S(1)}, bf16[128,256]{1,0:T(8,128)(2,1)S(1)}, u32[]{:S(2)}, u32[]{:S(2)}) collective-permute-start(bf16[128,256]{1,0:T(8,128)(2,1)S(1)} %get-tuple-element.35.send_ref), channel_id=1, source_target_pairs={{0,1},{1,0},{2,3},{3,2},{4,5},{5,4},{6,7},{7,6},{8,9},{9,8},{10,11... | collective-permute-start | bytes 196616 | tf_op jit(solution)/shard_map/ppermute | solution.py:39
  53.4 0.9 %collective-permute-done.7.other_ref = bf16[128,256]{1,0:T(8,128)(2,1)S(1)} collective-permute-done((bf16[128,256]{1,0:T(8,128)(2,1)S(1)}, bf16[128,256]{1,0:T(8,128)(2,1)S(1)}, u32[]{:S(2)}, u32[]{:S(2)}) %collective-permute-start.7) | collective-permute-done | bytes 65568 | tf_op jit(solution)/shard_map/ppermute | solution.py:39
  54.4 8.2 %collective-permute-start.9 = (bf16[256,256]{1,0:T(8,128)(2,1)S(1)}, bf16[256,256]{1,0:T(8,128)(2,1)S(1)}, u32[]{:S(2)}, u32[]{:S(2)}) collective-permute-start(bf16[256,256]{1,0:T(8,128)(2,1)S(1)} %constant_dynamic-update-slice_fusion), channel_id=1, source_target_pairs={{0,4},{1,509},{2,6},{3,511},{4,8},{5,1},{6,10},{7,3},{8,12},{9,5},... | collective-permute-start | bytes 393224 | tf_op jit(solution)/shard_map/ppermute | solution.py:39
  62.6 1.9 %collective-permute-start.10 = (bf16[256,256]{1,0:T(8,128)(2,1)S(1)}, bf16[256,256]{1,0:T(8,128)(2,1)S(1)}, u32[]{:S(2)}, u32[]{:S(2)}) collective-permute-start(bf16[256,256]{1,0:T(8,128)(2,1)S(1)} %constant_dynamic-update-slice_fusion), channel_id=1, source_target_pairs={{0,8},{1,505},{2,10},{3,507},{4,12},{5,509},{6,14},{7,511},{8,16},... | collective-permute-start | bytes 393224 | tf_op jit(solution)/shard_map/ppermute | solution.py:39
  64.5 2.9 %collective-permute-start.8 = (bf16[256,256]{1,0:T(8,128)(2,1)S(1)}, bf16[256,256]{1,0:T(8,128)(2,1)S(1)}, u32[]{:S(2)}, u32[]{:S(2)}) collective-permute-start(bf16[256,256]{1,0:T(8,128)(2,1)S(1)} %constant_dynamic-update-slice_fusion), channel_id=1, source_target_pairs={{0,2},{1,511},{2,4},{3,1},{4,6},{5,3},{6,8},{7,5},{8,10},{9,7},{10... | collective-permute-start | bytes 393224 | tf_op jit(solution)/shard_map/ppermute | solution.py:39
  67.5 0.0 copy-done.3
  67.5 1.2 %merge_chip.1.summed_ref = f32[1024,128]{1,0:T(8,128)S(1)} custom-call(s32[1,8]{1,0:T(1,128)S(1)} %copy-done.1, bf16[1024,128]{1,0:T(8,128)(2,1)S(1)} %copy-done.3, s32[8,512]{1,0:T(8,128)S(1)} %bitcast.4, bf16[128,256]{1,0:T(8,128)(2,1)S(1)} %get-tuple-element.35.send_ref, bf16[128,256]{1,0:T(8,128)(2,1)S(1)} %collective-permute-done.7.other_ref, ...), custom_call_target="tpu_custom_call" | custom-call | flops 1000000000 | bytes 1048576 | tf_op jit(solution)/shard_map/merge_chip/pallas_call | solution.py:341
  68.7 0.0 collective-permute-done.9.two_ref
  68.7 0.0 collective-permute-done.10.four_ref
  68.7 1.4 %merge_near.1.summed_ref = f32[1024,128]{1,0:T(8,128)S(1)} custom-call(s32[1,8]{1,0:T(1,128)S(1)} %copy-done.1, s32[8,512]{1,0:T(8,128)S(1)} %bitcast.5, f32[1024,128]{1,0:T(8,128)S(1)} %merge_chip.1.summed_ref, bf16[256,256]{1,0:T(8,128)(2,1)S(1)} %collective-permute-done.9.two_ref, bf16[256,256]{1,0:T(8,128)(2,1)S(1)} %collective-permute-done.10.four_ref, ...), custom_call_target="tpu_custom_call" | custom-call | flops 1 | bytes 1 | tf_op jit(solution)/shard_map/merge_near/pallas_call | solution.py:345
  70.1 0.5 collective-permute-done.8.vectors_ref.one_ref
  70.7 0.0 copy-start.2
  70.7 0.0 copy-start.4
  70.7 0.0 copy-start.5
  70.7 0.0 copy-start.6
  70.8 4.3 %collective-permute-start.11 = (bf16[384,256]{1,0:T(8,128)(2,1)S(1)}, bf16[384,256]{1,0:T(8,128)(2,1)S(1)}, u32[]{:S(2)}, u32[]{:S(2)}) collective-permute-start(bf16[384,256]{1,0:T(8,128)(2,1)S(1)} %pad_maximum_fusion.1), channel_id=1, source_target_pairs={{0,1},{1,0},{2,3},{3,2},{4,5},{5,4},{6,7},{7,6},{8,9},{9,8},{10,11... | collective-permute-start | bytes 589832 | tf_op jit(solution)/shard_map/ppermute | solution.py:39
  75.1 1.4 %merge_next.1.summed_ref = f32[1024,128]{1,0:T(8,128)S(1)} custom-call(s32[1,8]{1,0:T(1,128)S(1)} %copy-done.1, s32[8,512]{1,0:T(8,128)S(1)} %bitcast.6, f32[1024,128]{1,0:T(8,128)S(1)} %merge_near.1.summed_ref, bf16[256,256]{1,0:T(8,128)(2,1)S(1)} %collective-permute-done.8.vectors_ref.one_ref, ...), custom_call_target="tpu_custom_call" | custom-call | flops 1000000000 | bytes 1048576 | tf_op jit(solution)/shard_map/merge_next/pallas_call | solution.py:351
  76.5 0.0 collective-permute-done.11.far_ref
  76.5 0.0 copy-done.2
  76.6 0.0 copy-done.4
  76.6 0.0 copy-done.5
  76.6 0.0 copy-done.6
  76.6 3.1 %finish.1 = (bf16[1024,128]{1,0:T(8,128)(2,1)}, f32[128,128]{1,0:T(8,128)}) custom-call(s32[48]{0:T(128)S(1)} %copy-done.6, s32[1,8]{1,0:T(1,128)S(1)} %copy-done.1, bf16[48,128,128]{2,1,0:T(8,128)(2,1)S(1)} %copy-done.2, f32[8,128]{1,0:T(8,128)S(1)} %bitcast.9, bf16[1024,128]{1,0:T(8,128)(2,1)S(1)} %copy-done.4, s32[8,512]{1,0:T(8,128)S(1)} %bitcast.7, ...), custom_call_target="tpu_custom_call" | custom-call | flops 3000000000 | bytes 1048576 | tf_op jit(solution)/shard_map/finish/pallas_call | solution.py:355
  (10 shorter events, 0.2 us)
Async XLA Ops:
  0.6 11.7 %copy-start = (s32[1,8,512]{2,1,0:T(8,128)S(1)}, s32[1,8,512]{2,1,0:T(8,128)}, u32[]{:S(2)}) copy-start(s32[1,8,512]{2,1,0:T(8,128)} %param.13) | copy-start | bytes 49156
  3.6 10.7 %collective-permute-start.2 = (bf16[576,512]{1,0:T(8,128)(2,1)S(1)}, bf16[576,512]{1,0:T(8,128)(2,1)S(1)}, u32[]{:S(2)}, u32[]{:S(2)}) collective-permute-start(bf16[576,512]{1,0:T(8,128)(2,1)S(1)} %get-tuple-element.27), channel_id=1, source_target_pairs={{0,1},{1,0},{2,3},{3,2},{4,5},{5,4},{6,7},{7,6},{8,9},{9,8},{10,11... | collective-permute-start | bytes 1769480 | tf_op jit(solution)/shard_map/ppermute | solution.py:39
  14.4 22.3 %collective-permute-start.3 = (bf16[576,512]{1,0:T(8,128)(2,1)S(1)}, bf16[576,512]{1,0:T(8,128)(2,1)S(1)}, u32[]{:S(2)}, u32[]{:S(2)}) collective-permute-start(bf16[576,512]{1,0:T(8,128)(2,1)S(1)} %pad_maximum_fusion), channel_id=1, source_target_pairs={{0,2},{1,511},{2,4},{3,1},{4,6},{5,3},{6,8},{7,5},{8,10},{9,7},{10... | collective-permute-start | bytes 1769480 | tf_op jit(solution)/shard_map/ppermute | solution.py:39
  24.8 16.9 %collective-permute-start = (bf16[288,512]{1,0:T(8,128)(2,1)S(1)}, bf16[288,512]{1,0:T(8,128)(2,1)S(1)}, u32[]{:S(2)}, u32[]{:S(2)}) collective-permute-start(bf16[288,512]{1,0:T(8,128)(2,1)S(1)} %get-tuple-element.23.rest_0_), channel_id=1, source_target_pairs={{0,4},{1,5},{2,6},{3,7},{4,0},{5,1},{6,2},{7,3},{8,12},{9,13},{10,... | collective-permute-start | bytes 884744 | tf_op jit(solution)/shard_map/ppermute | solution.py:39
  26.7 15.0 %collective-permute-start.1 = (bf16[288,512]{1,0:T(8,128)(2,1)S(1)}, bf16[288,512]{1,0:T(8,128)(2,1)S(1)}, u32[]{:S(2)}, u32[]{:S(2)}) collective-permute-start(bf16[288,512]{1,0:T(8,128)(2,1)S(1)} %get-tuple-element.24.rest_1_), channel_id=1, source_target_pairs={{0,508},{1,509},{2,510},{3,511},{4,8},{5,9},{6,10},{7,11},{8,4},{9... | collective-permute-start | bytes 884744 | tf_op jit(solution)/shard_map/ppermute | solution.py:39
  32.4 12.9 %collective-permute-start.4 = (bf16[288,512]{1,0:T(8,128)(2,1)S(1)}, bf16[288,512]{1,0:T(8,128)(2,1)S(1)}, u32[]{:S(2)}, u32[]{:S(2)}) collective-permute-start(bf16[288,512]{1,0:T(8,128)(2,1)S(1)} %get-tuple-element.25.rest_2_), channel_id=1, source_target_pairs={{0,510},{1,3},{2,0},{3,5},{4,2},{5,7},{6,4},{7,9},{8,6},{9,11},{10... | collective-permute-start | bytes 884744 | tf_op jit(solution)/shard_map/ppermute | solution.py:39
  34.3 11.0 %copy-start.1 = (s32[1,8]{1,0:T(1,128)S(1)}, s32[1,8]{1,0:T(1,128)}, u32[]{:S(2)}) copy-start(s32[1,8]{1,0:T(1,128)} %adj_ref.11) | copy-start | bytes 100
  34.3 11.0 %collective-permute-start.5 = (bf16[288,512]{1,0:T(8,128)(2,1)S(1)}, bf16[288,512]{1,0:T(8,128)(2,1)S(1)}, u32[]{:S(2)}, u32[]{:S(2)}) collective-permute-start(bf16[288,512]{1,0:T(8,128)(2,1)S(1)} %get-tuple-element.28.rest_5_), channel_id=1, source_target_pairs={{0,8},{1,9},{2,10},{3,11},{4,12},{5,13},{6,14},{7,15},{8,0},{9,1},... | collective-permute-start | bytes 884744 | tf_op jit(solution)/shard_map/ppermute | solution.py:39
  36.7 13.5 %collective-permute-start.6 = (bf16[288,512]{1,0:T(8,128)(2,1)S(1)}, bf16[288,512]{1,0:T(8,128)(2,1)S(1)}, u32[]{:S(2)}, u32[]{:S(2)}) collective-permute-start(bf16[288,512]{1,0:T(8,128)(2,1)S(1)} %get-tuple-element.32.rest_0_), channel_id=1, source_target_pairs={{0,504},{1,505},{2,506},{3,507},{4,508},{5,509},{6,510},{7,511},{8... | collective-permute-start | bytes 884744 | tf_op jit(solution)/shard_map/ppermute | solution.py:39
  50.2 17.3 %copy-start.3 = (bf16[1024,128]{1,0:T(8,128)(2,1)S(1)}, bf16[1024,128]{1,0:T(8,128)(2,1)}, u32[]{:S(2)}) copy-start(bf16[1024,128]{1,0:T(8,128)(2,1)} %z_ref.1) | copy-start | bytes 786436
  51.2 3.1 %collective-permute-start.7 = (bf16[128,256]{1,0:T(8,128)(2,1)S(1)}, bf16[128,256]{1,0:T(8,128)(2,1)S(1)}, u32[]{:S(2)}, u32[]{:S(2)}) collective-permute-start(bf16[128,256]{1,0:T(8,128)(2,1)S(1)} %get-tuple-element.35.send_ref), channel_id=1, source_target_pairs={{0,1},{1,0},{2,3},{3,2},{4,5},{5,4},{6,7},{7,6},{8,9},{9,8},{10,11... | collective-permute-start | bytes 196616 | tf_op jit(solution)/shard_map/ppermute | solution.py:39
  54.4 14.3 %collective-permute-start.9 = (bf16[256,256]{1,0:T(8,128)(2,1)S(1)}, bf16[256,256]{1,0:T(8,128)(2,1)S(1)}, u32[]{:S(2)}, u32[]{:S(2)}) collective-permute-start(bf16[256,256]{1,0:T(8,128)(2,1)S(1)} %constant_dynamic-update-slice_fusion), channel_id=1, source_target_pairs={{0,4},{1,509},{2,6},{3,511},{4,8},{5,1},{6,10},{7,3},{8,12},{9,5},... | collective-permute-start | bytes 393224 | tf_op jit(solution)/shard_map/ppermute | solution.py:39
  62.6 6.1 %collective-permute-start.10 = (bf16[256,256]{1,0:T(8,128)(2,1)S(1)}, bf16[256,256]{1,0:T(8,128)(2,1)S(1)}, u32[]{:S(2)}, u32[]{:S(2)}) collective-permute-start(bf16[256,256]{1,0:T(8,128)(2,1)S(1)} %constant_dynamic-update-slice_fusion), channel_id=1, source_target_pairs={{0,8},{1,505},{2,10},{3,507},{4,12},{5,509},{6,14},{7,511},{8,16},... | collective-permute-start | bytes 393224 | tf_op jit(solution)/shard_map/ppermute | solution.py:39
  64.5 6.1 %collective-permute-start.8 = (bf16[256,256]{1,0:T(8,128)(2,1)S(1)}, bf16[256,256]{1,0:T(8,128)(2,1)S(1)}, u32[]{:S(2)}, u32[]{:S(2)}) collective-permute-start(bf16[256,256]{1,0:T(8,128)(2,1)S(1)} %constant_dynamic-update-slice_fusion), channel_id=1, source_target_pairs={{0,2},{1,511},{2,4},{3,1},{4,6},{5,3},{6,8},{7,5},{8,10},{9,7},{10... | collective-permute-start | bytes 393224 | tf_op jit(solution)/shard_map/ppermute | solution.py:39
  70.7 5.8 %copy-start.2 = (bf16[48,128,128]{2,1,0:T(8,128)(2,1)S(1)}, bf16[48,128,128]{2,1,0:T(8,128)(2,1)}, u32[]{:S(2)}) copy-start(bf16[48,128,128]{2,1,0:T(8,128)(2,1)} %tiles_ref.1) | copy-start | bytes 4718596
  70.7 5.8 %copy-start.4 = (bf16[1024,128]{1,0:T(8,128)(2,1)S(1)}, bf16[1024,128]{1,0:T(8,128)(2,1)}, u32[]{:S(2)}) copy-start(bf16[1024,128]{1,0:T(8,128)(2,1)} %rhs_ref.1) | copy-start | bytes 786436
  70.7 5.8 %copy-start.5 = (f32[1024]{0:T(1024)S(1)}, f32[1024]{0:T(1024)}, u32[]{:S(2)}) copy-start(f32[1024]{0:T(1024)} %param.10) | copy-start | bytes 12292
  70.7 5.8 %copy-start.6 = (s32[48]{0:T(128)S(1)}, s32[48]{0:T(128)}, u32[]{:S(2)}) copy-start(s32[48]{0:T(128)} %cols_ref.1) | copy-start | bytes 580
  70.8 5.8 %collective-permute-start.11 = (bf16[384,256]{1,0:T(8,128)(2,1)S(1)}, bf16[384,256]{1,0:T(8,128)(2,1)S(1)}, u32[]{:S(2)}, u32[]{:S(2)}) collective-permute-start(bf16[384,256]{1,0:T(8,128)(2,1)S(1)} %pad_maximum_fusion.1), channel_id=1, source_target_pairs={{0,1},{1,0},{2,3},{3,2},{4,5},{5,4},{6,7},{7,6},{8,9},{9,8},{10,11... | collective-permute-start | bytes 589832 | tf_op jit(solution)/shard_map/ppermute | solution.py:39
